TPU v7x, 32 devices: a whole 2x2x4 slice. The times are simulated.
32 devices in a mesh: chan: 4 (over x, core), half: 2 (over y), ctx: 4 (over z).
Axes of the slice: x: 2, y: 2, z: 4, core: 2. Of those that a mesh axis runs over, the one named last changes fastest.
Arguments:
- query_gate: bfloat16 [2048, 8192], P('ctx', 'chan'), parts along dimension 1, may hold values from -6 to 6
- key_gate: bfloat16 [2048, 8192], P('ctx', 'chan'), parts along dimension 1, may hold values from -6 to 6
- value_input: bfloat16 [2048, 8192], P('ctx', 'chan'), parts along dimension 1, may hold values from -6 to 6
- residues: float32 [16, 8192], P(None, 'chan'), parts along dimension 1, may hold values from -1.5 to 1.5
- decays: float32 [16, 8192], P(None, 'chan'), parts along dimension 1, may hold values from 2.4414063e-05 to 0.05
- skip_gain: float32 [8192], P('chan'), parts along dimension 0, may hold values from 0.25 to 1
Outputs:
- mixed: bfloat16 [2048, 8192], P('ctx', 'chan'), parts along dimension 1
There are 4 independent parts, one for each index of `chan`. A program takes and returns all parts, laid end to end along the dimension named above; each array names one. Nothing has to cross between parts.
All inputs are finite; a program needn't handle non-finite values.
Results may differ from a plain program's by a relative error of at most 0.00155.
Values may be sent and summed in bfloat16 or wider, within the bound.
No kernel may reach another device: no remote copies, remote signals or barrier semaphores. Data moves between devices by JAX's collectives and lax.ppermute only.
A program may use at most 128 MiB of HBM per device.

v0:
```python
import math

import jax
import jax.numpy as jnp
from jax import lax
from jax.sharding import PartitionSpec as P


def unit_phase(phase_index, period, direction):
    phase_angle = phase_index.astype(jnp.float32) * (direction * 2.0 * math.pi / period)
    return (jnp.cos(phase_angle), jnp.sin(phase_angle))


def dft_table(length_n, direction):
    index_row = jnp.arange(length_n, dtype=jnp.int32)
    cosine, sine_part = unit_phase(
        index_row[:, None] * index_row[None, :] % length_n, length_n, direction
    )
    upper = jnp.concatenate([cosine, -sine_part], 1)
    lower = jnp.concatenate([sine_part, cosine], 1)
    return jnp.concatenate([upper, lower], 0)


def apply_table(field, matrix):
    lead_shape = field.shape
    flat_data = field.reshape(matrix.shape[0], -1)
    result = jnp.dot(
        matrix, flat_data, precision=lax.Precision.HIGHEST, preferred_element_type=jnp.float32
    )
    return result.reshape(lead_shape)


def rotate(field, cosine, sine_part):
    real_out = cosine * field[0] - sine_part * field[1]
    imag_out = sine_part * field[0] + cosine * field[1]
    return jnp.stack([real_out, imag_out])


def spectrum(frequency, residues, decays, half_bit, seq_len):
    row_count = frequency.shape[0]
    block_rows = math.gcd(row_count, 64)
    grouped = frequency.reshape(row_count // block_rows, block_rows)
    decay_mode = decays[:, None, :]
    damping = jnp.exp(-decay_mode)
    decay_gap = -jnp.expm1(-decay_mode)
    end_value = jnp.exp(-decay_mode * seq_len)
    numerator = jnp.where(half_bit == 0, -jnp.expm1(-decay_mode * seq_len), 1.0 + end_value)
    scaled = residues[:, None, :] * jnp.sqrt(decay_mode) * numerator

    def one_block(block_freq):
        theta_row = ((2 * block_freq + half_bit).astype(jnp.float32) * (math.pi / seq_len))[
            None, :, None
        ]
        half_sine = jnp.sin(0.5 * theta_row)
        real_den = decay_gap + 2.0 * damping * half_sine * half_sine
        imag_den = damping * jnp.sin(theta_row)
        factor = scaled / (real_den * real_den + imag_den * imag_den)
        return (jnp.sum(factor * real_den, 0), -jnp.sum(factor * imag_den, 0))

    real_part, imag_part = lax.map(one_block, grouped)
    return (real_part.reshape(row_count, -1), imag_part.reshape(row_count, -1))


def spread_positions(signal, residues, decays, half_bit, ctx_rank, ctx_size):
    row_count, chan_width = signal.shape
    seq_len = row_count * ctx_size
    group_rows = row_count // ctx_size
    positions = ctx_rank * row_count + jnp.arange(row_count, dtype=jnp.int32)
    cosine, sine_part = unit_phase(positions * half_bit % (2 * seq_len), 2 * seq_len, -1.0)
    field = jnp.stack([signal * cosine[:, None], signal * sine_part[:, None]]).reshape(
        2, ctx_size, group_rows, chan_width
    )
    field = lax.all_to_all(field, "ctx", split_axis=1, concat_axis=1, tiled=True)
    field = apply_table(field, dft_table(ctx_size, -1.0))
    inner_idx = ctx_rank * group_rows + jnp.arange(group_rows, dtype=jnp.int32)
    outer_idx = jnp.arange(ctx_size, dtype=jnp.int32)
    cosine, sine_part = unit_phase(outer_idx[:, None] * inner_idx[None, :] % seq_len, seq_len, -1.0)
    field = rotate(field, cosine[:, :, None], sine_part[:, :, None])
    field = lax.all_to_all(field, "ctx", split_axis=1, concat_axis=2, tiled=True).reshape(
        2, row_count, chan_width
    )
    field = apply_table(field, dft_table(row_count, -1.0))
    frequency = ctx_rank + ctx_size * jnp.arange(row_count, dtype=jnp.int32)
    real_h, imag_h = spectrum(frequency, residues, decays, half_bit, seq_len)
    field = rotate(field, real_h, imag_h)
    field = apply_table(field, dft_table(row_count, 1.0))
    cosine, sine_part = unit_phase(
        jnp.arange(row_count, dtype=jnp.int32) * ctx_rank % seq_len, seq_len, 1.0
    )
    field = rotate(field, cosine[:, None], sine_part[:, None]).reshape(
        2, ctx_size, group_rows, chan_width
    )
    field = lax.all_to_all(field, "ctx", split_axis=1, concat_axis=1, tiled=True)
    field = apply_table(field, dft_table(ctx_size, 1.0))
    position_map = outer_idx[:, None] * row_count + inner_idx[None, :]
    cosine, sine_part = unit_phase(position_map * half_bit % (2 * seq_len), 2 * seq_len, 1.0)
    half_term = (cosine[:, :, None] * field[0] - sine_part[:, :, None] * field[1]) * (0.5 / seq_len)
    return lax.all_to_all(half_term, "ctx", split_axis=0, concat_axis=1, tiled=True).reshape(
        row_count, chan_width
    )


def shards(query_gate, key_gate, value_input, residues, decays, skip_gain):
    ctx_size = lax.axis_size("ctx")
    ctx_rank = lax.axis_index("ctx")
    half_bit = lax.axis_index("half")
    signal = key_gate.astype(jnp.float32) * value_input.astype(jnp.float32)
    half_term = spread_positions(signal, residues, decays, half_bit, ctx_rank, ctx_size)
    full_conv = lax.psum(half_term, "half")
    return (query_gate.astype(jnp.float32) * (full_conv + skip_gain * signal)).astype(jnp.bfloat16)


def solution(mesh):
    placed = (
        P("ctx", "chan"),
        P("ctx", "chan"),
        P("ctx", "chan"),
        P(None, "chan"),
        P(None, "chan"),
        P("chan"),
    )
    return jax.shard_map(
        shards, mesh=mesh, in_specs=placed, out_specs=P("ctx", "chan"), check_vma=False
    )
```

profile of v0, /device:TPU:0, one launch (start us, length us, event | category | flops | bytes accessed | tf_op | source)
XLA Modules:
  0.0 933.5 jit_solution(9512084686644852877)
XLA Ops:
  6.5 0.1 fusion.70
  6.6 3.0 fusion.32
  9.6 3.8 pad_maximum_fusion
  13.4 6.3 all-to-all-start
  19.7 0.1 fusion.79
  19.8 0.1 multiply_sine_fusion.2
  19.8 0.1 fusion.72
  19.9 4.6 fusion.39
  24.5 3.9 fusion.38
  28.4 5.0 multiply_sine_fusion
  33.3 5.5 multiply_sine_fusion.1
  38.8 0.1 fusion.77
  38.9 0.0 copy-done.4
  38.9 0.1 exponential_bitcast_fusion
  39.1 164.7 %all-to-all-done = f32[2,4,128,2048]{3,2,0,1:T(8,128)} async-done(((f32[2,4,128,2048]{3,2,0,1:T(8,128)}), f32[2,4,128,2048]{3,2,0,1:T(8,128)}, u32[]{:S(2)}, u32[]{:S(2)}) %all-to-all-start) | async-done | bytes 8388640 | tf_op jit(solution)/shard_map/all_to_all | solution.py:73
  203.8 4.0 copy.22
  207.8 4.9 copy.31
  212.6 9.2 fusion.48
  221.9 1.3 fusion.86
  223.2 4.9 fusion.9
  228.1 4.3 pad_maximum_fusion.1
  232.4 5.6 all-to-all-start.1
  238.1 41.1 %while.14 = (s32[]{:T(128)}, f32[8,64,2048]{2,1,0:T(8,128)}, f32[8,64,2048]{2,1,0:T(8,128)}, f32[16,1,2048]{2,0,1:T(8,128)S(1)}, f32[16,1,2048]{2,0,1:T(8,128)S(...) while((s32[]{:T(128)}, f32[8,64,2048]{2,1,0:T(8,128)}, ...), condition=%wide.region_3.4_spmd, body=%wide.region_0.3_spmd.sunk | while | flops 25067904 | bytes 3934565 | solution.py:60
  238.1 0.1 sine_bitcast_fusion.4
  238.2 3.9 fusion.92
  242.2 1.0 bitcast_dynamic-update-slice_fusion.3
  243.3 3.9 fusion.92
  247.3 1.1 bitcast_dynamic-update-slice_fusion.3
  248.4 3.9 fusion.92
  252.4 1.1 bitcast_dynamic-update-slice_fusion.3
  253.6 3.9 fusion.92
  257.5 1.1 bitcast_dynamic-update-slice_fusion.3
  258.7 3.9 fusion.92
  262.6 1.1 bitcast_dynamic-update-slice_fusion.3
  263.8 3.9 fusion.92
  267.7 1.1 bitcast_dynamic-update-slice_fusion.3
  268.9 3.9 fusion.92
  272.9 1.0 bitcast_dynamic-update-slice_fusion.3
  274.0 3.9 fusion.92
  278.0 1.2 bitcast_dynamic-update-slice_fusion.3
  279.1 141.7 %all-to-all-done.1 = f32[2,4,128,2048]{3,2,0,1:T(8,128)} async-done(((f32[2,4,128,2048]{3,2,0,1:T(8,128)}), f32[2,4,128,2048]{3,2,0,1:T(8,128)}, u32[]{:S(2)}, u32[]{:S(2)}) %all-to-all-start.1) | async-done | bytes 8388640 | tf_op jit(solution)/shard_map/all_to_all | solution.py:79
  420.9 4.1 copy.27
  425.0 0.1 copy-done.3
  425.1 29.5 %fusion.21 = f32[1024,2048]{1,0:T(8,128)} fusion(f32[1024,2048]{1,0:T(8,128)S(1)} %bitcast.144, f32[512,512]{1,0:T(8,128)S(1)} %copy-done.3, f32[512,512]{1,0:T(8,128)S(1)} %copy-done.2, f32[512,512]{1,0:T(8,128)S(1)} %copy-done.1), kind=kOutput, calls=%fused_computation.39 | convolution fusion | flops 25772949504 | bytes 19922944 | tf_op jit(solution)/shard_map/dot_general | solution.py:27
  454.6 10.2 %fusion.29 = (f32[512,2048]{1,0:T(8,128)S(1)}, f32[512,2048]{1,0:T(8,128)}) fusion(f32[8,64,2048]{2,1,0:T(8,128)} %get-tuple-element.108, f32[8,64,2048]{2,1,0:T(8,128)} %get-tuple-element.107, f32[1024,2048]{1,0:T(8,128)} %fusion.21), kind=kLoop, calls=%fused_computation.49 | loop fusion | flops 6291456 | bytes 25165824 | tf_op jit(solution)/shard_map/sub | solution.py:34
  464.8 2.8 pad_maximum_fusion.2
  467.6 30.9 %fusion.13 = f32[1024,2048]{1,0:T(8,128)S(1)} fusion(f32[1024,2048]{1,0:T(8,128)S(1)} %bitcast.143, f32[512,512]{1,0:T(8,128)} %get-tuple-element.159, f32[512,512]{1,0:T(8,128)S(1)} %get-tuple-element.158, f32[512,512]{1,0:T(8,128)S(1)} %fusion.38), kind=kOutput, calls=%fused_computation.31 | convolution fusion | flops 25772949504 | bytes 19922944 | tf_op jit(solution)/shard_map/dot_general | solution.py:27
  498.5 2.1 multiply_subtract_fusion
  500.6 3.8 pad_maximum_fusion.3
  504.4 5.6 all-to-all-start.2
  510.0 0.2 all-reduce.2.cloned.1.call-start
  510.3 0.1 fusion.78
  510.3 0.1 multiply_sine_fusion.3
  510.4 182.2 %all-to-all-done.2 = f32[2,4,128,2048]{3,2,0,1:T(8,128)} async-done(((f32[2,4,128,2048]{3,2,0,1:T(8,128)}), f32[2,4,128,2048]{3,2,0,1:T(8,128)}, u32[]{:S(2)}, u32[]{:S(2)}) %all-to-all-start.2) | async-done | bytes 8388640 | tf_op jit(solution)/shard_map/all_to_all | solution.py:93
  692.6 4.0 copy.30
  696.6 4.9 copy.34
  701.4 9.0 fusion.40
  710.5 1.3 fusion.85
  711.8 5.4 fusion.6
  717.2 96.2 %all_to_all.28 = f32[4,128,2048]{2,1,0:T(8,128)} all-to-all(f32[4,128,2048]{2,1,0:T(8,128)S(1)} %fusion.6), channel_id=1, replica_groups=mesh['chan'=4,'half'=2,'ctx'=4] {'ctx'}, dimensions={0} | all-to-all | bytes 8388608 | tf_op jit(solution)/shard_map/all_to_all | solution.py:98
  813.5 0.0 all-reduce.2.cloned.1.call-update
  813.5 106.7 %all-reduce.2.cloned.1.call-done = f32[512,2048]{1,0:T(8,128)} async-done(((f32[512,2048]{1,0:T(8,128)}), f32[512,2048]{1,0:T(8,128)}) %all-reduce.2.cloned.1.call-update) | async-done | bytes 4194320 | tf_op jit(solution)/shard_map/psum | solution.py:109
  920.2 0.0 copy-done
  920.2 6.3 multiply_convert_fusion
  (39 shorter events, 0.8 us)
Async XLA Ops:
  13.4 190.4 %all-to-all-start = ((f32[2,4,128,2048]{3,2,0,1:T(8,128)}), f32[2,4,128,2048]{3,2,0,1:T(8,128)}, u32[]{:S(2)}, u32[]{:S(2)}) async-start(f32[2,4,128,2048]{3,2,0,1:T(8,128)} %pad_maximum_fusion), calls=%async_computation | async-start | bytes 16777216 | tf_op jit(solution)/shard_map/all_to_all | solution.py:73
  19.7 19.2 %copy-start.4 = (f32[16,2048]{1,0:T(8,128)S(1)}, f32[16,2048]{1,0:T(8,128)}, u32[]{:S(2)}) copy-start(f32[16,2048]{1,0:T(8,128)} %param.12) | copy-start | bytes 393220
  19.7 19.2 %copy-start.5 = (f32[16,2048]{1,0:T(8,128)S(1)}, f32[16,2048]{1,0:T(8,128)}, u32[]{:S(2)}) copy-start(f32[16,2048]{1,0:T(8,128)} %param.11) | copy-start | bytes 393220
  232.4 188.4 %all-to-all-start.1 = ((f32[2,4,128,2048]{3,2,0,1:T(8,128)}), f32[2,4,128,2048]{3,2,0,1:T(8,128)}, u32[]{:S(2)}, u32[]{:S(2)}) async-start(f32[2,4,128,2048]{3,2,0,1:T(8,128)} %pad_maximum_fusion.1), calls=%async_computation.1 | async-start | bytes 16777216 | tf_op jit(solution)/shard_map/all_to_all | solution.py:79
  420.9 4.1 copy-start.1
  420.9 4.1 copy-start.2
  420.9 4.2 copy-start.3
  504.4 188.2 %all-to-all-start.2 = ((f32[2,4,128,2048]{3,2,0,1:T(8,128)}), f32[2,4,128,2048]{3,2,0,1:T(8,128)}, u32[]{:S(2)}, u32[]{:S(2)}) async-start(f32[2,4,128,2048]{3,2,0,1:T(8,128)} %pad_maximum_fusion.3), calls=%async_computation.2 | async-start | bytes 16777216 | tf_op jit(solution)/shard_map/all_to_all | solution.py:93
  510.0 410.1 %all-reduce.2.cloned.1.call-start = ((), (), s32[]{:S(2)}) async-start(), calls=%async_computation.4 | async-start | bytes 8388608 | tf_op jit(solution)/shard_map/psum | solution.py:109
  813.5 106.7 %copy-start = (bf16[512,2048]{1,0:T(8,128)(2,1)S(1)}, bf16[512,2048]{1,0:T(8,128)(2,1)}, u32[]{:S(2)}) copy-start(bf16[512,2048]{1,0:T(8,128)(2,1)} %param.10) | copy-start | bytes 6291460
  813.5 106.7 %copy-start.6 = (f32[2048]{0:T(1024)S(1)}, f32[2048]{0:T(1024)}, u32[]{:S(2)}) copy-start(f32[2048]{0:T(1024)} %param.13) | copy-start | bytes 24580
Sparse Core Ops, SparseCore 0:
  813.6 106.5 all-reduce.1
where the time goes:
time: 940 us; the launch traced here: 934 us
  waiting for transfers between devices  595 us (63%)
  other arithmetic  107 us (11%)
  blocking collectives  96.2 us (10%)
  matrix products  78.6 us (8%)
  local copies, waits for them, and re-layouts  24.5 us (3%)
  starting transfers between devices  17.8 us (2%)
  between operations  13.8 us (1%)
    all_to_all x2, waiting for transfers between devices, spread_positions(): lax.all_to_all(field, 'ctx', split_axis=1, concat_axis=1, tiled=True)  347 us
    all_to_all x1, waiting for transfers between devices, spread_positions(): lax.all_to_all(field, 'ctx', split_axis=1, concat_axis=2, tiled=True)  142 us
    psum x1, waiting for transfers between devices, shards(): full_conv = lax.psum(half_term, 'half')  107 us
    all_to_all x1, blocking collectives, spread_positions(): lax.all_to_all(half_term, 'ctx', split_axis=0, concat_axis=1, tiled=True)  96.2 us
    dot_general x4, matrix products, apply_table(): jnp.dot(matrix, flat_data, precision=lax.Precision.HIGHEST, preferred_ele...  78.6 us
    reduce_sum x8, other arithmetic, one_block(): return (jnp.sum(factor * real_den, 0), -jnp.sum(factor * imag_den, 0))  31.5 us
  transfers between devices with their start and end apart: 4, of which 4 were waited for; matrix products, arithmetic and copies ran while one was open for 6% of the time, Pallas kernels for 0%

commit v1 on v0

v1 whole, which is shorter than its diff:
```python
import functools

import jax
import jax.numpy as jnp
from jax import lax
from jax.experimental import pallas as pl
from jax.experimental.pallas import tpu as pltpu
from jax.sharding import PartitionSpec as P

SEG = 8
CHUNK = 8
LANES = 128
GROUPS = 1
BLOCK = 512


def row(ref, index, lanes):
    return jnp.broadcast_to(ref[pl.ds(index, 1), lanes], (SEG, LANES))


def gather_states(key_ref, value_ref, decays_ref, signal_ref, sums_ref, scan_ref, end_ref, natural, damp, damp_chunk):
    rows, width = key_ref.shape
    modes = decays_ref.shape[0]
    seg_len = rows // SEG
    chunks = seg_len // CHUNK
    segment = lax.broadcasted_iota(jnp.int32, (SEG, LANES), 0)

    @pl.loop(0, width // LANES)
    def _(block):
        lanes = pl.ds(pl.multiple_of(block * LANES, LANES), LANES)
        natural[...] = key_ref[:, lanes].astype(jnp.float32) * value_ref[:, lanes].astype(jnp.float32)
        decay = decays_ref[:, lanes]
        damp[...] = jnp.exp(-decay)
        damp_chunk[...] = jnp.exp(-CHUNK * decay)
        every = slice(None)

        def one_chunk(chunk, states):
            signal = [natural[pl.ds(chunk * CHUNK + step, SEG, stride=seg_len), :] for step in range(CHUNK)]
            for step in range(CHUNK):
                signal_ref[chunk * CHUNK + step, :, lanes] = signal[step]
            result = []
            for mode in range(modes):
                factor = row(damp, mode, every)
                total = signal[0]
                for step in range(1, CHUNK):
                    total = total * factor + signal[step]
                sums_ref[chunk, mode, :, lanes] = total
                result.append(states[mode] * row(damp_chunk, mode, every) + total)
            return result

        zeros = jnp.zeros((SEG, LANES), jnp.float32)
        states = lax.fori_loop(0, chunks, one_chunk, [zeros] * modes)
        for mode in range(modes):
            state = states[mode]
            decay_mode = row(decays_ref, mode, lanes)
            reach = 1
            while reach < SEG:
                factor = jnp.where(segment >= reach, jnp.exp(-(reach * seg_len) * decay_mode), 0.0)
                state = state + factor * pltpu.roll(state, reach, 0)
                reach *= 2
            scan_ref[mode, :, lanes] = state
            end_ref[pl.ds(mode, 1), lanes] = state[SEG - 1 :, :]


def near_terms(signal_ref, residues_ref, decays_ref, skip_ref, near_ref):
    steps, _, width = signal_ref.shape
    chunks = steps // CHUNK

    @pl.loop(0, width // LANES)
    def _(block):
        lanes = pl.ds(pl.multiple_of(block * LANES, LANES), LANES)
        decay = decays_ref[:, lanes]
        term = residues_ref[:, lanes] * jnp.sqrt(decay)
        damp = jnp.exp(-decay)
        taps = []
        for step in range(CHUNK):
            tap = jnp.sum(term, 0, keepdims=True)
            if step == 0:
                tap = tap + skip_ref[:, lanes]
            taps.append(jnp.broadcast_to(tap, (SEG, LANES)))
            term = term * damp

        @pl.loop(0, chunks)
        def _(chunk):
            signal = [signal_ref[chunk * CHUNK + step, :, lanes] for step in range(CHUNK)]
            for step in range(CHUNK):
                total = taps[0] * signal[step]
                for back in range(1, step + 1):
                    total = total + taps[back] * signal[step - back]
                near_ref[chunk * CHUNK + step, :, lanes] = total


def spread_states(query_ref, near_ref, sums_ref, scan_ref, enter_ref, residues_ref, decays_ref, mixed_ref, natural, damp, weight):
    rows, width = query_ref.shape
    modes = decays_ref.shape[0]
    seg_len = rows // SEG
    chunks = seg_len // CHUNK
    segment = lax.broadcasted_iota(jnp.int32, (SEG, LANES), 0)
    passed = (segment * seg_len).astype(jnp.float32)

    @pl.loop(0, width // LANES)
    def _(block):
        lanes = pl.ds(pl.multiple_of(block * LANES, LANES), LANES)
        decay = decays_ref[:, lanes]
        damp[...] = jnp.exp(-decay)
        weight[...] = residues_ref[:, lanes] * jnp.sqrt(decay) * damp[...]
        every = slice(None)
        states = []
        for mode in range(modes):
            before = jnp.where(segment >= 1, pltpu.roll(scan_ref[mode, :, lanes], 1, 0), 0.0)
            state = before + jnp.exp(-passed * row(decays_ref, mode, lanes)) * row(enter_ref, mode, lanes)
            states.append(state * row(weight, mode, every))

        def one_chunk(chunk, states):
            conv = [near_ref[chunk * CHUNK + step, :, lanes] for step in range(CHUNK)]
            result = []
            for mode in range(modes):
                factor = row(damp, mode, every)
                state = states[mode]
                for step in range(CHUNK):
                    conv[step] = conv[step] + state
                    state = state * factor
                result.append(state + row(weight, mode, every) * sums_ref[chunk, mode, :, lanes])
            for step in range(CHUNK):
                natural[pl.ds(chunk * CHUNK + step, SEG, stride=seg_len), :] = conv[step]
            return result

        lax.fori_loop(0, chunks, one_chunk, states)
        mixed_ref[:, lanes] = (query_ref[:, lanes].astype(jnp.float32) * natural[...]).astype(jnp.bfloat16)


def shards(query_gate, key_gate, value_input, residues, decays, skip_gain):
    rows, width = key_gate.shape
    modes = residues.shape[0]
    seg_len = rows // SEG
    chunks = seg_len // CHUNK
    ctx_size = lax.axis_size("ctx")
    ctx_rank = lax.axis_index("ctx")
    skip_gain = skip_gain[None, :]
    group = width // GROUPS
    block = min(BLOCK, group)
    blocks = group // block
    real = functools.partial(jax.ShapeDtypeStruct, dtype=jnp.float32)
    scratch = [pltpu.VMEM((rows, LANES), jnp.float32)] + [pltpu.VMEM((modes, LANES), jnp.float32)] * 2
    params = pltpu.CompilerParams(vmem_limit_bytes=48 * 2**20)
    points = rows * group

    def flat(count, part=0):
        return pl.BlockSpec((count, block), lambda i: (0, part * blocks + i))

    def deep(*lead):
        return pl.BlockSpec(lead + (block,), lambda i: (0,) * len(lead) + (i,))

    first, mixed = [], []
    for part in range(GROUPS):
        first.append(
            pl.pallas_call(
                gather_states,
                grid=(blocks,),
                in_specs=[flat(rows, part), flat(rows, part), flat(modes, part)],
                out_specs=[deep(seg_len, SEG), deep(chunks, modes, SEG), deep(modes, SEG), flat(modes)],
                out_shape=[
                    real((seg_len, SEG, group)),
                    real((chunks, modes, SEG, group)),
                    real((modes, SEG, group)),
                    real((modes, group)),
                ],
                scratch_shapes=scratch,
                compiler_params=params,
                cost_estimate=pl.CostEstimate(flops=2 * modes * points, bytes_accessed=8 * points, transcendentals=0),
                name="gather_states",
            )(key_gate, value_input, decays)
        )
    enters = []
    for part in range(GROUPS):
        decay = decays[:, part * group : (part + 1) * group]
        total = first[part][3]
        enter = jnp.zeros_like(total)
        reach = 1
        while reach < ctx_size:
            come = lax.ppermute(total, "ctx", [(i, i ^ reach) for i in range(ctx_size)])
            upper = (ctx_rank // reach) % 2 == 1
            behind = (ctx_rank % reach * rows).astype(jnp.float32)
            enter = enter + jnp.where(upper, jnp.exp(-behind * decay) * come, 0.0)
            over = jnp.exp(-float(reach * rows) * decay)
            total = jnp.where(upper, total + over * come, come + over * total)
            reach *= 2
        enters.append(enter)
    for part in range(GROUPS):
        signal, sums, scan, _ = first[part]
        near = pl.pallas_call(
            near_terms,
            grid=(blocks,),
            in_specs=[deep(seg_len, SEG), flat(modes, part), flat(modes, part), flat(1, part)],
            out_specs=deep(seg_len, SEG),
            out_shape=real((seg_len, SEG, group)),
            compiler_params=params,
            cost_estimate=pl.CostEstimate(flops=9 * points, bytes_accessed=8 * points, transcendentals=0),
            name="near_terms",
        )(signal, residues, decays, skip_gain)
        mixed.append(
            pl.pallas_call(
                spread_states,
                grid=(blocks,),
                in_specs=[
                    flat(rows, part),
                    deep(seg_len, SEG),
                    deep(chunks, modes, SEG),
                    deep(modes, SEG),
                    flat(modes),
                    flat(modes, part),
                    flat(modes, part),
                ],
                out_specs=flat(rows),
                out_shape=jax.ShapeDtypeStruct((rows, group), jnp.bfloat16),
                scratch_shapes=scratch,
                compiler_params=params,
                cost_estimate=pl.CostEstimate(flops=2 * modes * points, bytes_accessed=12 * points, transcendentals=0),
                name="spread_states",
            )(query_gate, near, sums, scan, enters[part], residues, decays)
        )
    return jnp.concatenate(mixed, 1)


def solution(mesh):
    placed = (
        P("ctx", "chan"),
        P("ctx", "chan"),
        P("ctx", "chan"),
        P(None, "chan"),
        P(None, "chan"),
        P("chan"),
    )
    return jax.shard_map(shards, mesh=mesh, in_specs=placed, out_specs=P("ctx", "chan"), check_vma=False)
```

time: 940 us -> 42.9 us (0.05)
  waiting for transfers between devices: 595 us -> 3.5 us
  other arithmetic: 107 us -> 0.1 us
  blocking collectives: 96.2 us -> 0 us
  matrix products: 78.6 us -> 0 us
  Pallas kernels: 0 us -> 27.2 us
  local copies, waits for them, and re-layouts: 24.5 us -> 6.06 us
  between operations: 13.8 us -> 0.04 us
  starting transfers between devices: 17.8 us -> 5.84 us
    all_to_all x3 -> x0, waiting for transfers between devices: 489 us -> none  [the longest x2 347 us: spread_positions(): lax.all_to_all(field, 'ctx', split_axis=1, concat_axis=1, tiled=True)]
    psum x1 -> x0, waiting for transfers between devices: 107 us -> none  [shards(): full_conv = lax.psum(half_term, 'half')]
    all_to_all x1 -> x0, blocking collectives: 96.2 us -> none  [spread_positions(): lax.all_to_all(half_term, 'ctx', split_axis=0, concat_axis=1, tiled=True)]
    dot_general x4 -> x0, matrix products: 78.6 us -> none  [apply_table(): jnp.dot(matrix, flat_data, precision=lax.Precision.HIGHEST, preferred_ele...]
    reduce_sum x8 -> x0, other arithmetic: 31.5 us -> none  [one_block(): return (jnp.sum(factor * real_den, 0), -jnp.sum(factor * imag_den, 0))]
    pallas_call x0 -> x3, Pallas kernels: none -> 27.2 us  [the longest x1 11.4 us: shards(): pl.pallas_call(gather_states, grid=(blocks,), in_specs=[flat(rows, part),...]
    all_to_all x3 -> x0, starting transfers between devices: 17.6 us -> none  [the longest x2 12 us: spread_positions(): lax.all_to_all(field, 'ctx', split_axis=1, concat_axis=1, tiled=True)]
    sub x3 -> x0, other arithmetic: 17.2 us -> none  [rotate(): real_out = cosine * field[0] - sine_part * field[1]]
  transfers between devices with their start and end apart: 4 -> 2, of which waited for: 4 -> 1; matrix products, arithmetic and copies ran while one was open for 6% -> 0% of each run, Pallas kernels for 0% -> 11%
where the time goes in v1:
time: 42.9 us; the launch traced here: 42.7 us
  Pallas kernels  27.2 us (63%)
  local copies, waits for them, and re-layouts  6.06 us (14%)
  starting transfers between devices  5.84 us (14%)
  waiting for transfers between devices  3.5 us (8%)
    pallas_call x1, Pallas kernels, shards(): pl.pallas_call(gather_states, grid=(blocks,), in_specs=[flat(rows, part),...  11.4 us
    pallas_call x1, Pallas kernels, shards(): pl.pallas_call(spread_states, grid=(blocks,), in_specs=[flat(rows, part),...  10.9 us
    unnamed x16, local copies, waits for them, and re-layouts  6.06 us
    ppermute x2, starting transfers between devices, shards(): come = lax.ppermute(total, 'ctx', [(i, i ^ reach) for i in range(ctx_size)])  5.84 us
    pallas_call x1, Pallas kernels, shards(): pl.pallas_call(near_terms, grid=(blocks,), in_specs=[deep(seg_len, SEG),...  4.82 us
    ppermute x2, waiting for transfers between devices, shards(): come = lax.ppermute(total, 'ctx', [(i, i ^ reach) for i in range(ctx_size)])  3.5 us
  transfers between devices with their start and end apart: 2, of which 1 were waited for; matrix products, arithmetic and copies ran while one was open for 0% of the time, Pallas kernels for 11%

profile of v1, /device:TPU:0, one launch (start us, length us, event | category | flops | bytes accessed | tf_op | source)
XLA Modules:
  0.0 42.7 jit_solution(17346135203170582432)
XLA Ops:
  0.0 0.0 copy-start.1
  0.0 0.9 %copy-done.1 = f32[16,2048]{1,0:T(8,128)S(1)} copy-done((f32[16,2048]{1,0:T(8,128)S(1)}, f32[16,2048]{1,0:T(8,128)}, u32[]{:S(2)}) %copy-start.1) | copy-done | bytes 131096
  0.9 0.0 copy-start.4
  0.9 1.6 %copy-done.4 = bf16[512,2048]{1,0:T(8,128)(2,1)S(1)} copy-done((bf16[512,2048]{1,0:T(8,128)(2,1)S(1)}, bf16[512,2048]{1,0:T(8,128)(2,1)}, u32[]{:S(2)}) %copy-start.4) | copy-done | bytes 2097176
  2.5 0.0 copy-start.5
  2.5 1.6 %copy-done.5 = bf16[512,2048]{1,0:T(8,128)(2,1)S(1)} copy-done((bf16[512,2048]{1,0:T(8,128)(2,1)S(1)}, bf16[512,2048]{1,0:T(8,128)(2,1)}, u32[]{:S(2)}) %copy-start.5) | copy-done | bytes 2097176
  4.1 0.0 copy-start.2
  4.1 0.0 copy-start.6
  4.1 0.0 copy-start.7
  4.1 11.4 %gather_states.1 = (f32[64,8,2048]{2,1,0:T(8,128)}, f32[8,16,8,2048]{3,2,1,0:T(8,128)}, f32[16,8,2048]{2,1,0:T(8,128)S(1)}, f32[16,2048]{1,0:T(8,128)S(1)}) custom-call(bf16[512,2048]{1,0:T(8,128)(2,1)S(1)} %copy-done.4, bf16[512,2048]{1,0:T(8,128)(2,1)S(1)} %copy-done.5, f32[16,2048]{1,0:T(8,128)S(1)} %copy-done.1), custom_call_target="tpu_custom_call" | custom-call | flops 33554432 | bytes 8388608 | tf_op jit(solution)/shard_map/gather_states/pallas_call | solution.py:157
  15.5 3.0 %collective-permute-start = (f32[16,2048]{1,0:T(8,128)S(1)}, f32[16,2048]{1,0:T(8,128)S(1)}, u32[]{:S(2)}, u32[]{:S(2)}) collective-permute-start(f32[16,2048]{1,0:T(8,128)S(1)} %get-tuple-element.12), channel_id=1, source_target_pairs={{0,1},{1,0},{2,3},{3,2},{4,5},{5,4},{6,7},{7,6},{8,9},{9,8},{10,11... | collective-permute-start | bytes 393224 | tf_op jit(solution)/shard_map/ppermute | solution.py:181
  18.5 3.5 %collective-permute-done = f32[16,2048]{1,0:T(8,128)S(1)} collective-permute-done((f32[16,2048]{1,0:T(8,128)S(1)}, f32[16,2048]{1,0:T(8,128)S(1)}, u32[]{:S(2)}, u32[]{:S(2)}) %collective-permute-start) | collective-permute-done | bytes 131104 | tf_op jit(solution)/shard_map/ppermute | solution.py:181
  22.0 0.0 copy-done.2
  22.1 2.8 %collective-permute-start.1 = (f32[16,2048]{1,0:T(8,128)S(1)}, f32[16,2048]{1,0:T(8,128)S(1)}, u32[]{:S(2)}, u32[]{:S(2)}) collective-permute-start(f32[16,2048]{1,0:T(8,128)S(1)} %add_select_fusion), channel_id=1, source_target_pairs={{0,2},{1,3},{2,0},{3,1},{4,6},{5,7},{6,4},{7,5},{8,10},{9,11},{10,... | collective-permute-start | bytes 393224 | tf_op jit(solution)/shard_map/ppermute | solution.py:181
  24.9 0.0 copy-done.6
  24.9 0.0 copy-done.7
  24.9 0.0 copy-start.3
  24.9 4.8 %near_terms.1.near_ref = f32[64,8,2048]{2,1,0:T(8,128)S(1)} custom-call(f32[64,8,2048]{2,1,0:T(8,128)} %get-tuple-element.9.signal_ref, f32[16,2048]{1,0:T(8,128)S(1)} %copy-done.6, f32[16,2048]{1,0:T(8,128)S(1)} %copy-done.2, f32[1,2048]{1,0:T(1,128)S(1)} %bitcast.1), custom_call_target="tpu_custom_call" | custom-call | flops 9437184 | bytes 8388608 | tf_op jit(solution)/shard_map/near_terms/pallas_call | solution.py:191
  29.7 0.0 copy-start
  29.7 2.0 %copy-done = f32[64,8,2048]{2,1,0:T(8,128)} copy-done((f32[64,8,2048]{2,1,0:T(8,128)}, f32[64,8,2048]{2,1,0:T(8,128)S(1)}, u32[]{:S(2)}) %copy-start) | copy-done | bytes 4194328
  31.7 0.0 collective-permute-done.1
  31.7 0.1 select_add_fusion.enter_ref
  31.7 0.0 copy-done.3
  31.8 10.9 %spread_states.1 = bf16[512,2048]{1,0:T(8,128)(2,1)} custom-call(bf16[512,2048]{1,0:T(8,128)(2,1)S(1)} %copy-done.3, f32[64,8,2048]{2,1,0:T(8,128)} %copy-done, f32[8,16,8,2048]{3,2,1,0:T(8,128)} %get-tuple-element.10.sums_ref, f32[16,8,2048]{2,1,0:T(8,128)S(1)} %get-tuple-element.11.scan_ref, f32[16,2048]{1,0:T(8,128)S(1)} %select_add_fusion.enter_ref, ...), custom_call_target="tpu_custom_call" | custom-call | flops 33554432 | bytes 12582912 | tf_op jit(solution)/shard_map/spread_states/pallas_call | solution.py:202
  (1 shorter events, 0.0 us)
Async XLA Ops:
  0.0 0.9 %copy-start.1 = (f32[16,2048]{1,0:T(8,128)S(1)}, f32[16,2048]{1,0:T(8,128)}, u32[]{:S(2)}) copy-start(f32[16,2048]{1,0:T(8,128)} %decays_ref.5) | copy-start | bytes 393220
  0.9 1.6 %copy-start.4 = (bf16[512,2048]{1,0:T(8,128)(2,1)S(1)}, bf16[512,2048]{1,0:T(8,128)(2,1)}, u32[]{:S(2)}) copy-start(bf16[512,2048]{1,0:T(8,128)(2,1)} %key_ref.1) | copy-start | bytes 6291460
  2.5 1.6 %copy-start.5 = (bf16[512,2048]{1,0:T(8,128)(2,1)S(1)}, bf16[512,2048]{1,0:T(8,128)(2,1)}, u32[]{:S(2)}) copy-start(bf16[512,2048]{1,0:T(8,128)(2,1)} %value_ref.1) | copy-start | bytes 6291460
  4.1 17.9 %copy-start.2 = (f32[16,2048]{1,0:T(8,128)S(1)}, f32[16,2048]{1,0:T(8,128)}, u32[]{:S(2)}) copy-start(f32[16,2048]{1,0:T(8,128)} %decays_ref.5) | copy-start | bytes 393220
  4.1 20.8 %copy-start.6 = (f32[16,2048]{1,0:T(8,128)S(1)}, f32[16,2048]{1,0:T(8,128)}, u32[]{:S(2)}) copy-start(f32[16,2048]{1,0:T(8,128)} %residues_ref.3) | copy-start | bytes 393220
  4.1 20.8 %copy-start.7 = (f32[2048]{0:T(1024)S(1)}, f32[2048]{0:T(1024)}, u32[]{:S(2)}) copy-start(f32[2048]{0:T(1024)} %param.11) | copy-start | bytes 24580
  15.5 6.5 %collective-permute-start = (f32[16,2048]{1,0:T(8,128)S(1)}, f32[16,2048]{1,0:T(8,128)S(1)}, u32[]{:S(2)}, u32[]{:S(2)}) collective-permute-start(f32[16,2048]{1,0:T(8,128)S(1)} %get-tuple-element.12), channel_id=1, source_target_pairs={{0,1},{1,0},{2,3},{3,2},{4,5},{5,4},{6,7},{7,6},{8,9},{9,8},{10,11... | collective-permute-start | bytes 393224 | tf_op jit(solution)/shard_map/ppermute | solution.py:181
  22.1 9.6 %collective-permute-start.1 = (f32[16,2048]{1,0:T(8,128)S(1)}, f32[16,2048]{1,0:T(8,128)S(1)}, u32[]{:S(2)}, u32[]{:S(2)}) collective-permute-start(f32[16,2048]{1,0:T(8,128)S(1)} %add_select_fusion), channel_id=1, source_target_pairs={{0,2},{1,3},{2,0},{3,1},{4,6},{5,7},{6,4},{7,5},{8,10},{9,11},{10,... | collective-permute-start | bytes 393224 | tf_op jit(solution)/shard_map/ppermute | solution.py:181
  24.9 6.9 %copy-start.3 = (bf16[512,2048]{1,0:T(8,128)(2,1)S(1)}, bf16[512,2048]{1,0:T(8,128)(2,1)}, u32[]{:S(2)}) copy-start(bf16[512,2048]{1,0:T(8,128)(2,1)} %query_ref.1) | copy-start | bytes 6291460
  29.7 2.0 %copy-start = (f32[64,8,2048]{2,1,0:T(8,128)}, f32[64,8,2048]{2,1,0:T(8,128)S(1)}, u32[]{:S(2)}) copy-start(f32[64,8,2048]{2,1,0:T(8,128)S(1)} %near_terms.1.near_ref) | copy-start | bytes 12582916

commit v2 on v1

v2 whole, which is shorter than its diff:
```python
import functools

import jax
import jax.numpy as jnp
from jax import lax
from jax.experimental import pallas as pl
from jax.experimental.pallas import tpu as pltpu
from jax.sharding import PartitionSpec as P

SEG = 8
CHUNK = 8
LANES = 128
GROUPS = 2
SLABS = (0, 1, 4)
MIB = 2**20

VMEM = pl.BlockSpec(memory_space=pltpu.VMEM)
HBM = pl.BlockSpec(memory_space=pltpu.HBM)


def row(ref, index, lanes=slice(None)):
    return jnp.broadcast_to(ref[pl.ds(index, 1), lanes], (SEG, LANES))


def lane_block(block):
    return pl.ds(pl.multiple_of(block * LANES, LANES), LANES)


def gather_states(
    first, key_ref, value_ref, decays_ref, signal_ref, sums_ref, scan_ref, end_ref, keys, values, rates, natural, turned, damp, damp_chunk, sems
):
    rows, width = keys.shape
    modes = rates.shape[0]
    blocks = width // LANES
    seg_len = rows // SEG
    chunks = seg_len // CHUNK
    pitch = seg_len + 1

    rate_copy = pltpu.make_async_copy(decays_ref.at[:, pl.ds(first, width)], rates, sems.at[2, 0])
    starts = [start for start in SLABS if start < blocks]
    slabs = []
    for index, (start, stop) in enumerate(zip(starts, starts[1:] + [blocks])):
        inner = pl.ds(start * LANES, (stop - start) * LANES)
        outer = pl.ds(first + start * LANES, (stop - start) * LANES)
        slabs.append(
            (
                pltpu.make_async_copy(key_ref.at[:, outer], keys.at[:, inner], sems.at[0, index]),
                pltpu.make_async_copy(value_ref.at[:, outer], values.at[:, inner], sems.at[1, index]),
            )
        )
        for copy in slabs[-1]:
            copy.start()
        if index == 0:
            rate_copy.start()
    rate_copy.wait()

    @pl.loop(0, blocks)
    def _(block):
        lanes = lane_block(block)
        decay = rates[:, lanes]
        damp[...] = jnp.exp(-decay)
        damp_chunk[...] = jnp.exp(-CHUNK * decay)
        damp_segment = jnp.exp(-seg_len * decay)
        for start, copies in zip(starts, slabs):

            @pl.when(block == start)
            def _(copies=copies):
                for copy in copies:
                    copy.wait()

        for start in range(0, rows, 16):
            part = pl.ds(start, 16)
            place = start // seg_len * pitch + start % seg_len
            natural[pl.ds(place, 16), :] = keys[part, lanes].astype(jnp.float32) * values[part, lanes].astype(jnp.float32)
        states = [None] * modes
        for chunk in range(chunks):
            signal = [natural[pl.ds(chunk * CHUNK + step, SEG, stride=pitch), :] for step in range(CHUNK)]
            for step in range(CHUNK):
                signal_ref[chunk * CHUNK + step, :, lanes] = signal[step]
            for mode in range(modes):
                factor = row(damp, mode)
                total = signal[0]
                for step in range(1, CHUNK):
                    total = total * factor + signal[step]
                if chunk < chunks - 1:
                    sums_ref[chunk, mode, :, lanes] = total
                states[mode] = total if chunk == 0 else states[mode] * row(damp_chunk, mode) + total
        for mode in range(modes):
            turned[pl.ds(mode * (SEG + 1), SEG), :] = states[mode]
        state = jnp.zeros((modes, LANES), jnp.float32)
        for segment in range(SEG):
            scan_ref[segment, :, lanes] = state
            state = state * damp_segment + turned[pl.ds(segment, modes, stride=SEG + 1), :]
        end_ref[:, lanes] = state


def carry(first, positions, reach, opening, final, rank_ref, decays_ref, come_ref, *refs):
    decay = decays_ref[:, pl.ds(first, come_ref.shape[1])]
    come = come_ref[...]
    rank = rank_ref[0]
    upper = rank & reach != 0
    behind = ((rank & (reach - 1)) * (positions // reach)).astype(jnp.float32)
    refs = list(refs)
    total = None if final else refs.pop(0)[...]
    enter = 0.0 if opening else refs.pop(0)[...]
    refs[0][...] = enter + jnp.where(upper, jnp.exp(-behind * decay) * come, 0.0)
    if not final:
        over = jnp.exp(-positions * decay)
        refs[1][...] = jnp.where(upper, total + over * come, come + over * total)


def near_terms(first, signal_ref, residues_ref, decays_ref, skip_ref, near_ref):
    steps, _, width = signal_ref.shape
    chunks = steps // CHUNK

    @pl.loop(0, width // LANES)
    def _(block):
        lanes = lane_block(block)
        wide = pl.ds(pl.multiple_of(first + block * LANES, LANES), LANES)
        decay = decays_ref[:, wide]
        term = residues_ref[:, wide] * jnp.sqrt(decay)
        damp = jnp.exp(-decay)
        taps = []
        for step in range(CHUNK):
            tap = jnp.sum(term, 0, keepdims=True)
            if step == 0:
                tap = tap + skip_ref[:, wide]
            taps.append(jnp.broadcast_to(tap, (SEG, LANES)))
            term = term * damp
        for chunk in range(chunks):
            signal = [signal_ref[chunk * CHUNK + step, :, lanes] for step in range(CHUNK)]
            for step in range(CHUNK):
                total = taps[0] * signal[step]
                for back in range(1, step + 1):
                    total = total + taps[back] * signal[step - back]
                near_ref[chunk * CHUNK + step, :, lanes] = total


def spread_states(
    first, query_ref, near_ref, sums_ref, scan_ref, enter_ref, residues_ref, decays_ref, held_ref, mixed_ref, natural, turned, damp, weight, gated, sems
):
    rows = query_ref.shape[0]
    blocks = gated.shape[0]
    modes = decays_ref.shape[0]
    seg_len = rows // SEG
    chunks = seg_len // CHUNK
    pitch = seg_len + 1

    def copy(block):
        wide = pl.ds(pl.multiple_of(first + block * LANES, LANES), LANES)
        return pltpu.make_async_copy(gated.at[block], mixed_ref.at[:, wide], sems.at[block])

    @pl.loop(0, blocks)
    def _(block):
        lanes = lane_block(block)
        wide = pl.ds(pl.multiple_of(first + block * LANES, LANES), LANES)
        decay = decays_ref[:, wide]
        damp[...] = jnp.exp(-decay)
        scale = residues_ref[:, wide] * jnp.sqrt(decay) * jnp.exp(-decay)
        weight[...] = scale
        damp_segment = jnp.exp(-seg_len * decay)
        enter = enter_ref[:, lanes]
        for segment in range(SEG):
            turned[pl.ds(segment * (modes + 1), modes), :] = (scan_ref[segment, :, lanes] + enter) * scale
            enter = enter * damp_segment
        states = [turned[pl.ds(mode, SEG, stride=modes + 1), :] for mode in range(modes)]
        for chunk in range(chunks):
            conv = [near_ref[chunk * CHUNK + step, :, lanes] for step in range(CHUNK)]
            for mode in range(modes):
                factor = row(damp, mode)
                state = states[mode]
                for step in range(CHUNK):
                    conv[step] = conv[step] + state
                    if step < CHUNK - 1 or chunk < chunks - 1:
                        state = state * factor
                if chunk < chunks - 1:
                    states[mode] = state + row(weight, mode) * sums_ref[chunk, mode, :, lanes]
            for step in range(CHUNK):
                natural[pl.ds(chunk * CHUNK + step, SEG, stride=pitch), :] = conv[step]
        for start in range(0, rows, 16):
            part = pl.ds(start, 16)
            place = start // seg_len * pitch + start % seg_len
            gated[block, part, :] = (query_ref[part, wide].astype(jnp.float32) * natural[pl.ds(place, 16), :]).astype(jnp.bfloat16)
        copy(block).start()

    @pl.loop(0, blocks)
    def _(block):
        copy(block).wait()


def shards(query_gate, key_gate, value_input, residues, decays, skip_gain):
    rows, width = key_gate.shape
    modes = residues.shape[0]
    seg_len = rows // SEG
    chunks = seg_len // CHUNK
    ctx_size = lax.axis_size("ctx")
    ctx_rank = lax.axis_index("ctx")
    skip_gain = skip_gain[None, :]
    group = width // GROUPS
    blocks = group // LANES
    real = functools.partial(pltpu.VMEM, dtype=jnp.float32)
    natural = pltpu.VMEM((SEG * (seg_len + 1), LANES), jnp.float32)
    table = pltpu.VMEM((modes, LANES), jnp.float32)
    points = rows * group

    gathered = []
    for part in range(GROUPS):
        gathered.append(
            pl.pallas_call(
                functools.partial(gather_states, part * group),
                in_specs=[HBM, HBM, HBM],
                out_specs=[VMEM] * 4,
                out_shape=[
                    real((seg_len, SEG, group)),
                    real((chunks - 1, modes, SEG, group)),
                    real((SEG, modes, group)),
                    real((modes, group)),
                ],
                scratch_shapes=[
                    pltpu.VMEM((rows, group), jnp.bfloat16),
                    pltpu.VMEM((rows, group), jnp.bfloat16),
                    pltpu.VMEM((modes, group), jnp.float32),
                    natural,
                    pltpu.VMEM((modes * (SEG + 1), LANES), jnp.float32),
                    table,
                    table,
                    pltpu.SemaphoreType.DMA((3, len(SLABS))),
                ],
                compiler_params=pltpu.CompilerParams(vmem_limit_bytes=12 * MIB),
                cost_estimate=pl.CostEstimate(flops=2 * modes * points, bytes_accessed=4 * points, transcendentals=0),
                name="gather_states",
            )(*(pltpu.with_memory_space_constraint(array, pltpu.HBM) for array in (key_gate, value_input, decays)))
        )
    rank = ctx_rank.astype(jnp.int32).reshape(1)
    enters = []
    for part in range(GROUPS):
        total = gathered[part][3]
        enter = None
        reach = 1
        while reach < ctx_size:
            come = lax.ppermute(total, "ctx", [(i, i ^ reach) for i in range(ctx_size)])
            final = 2 * reach == ctx_size
            operands = [rank, decays, come] + ([] if final else [total]) + ([] if enter is None else [enter])
            result = pl.pallas_call(
                functools.partial(carry, part * group, reach * rows, reach, reach == 1, final),
                in_specs=[pl.BlockSpec(memory_space=pltpu.SMEM)] + [VMEM] * (len(operands) - 1),
                out_specs=[VMEM] * (1 if final else 2),
                out_shape=[real((modes, group))] * (1 if final else 2),
                compiler_params=pltpu.CompilerParams(vmem_limit_bytes=4 * MIB),
                name="carry",
            )(*operands)
            enter = result[0]
            total = result[-1]
            reach *= 2
        enters.append(enter)
    mixed = None
    for part in range(GROUPS):
        signal, sums, scan, _ = gathered[part]
        near = pl.pallas_call(
            functools.partial(near_terms, part * group),
            in_specs=[VMEM] * 4,
            out_specs=VMEM,
            out_shape=real((seg_len, SEG, group)),
            compiler_params=pltpu.CompilerParams(vmem_limit_bytes=12 * MIB),
            cost_estimate=pl.CostEstimate(flops=9 * points, bytes_accessed=0, transcendentals=0),
            name="near_terms",
        )(signal, residues, decays, skip_gain)
        operands = [query_gate, near, sums, scan, enters[part], residues, decays]
        specs = [VMEM] * 7
        aliases = {}
        body = functools.partial(spread_states, part * group)
        if part:
            operands.append(mixed)
            specs.append(HBM)
            aliases = {7: 0}
        else:
            body = functools.partial(lambda body, *refs: body(*refs[:7], None, *refs[7:]), body)
        mixed = pl.pallas_call(
            body,
            in_specs=specs,
            out_specs=HBM,
            out_shape=jax.ShapeDtypeStruct((rows, width), jnp.bfloat16),
            input_output_aliases=aliases,
            scratch_shapes=[
                natural,
                pltpu.VMEM((SEG * (modes + 1), LANES), jnp.float32),
                table,
                table,
                pltpu.VMEM((blocks, rows, LANES), jnp.bfloat16),
                pltpu.SemaphoreType.DMA((blocks,)),
            ],
            compiler_params=pltpu.CompilerParams(vmem_limit_bytes=12 * MIB),
            cost_estimate=pl.CostEstimate(flops=2 * modes * points, bytes_accessed=2 * points, transcendentals=0),
            name="spread_states",
        )(*operands)
    return mixed


def solution(mesh):
    placed = (
        P("ctx", "chan"),
        P("ctx", "chan"),
        P("ctx", "chan"),
        P(None, "chan"),
        P(None, "chan"),
        P("chan"),
    )
    return jax.shard_map(shards, mesh=mesh, in_specs=placed, out_specs=P("ctx", "chan"), check_vma=False)
```

time: 42.9 us -> 35.4 us (0.83)
  Pallas kernels: 27.2 us -> 19.3 us
  starting transfers between devices: 5.84 us -> 8.37 us
  waiting for transfers between devices: 3.5 us -> 1.1 us
    pallas_call x3 -> x10, Pallas kernels: 27.2 us -> 19.3 us  [the longest x2 8.25 us: shards(): pl.pallas_call(functools.partial(gather_states, part * group), in_specs=[...]
    ppermute x2 -> x4, starting transfers between devices: 5.84 us -> 8.37 us  [shards(): come = lax.ppermute(total, 'ctx', [(i, i ^ reach) for i in range(ctx_size)])]
    ppermute x2 -> x4, waiting for transfers between devices: 3.5 us -> 1.1 us  [shards(): come = lax.ppermute(total, 'ctx', [(i, i ^ reach) for i in range(ctx_size)])]
    unnamed x16 -> x20, local copies, waits for them, and re-layouts: 6.06 us -> 6.27 us
  transfers between devices with their start and end apart: 2 -> 4, of which waited for: 1 -> 1; matrix products, arithmetic and copies ran while one was open for 0% -> 0% of each run, Pallas kernels for 11% -> 32%
where the time goes in v2:
time: 35.4 us; the launch traced here: 35.2 us
  Pallas kernels  19.3 us (55%)
  starting transfers between devices  8.37 us (24%)
  local copies, waits for them, and re-layouts  6.27 us (18%)
  waiting for transfers between devices  1.1 us (3%)
    ppermute x4, starting transfers between devices, shards(): come = lax.ppermute(total, 'ctx', [(i, i ^ reach) for i in range(ctx_size)])  8.37 us
    pallas_call x2, Pallas kernels, shards(): pl.pallas_call(functools.partial(gather_states, part * group), in_specs=[...  8.25 us
    pallas_call x2, Pallas kernels, shards(): pl.pallas_call(body, in_specs=specs, out_specs=HBM, out_shape=jax.ShapeDt...  7.6 us
    unnamed x20, local copies, waits for them, and re-layouts  6.27 us
    pallas_call x4, Pallas kernels, shards(): pl.pallas_call(functools.partial(carry, part * group, reach * rows, reach...  1.95 us
    pallas_call x2, Pallas kernels, shards(): pl.pallas_call(functools.partial(near_terms, part * group), in_specs=[VME...  1.52 us
    ppermute x4, waiting for transfers between devices, shards(): come = lax.ppermute(total, 'ctx', [(i, i ^ reach) for i in range(ctx_size)])  1.1 us
  transfers between devices with their start and end apart: 4, of which 1 were waited for; matrix products, arithmetic and copies ran while one was open for 0% of the time, Pallas kernels for 32%

profile of v2, /device:TPU:0, one launch (start us, length us, event | category | flops | bytes accessed | tf_op | source)
XLA Modules:
  0.0 35.2 jit_solution(14119354626260336852)
XLA Ops:
  0.0 4.1 %gather_states.3 = (f32[64,8,1024]{2,1,0:T(8,128)S(1)}, f32[7,16,8,1024]{3,2,1,0:T(8,128)S(1)}, f32[8,16,1024]{2,1,0:T(8,128)S(1)}, f32[16,1024]{1,0:T(8,128)S(1)}) custom-call(bf16[512,2048]{1,0:T(8,128)(2,1)} %key_ref.3, bf16[512,2048]{1,0:T(8,128)(2,1)} %value_ref.3, f32[16,2048]{1,0:T(8,128)} %decays_ref.17), custom_call_target="tpu_custom_call" | custom-call | flops 16777216 | bytes 2097152 | tf_op jit(solution)/shard_map/gather_states/pallas_call | solution.py:209
  4.1 0.0 copy-start.4
  4.1 1.8 %copy-done.4 = f32[7,16,8,1024]{3,2,1,0:T(8,128)} copy-done((f32[7,16,8,1024]{3,2,1,0:T(8,128)}, f32[7,16,8,1024]{3,2,1,0:T(8,128)S(1)}, u32[]{:S(2)}) %copy-start.4) | copy-done | bytes 3670040
  6.0 0.0 copy-start
  6.0 0.0 copy-start.6
  6.0 0.0 copy-start.9
  6.0 3.0 %collective-permute-start.2 = (f32[16,1024]{1,0:T(8,128)S(1)}, f32[16,1024]{1,0:T(8,128)}, u32[]{:S(2)}, u32[]{:S(2)}) collective-permute-start(f32[16,1024]{1,0:T(8,128)S(1)} %get-tuple-element.26.refs_0_), channel_id=1, source_target_pairs={{0,1},{1,0},{2,3},{3,2},{4,5},{5,4},{6,7},{7,6},{8,9},{9,8},{10,11... | collective-permute-start | bytes 196616 | tf_op jit(solution)/shard_map/ppermute | solution.py:241
  9.0 4.1 %gather_states.2 = (f32[64,8,1024]{2,1,0:T(8,128)S(1)}, f32[7,16,8,1024]{3,2,1,0:T(8,128)S(1)}, f32[8,16,1024]{2,1,0:T(8,128)S(1)}, f32[16,1024]{1,0:T(8,128)S(1)}) custom-call(bf16[512,2048]{1,0:T(8,128)(2,1)} %key_ref.3, bf16[512,2048]{1,0:T(8,128)(2,1)} %value_ref.3, f32[16,2048]{1,0:T(8,128)} %decays_ref.17), custom_call_target="tpu_custom_call" | custom-call | flops 16777216 | bytes 2097152 | tf_op jit(solution)/shard_map/gather_states/pallas_call | solution.py:209
  13.2 0.0 copy-start.2
  13.2 1.8 %copy-done.2 = f32[7,16,8,1024]{3,2,1,0:T(8,128)} copy-done((f32[7,16,8,1024]{3,2,1,0:T(8,128)}, f32[7,16,8,1024]{3,2,1,0:T(8,128)S(1)}, u32[]{:S(2)}) %copy-start.2) | copy-done | bytes 3670040
  14.9 0.0 copy-start.7
  14.9 1.3 %copy-done.7 = f32[64,8,1024]{2,1,0:T(8,128)} copy-done((f32[64,8,1024]{2,1,0:T(8,128)}, f32[64,8,1024]{2,1,0:T(8,128)S(1)}, u32[]{:S(2)}) %copy-start.7) | copy-done | bytes 2097176
  16.3 0.1 collective-permute-start
  16.3 0.0 collective-permute-done.2.come_ref
  16.3 0.0 copy-done
  16.3 0.9 %carry.6 = (f32[16,1024]{1,0:T(8,128)S(1)}, f32[16,1024]{1,0:T(8,128)S(1)}) custom-call(s32[1]{0:T(128)} %bitcast.1.rank_ref, f32[16,2048]{1,0:T(8,128)S(1)} %copy-done, f32[16,1024]{1,0:T(8,128)} %collective-permute-done.2.come_ref, f32[16,1024]{1,0:T(8,128)S(1)} %get-tuple-element.26.refs_0_), custom_call_target="tpu_custom_call" | custom-call | tf_op jit(solution)/shard_map/carry/pallas_call | solution.py:244
  17.2 3.0 %collective-permute-start.3 = (f32[16,1024]{1,0:T(8,128)S(1)}, f32[16,1024]{1,0:T(8,128)S(1)}, u32[]{:S(2)}, u32[]{:S(2)}) collective-permute-start(f32[16,1024]{1,0:T(8,128)S(1)} %get-tuple-element.27), channel_id=1, source_target_pairs={{0,2},{1,3},{2,0},{3,1},{4,6},{5,7},{6,4},{7,5},{8,10},{9,11},{10,... | collective-permute-start | bytes 196616 | tf_op jit(solution)/shard_map/ppermute | solution.py:241
  20.2 1.1 %collective-permute-done.come_ref = f32[16,1024]{1,0:T(8,128)} collective-permute-done((f32[16,1024]{1,0:T(8,128)S(1)}, f32[16,1024]{1,0:T(8,128)}, u32[]{:S(2)}, u32[]{:S(2)}) %collective-permute-start) | collective-permute-done | bytes 65568 | tf_op jit(solution)/shard_map/ppermute | solution.py:241
  21.3 0.0 copy-start.8
  21.3 1.0 %carry.4 = (f32[16,1024]{1,0:T(8,128)S(1)}, f32[16,1024]{1,0:T(8,128)S(1)}) custom-call(s32[1]{0:T(128)} %bitcast.1.rank_ref, f32[16,2048]{1,0:T(8,128)S(1)} %copy-done, f32[16,1024]{1,0:T(8,128)} %collective-permute-done.come_ref, f32[16,1024]{1,0:T(8,128)S(1)} %get-tuple-element.20.refs_0_), custom_call_target="tpu_custom_call" | custom-call | tf_op jit(solution)/shard_map/carry/pallas_call | solution.py:244
  22.4 2.2 %collective-permute-start.1 = (f32[16,1024]{1,0:T(8,128)S(1)}, f32[16,1024]{1,0:T(8,128)S(1)}, u32[]{:S(2)}, u32[]{:S(2)}) collective-permute-start(f32[16,1024]{1,0:T(8,128)S(1)} %get-tuple-element.21), channel_id=1, source_target_pairs={{0,2},{1,3},{2,0},{3,1},{4,6},{5,7},{6,4},{7,5},{8,10},{9,11},{10,... | collective-permute-start | bytes 196616 | tf_op jit(solution)/shard_map/ppermute | solution.py:241
  24.6 0.0 copy-done.6
  24.6 0.0 copy-done.9
  24.6 0.0 copy-start.5
  24.6 0.8 %near_terms.3.refs_1_ = f32[64,8,1024]{2,1,0:T(8,128)S(1)} custom-call(f32[64,8,1024]{2,1,0:T(8,128)S(1)} %get-tuple-element.23.signal_ref, f32[16,2048]{1,0:T(8,128)S(1)} %copy-done.6, f32[16,2048]{1,0:T(8,128)S(1)} %copy-done, f32[1,2048]{1,0:T(1,128)S(1)} %bitcast.2), custom_call_target="tpu_custom_call" | custom-call | flops 4718592 | tf_op jit(solution)/shard_map/near_terms/pallas_call | solution.py:259
  25.4 0.0 copy-done.8
  25.4 0.0 copy-start.1
  25.4 0.8 %near_terms.2.near_ref = f32[64,8,1024]{2,1,0:T(8,128)S(1)} custom-call(f32[64,8,1024]{2,1,0:T(8,128)S(1)} %copy-done.8, f32[16,2048]{1,0:T(8,128)S(1)} %copy-done.6, f32[16,2048]{1,0:T(8,128)S(1)} %copy-done, f32[1,2048]{1,0:T(1,128)S(1)} %bitcast.3), custom_call_target="tpu_custom_call" | custom-call | flops 4718592 | tf_op jit(solution)/shard_map/near_terms/pallas_call | solution.py:259
  26.2 0.0 collective-permute-done.3.come_ref
  26.2 0.4 %copy-done.5 = f32[7,16,8,1024]{3,2,1,0:T(8,128)S(1)} copy-done((f32[7,16,8,1024]{3,2,1,0:T(8,128)S(1)}, f32[7,16,8,1024]{3,2,1,0:T(8,128)}, u32[]{:S(2)}) %copy-start.5) | copy-done | bytes 3670040
  26.6 0.9 %copy-done.1 = bf16[512,2048]{1,0:T(8,128)(2,1)S(1)} copy-done((bf16[512,2048]{1,0:T(8,128)(2,1)S(1)}, bf16[512,2048]{1,0:T(8,128)(2,1)}, u32[]{:S(2)}) %copy-start.1) | copy-done | bytes 2097176
  27.5 0.0 copy-start.3
  27.5 3.8 %spread_states.2.held_ref = bf16[512,2048]{1,0:T(8,128)(2,1)} custom-call(bf16[512,2048]{1,0:T(8,128)(2,1)S(1)} %copy-done.1, f32[64,8,1024]{2,1,0:T(8,128)S(1)} %near_terms.3.refs_1_, f32[7,16,8,1024]{3,2,1,0:T(8,128)S(1)} %copy-done.5, f32[8,16,1024]{2,1,0:T(8,128)S(1)} %get-tuple-element.25.refs_3_, f32[16,1024]{1,0:T(8,128)S(1)} %carry.7.refs_4_, ...), custom_call_target="tpu_custom_call" | custom-call | flops 16777216 | bytes 1048576 | tf_op jit(solution)/shard_map/spread_states/pallas_call | solution.py:278
  31.3 0.0 collective-permute-done.1.come_ref
  31.4 0.0 copy-done.3
  31.4 3.8 %spread_states.3 = bf16[512,2048]{1,0:T(8,128)(2,1)} custom-call(bf16[512,2048]{1,0:T(8,128)(2,1)S(1)} %copy-done.1, f32[64,8,1024]{2,1,0:T(8,128)S(1)} %near_terms.2.near_ref, f32[7,16,8,1024]{3,2,1,0:T(8,128)S(1)} %copy-done.3, f32[8,16,1024]{2,1,0:T(8,128)S(1)} %get-tuple-element.19.scan_ref, ...), custom_call_target="tpu_custom_call", output_to_operand_aliasing={{}: (7, {})} | custom-call | flops 16777216 | bytes 1048576 | tf_op jit(solution)/shard_map/spread_states/pallas_call | solution.py:278
  (2 shorter events, 0.1 us)
Async XLA Ops:
  4.1 1.9 %copy-start.4 = (f32[7,16,8,1024]{3,2,1,0:T(8,128)}, f32[7,16,8,1024]{3,2,1,0:T(8,128)S(1)}, u32[]{:S(2)}) copy-start(f32[7,16,8,1024]{3,2,1,0:T(8,128)S(1)} %get-tuple-element.24.refs_2_) | copy-start | bytes 11010052
  6.0 10.3 %copy-start = (f32[16,2048]{1,0:T(8,128)S(1)}, f32[16,2048]{1,0:T(8,128)}, u32[]{:S(2)}) copy-start(f32[16,2048]{1,0:T(8,128)} %decays_ref.17) | copy-start | bytes 393220
  6.0 18.6 %copy-start.6 = (f32[16,2048]{1,0:T(8,128)S(1)}, f32[16,2048]{1,0:T(8,128)}, u32[]{:S(2)}) copy-start(f32[16,2048]{1,0:T(8,128)} %residues_ref.5) | copy-start | bytes 393220
  6.0 18.6 %copy-start.9 = (f32[2048]{0:T(1024)S(1)}, f32[2048]{0:T(1024)}, u32[]{:S(2)}) copy-start(f32[2048]{0:T(1024)} %param.11) | copy-start | bytes 24580
  6.0 10.3 %collective-permute-start.2 = (f32[16,1024]{1,0:T(8,128)S(1)}, f32[16,1024]{1,0:T(8,128)}, u32[]{:S(2)}, u32[]{:S(2)}) collective-permute-start(f32[16,1024]{1,0:T(8,128)S(1)} %get-tuple-element.26.refs_0_), channel_id=1, source_target_pairs={{0,1},{1,0},{2,3},{3,2},{4,5},{5,4},{6,7},{7,6},{8,9},{9,8},{10,11... | collective-permute-start | bytes 196616 | tf_op jit(solution)/shard_map/ppermute | solution.py:241
  13.2 1.8 %copy-start.2 = (f32[7,16,8,1024]{3,2,1,0:T(8,128)}, f32[7,16,8,1024]{3,2,1,0:T(8,128)S(1)}, u32[]{:S(2)}) copy-start(f32[7,16,8,1024]{3,2,1,0:T(8,128)S(1)} %get-tuple-element.18.sums_ref) | copy-start | bytes 11010052
  14.9 1.3 %copy-start.7 = (f32[64,8,1024]{2,1,0:T(8,128)}, f32[64,8,1024]{2,1,0:T(8,128)S(1)}, u32[]{:S(2)}) copy-start(f32[64,8,1024]{2,1,0:T(8,128)S(1)} %get-tuple-element.17.signal_ref) | copy-start | bytes 6291460
  16.3 5.1 %collective-permute-start = (f32[16,1024]{1,0:T(8,128)S(1)}, f32[16,1024]{1,0:T(8,128)}, u32[]{:S(2)}, u32[]{:S(2)}) collective-permute-start(f32[16,1024]{1,0:T(8,128)S(1)} %get-tuple-element.20.refs_0_), channel_id=1, source_target_pairs={{0,1},{1,0},{2,3},{3,2},{4,5},{5,4},{6,7},{7,6},{8,9},{9,8},{10,11... | collective-permute-start | bytes 196616 | tf_op jit(solution)/shard_map/ppermute | solution.py:241
  17.2 9.0 %collective-permute-start.3 = (f32[16,1024]{1,0:T(8,128)S(1)}, f32[16,1024]{1,0:T(8,128)S(1)}, u32[]{:S(2)}, u32[]{:S(2)}) collective-permute-start(f32[16,1024]{1,0:T(8,128)S(1)} %get-tuple-element.27), channel_id=1, source_target_pairs={{0,2},{1,3},{2,0},{3,1},{4,6},{5,7},{6,4},{7,5},{8,10},{9,11},{10,... | collective-permute-start | bytes 196616 | tf_op jit(solution)/shard_map/ppermute | solution.py:241
  21.3 4.0 %copy-start.8 = (f32[64,8,1024]{2,1,0:T(8,128)S(1)}, f32[64,8,1024]{2,1,0:T(8,128)}, u32[]{:S(2)}) copy-start(f32[64,8,1024]{2,1,0:T(8,128)} %copy-done.7) | copy-start | bytes 6291460
  22.4 9.0 %collective-permute-start.1 = (f32[16,1024]{1,0:T(8,128)S(1)}, f32[16,1024]{1,0:T(8,128)S(1)}, u32[]{:S(2)}, u32[]{:S(2)}) collective-permute-start(f32[16,1024]{1,0:T(8,128)S(1)} %get-tuple-element.21), channel_id=1, source_target_pairs={{0,2},{1,3},{2,0},{3,1},{4,6},{5,7},{6,4},{7,5},{8,10},{9,11},{10,... | collective-permute-start | bytes 196616 | tf_op jit(solution)/shard_map/ppermute | solution.py:241
  24.6 2.0 %copy-start.5 = (f32[7,16,8,1024]{3,2,1,0:T(8,128)S(1)}, f32[7,16,8,1024]{3,2,1,0:T(8,128)}, u32[]{:S(2)}) copy-start(f32[7,16,8,1024]{3,2,1,0:T(8,128)} %copy-done.4) | copy-start | bytes 11010052
  25.4 2.1 %copy-start.1 = (bf16[512,2048]{1,0:T(8,128)(2,1)S(1)}, bf16[512,2048]{1,0:T(8,128)(2,1)}, u32[]{:S(2)}) copy-start(bf16[512,2048]{1,0:T(8,128)(2,1)} %query_ref.1) | copy-start | bytes 6291460
  27.5 3.9 %copy-start.3 = (f32[7,16,8,1024]{3,2,1,0:T(8,128)S(1)}, f32[7,16,8,1024]{3,2,1,0:T(8,128)}, u32[]{:S(2)}) copy-start(f32[7,16,8,1024]{3,2,1,0:T(8,128)} %copy-done.2) | copy-start | bytes 11010052

commit v3 on v2

--- a/solution.py
+++ b/solution.py
@@ -94,10 +94,10 @@
         end_ref[:, lanes] = state
 
 
-def carry(first, positions, reach, opening, final, rank_ref, decays_ref, come_ref, *refs):
+def carry(first, positions, reach, opening, final, decays_ref, come_ref, *refs):
     decay = decays_ref[:, pl.ds(first, come_ref.shape[1])]
     come = come_ref[...]
-    rank = rank_ref[0]
+    rank = lax.axis_index("ctx")
     upper = rank & reach != 0
     behind = ((rank & (reach - 1)) * (positions // reach)).astype(jnp.float32)
     refs = list(refs)
@@ -194,7 +194,6 @@
     seg_len = rows // SEG
     chunks = seg_len // CHUNK
     ctx_size = lax.axis_size("ctx")
-    ctx_rank = lax.axis_index("ctx")
     skip_gain = skip_gain[None, :]
     group = width // GROUPS
     blocks = group // LANES
@@ -231,7 +230,6 @@
                 name="gather_states",
             )(*(pltpu.with_memory_space_constraint(array, pltpu.HBM) for array in (key_gate, value_input, decays)))
         )
-    rank = ctx_rank.astype(jnp.int32).reshape(1)
     enters = []
     for part in range(GROUPS):
         total = gathered[part][3]
@@ -240,10 +238,10 @@
         while reach < ctx_size:
             come = lax.ppermute(total, "ctx", [(i, i ^ reach) for i in range(ctx_size)])
             final = 2 * reach == ctx_size
-            operands = [rank, decays, come] + ([] if final else [total]) + ([] if enter is None else [enter])
+            operands = [decays, come] + ([] if final else [total]) + ([] if enter is None else [enter])
             result = pl.pallas_call(
                 functools.partial(carry, part * group, reach * rows, reach, reach == 1, final),
-                in_specs=[pl.BlockSpec(memory_space=pltpu.SMEM)] + [VMEM] * (len(operands) - 1),
+                in_specs=[VMEM] * len(operands),
                 out_specs=[VMEM] * (1 if final else 2),
                 out_shape=[real((modes, group))] * (1 if final else 2),
                 compiler_params=pltpu.CompilerParams(vmem_limit_bytes=4 * MIB),

time: 35.4 us -> 28.6 us (0.81)
  local copies, waits for them, and re-layouts: 6.27 us -> 0.79 us
  Pallas kernels: 19.3 us -> 17.5 us
  waiting for transfers between devices: 1.1 us -> 1.54 us
    unnamed x20 -> x8, local copies, waits for them, and re-layouts: 6.27 us -> 0.79 us
    pallas_call x4, Pallas kernels: 1.95 us -> 0.12 us  [shards(): pl.pallas_call(functools.partial(carry, part * group, reach * rows, reach...]
    ppermute x4, waiting for transfers between devices: 1.1 us -> 1.54 us  [shards(): come = lax.ppermute(total, 'ctx', [(i, i ^ reach) for i in range(ctx_size)])]
  transfers between devices with their start and end apart: 4 -> 4, of which waited for: 1 -> 1; matrix products, arithmetic and copies ran while one was open for 0% -> 0% of each run, Pallas kernels for 32% -> 34%
where the time goes in v3:
time: 28.6 us; the launch traced here: 28.4 us
  Pallas kernels  17.5 us (61%)
  starting transfers between devices  8.5 us (30%)
  waiting for transfers between devices  1.54 us (5%)
  local copies, waits for them, and re-layouts  0.79 us (3%)
    ppermute x4, starting transfers between devices, shards(): come = lax.ppermute(total, 'ctx', [(i, i ^ reach) for i in range(ctx_size)])  8.5 us
    pallas_call x2, Pallas kernels, shards(): pl.pallas_call(functools.partial(gather_states, part * group), in_specs=[...  8.25 us
    pallas_call x2, Pallas kernels, shards(): pl.pallas_call(body, in_specs=specs, out_specs=HBM, out_shape=jax.ShapeDt...  7.6 us
    ppermute x4, waiting for transfers between devices, shards(): come = lax.ppermute(total, 'ctx', [(i, i ^ reach) for i in range(ctx_size)])  1.54 us
    pallas_call x2, Pallas kernels, shards(): pl.pallas_call(functools.partial(near_terms, part * group), in_specs=[VME...  1.52 us
    unnamed x8, local copies, waits for them, and re-layouts  0.79 us
  transfers between devices with their start and end apart: 4, of which 1 were waited for; matrix products, arithmetic and copies ran while one was open for 0% of the time, Pallas kernels for 34%

profile of v3, /device:TPU:0, one launch (start us, length us, event | category | flops | bytes accessed | tf_op | source)
XLA Modules:
  0.0 28.4 jit_solution(4976120912664000872)
XLA Ops:
  0.0 4.1 %gather_states.3 = (f32[64,8,1024]{2,1,0:T(8,128)S(1)}, f32[7,16,8,1024]{3,2,1,0:T(8,128)S(1)}, f32[8,16,1024]{2,1,0:T(8,128)S(1)}, f32[16,1024]{1,0:T(8,128)S(1)}) custom-call(bf16[512,2048]{1,0:T(8,128)(2,1)} %key_ref.3, bf16[512,2048]{1,0:T(8,128)(2,1)} %value_ref.3, f32[16,2048]{1,0:T(8,128)} %decays_ref.17), custom_call_target="tpu_custom_call" | custom-call | flops 16777216 | bytes 2097152 | tf_op jit(solution)/shard_map/gather_states/pallas_call | solution.py:208
  4.1 0.0 copy-start
  4.1 0.0 copy-start.2
  4.2 0.0 copy-start.3
  4.2 3.1 %collective-permute-start.2 = (f32[16,1024]{1,0:T(8,128)S(1)}, f32[16,1024]{1,0:T(8,128)S(1)}, u32[]{:S(2)}, u32[]{:S(2)}) collective-permute-start(f32[16,1024]{1,0:T(8,128)S(1)} %get-tuple-element.26.refs_0_), channel_id=1, source_target_pairs={{0,1},{1,0},{2,3},{3,2},{4,5},{5,4},{6,7},{7,6},{8,9},{9,8},{10,11... | collective-permute-start | bytes 196616 | tf_op jit(solution)/shard_map/ppermute | solution.py:239
  7.3 4.1 %gather_states.2 = (f32[64,8,1024]{2,1,0:T(8,128)S(1)}, f32[7,16,8,1024]{3,2,1,0:T(8,128)S(1)}, f32[8,16,1024]{2,1,0:T(8,128)S(1)}, f32[16,1024]{1,0:T(8,128)S(1)}) custom-call(bf16[512,2048]{1,0:T(8,128)(2,1)} %key_ref.3, bf16[512,2048]{1,0:T(8,128)(2,1)} %value_ref.3, f32[16,2048]{1,0:T(8,128)} %decays_ref.17), custom_call_target="tpu_custom_call" | custom-call | flops 16777216 | bytes 2097152 | tf_op jit(solution)/shard_map/gather_states/pallas_call | solution.py:208
  11.4 0.1 collective-permute-start
  11.5 0.0 collective-permute-done.2.come_ref
  11.5 0.0 copy-done
  11.6 3.1 %collective-permute-start.3 = (f32[16,1024]{1,0:T(8,128)S(1)}, f32[16,1024]{1,0:T(8,128)S(1)}, u32[]{:S(2)}, u32[]{:S(2)}) collective-permute-start(f32[16,1024]{1,0:T(8,128)S(1)} %get-tuple-element.27), channel_id=1, source_target_pairs={{0,2},{1,3},{2,0},{3,1},{4,6},{5,7},{6,4},{7,5},{8,10},{9,11},{10,... | collective-permute-start | bytes 196616 | tf_op jit(solution)/shard_map/ppermute | solution.py:239
  14.6 1.5 %collective-permute-done.come_ref = f32[16,1024]{1,0:T(8,128)S(1)} collective-permute-done((f32[16,1024]{1,0:T(8,128)S(1)}, f32[16,1024]{1,0:T(8,128)S(1)}, u32[]{:S(2)}, u32[]{:S(2)}) %collective-permute-start) | collective-permute-done | bytes 65568 | tf_op jit(solution)/shard_map/ppermute | solution.py:239
  16.2 2.2 %collective-permute-start.1 = (f32[16,1024]{1,0:T(8,128)S(1)}, f32[16,1024]{1,0:T(8,128)S(1)}, u32[]{:S(2)}, u32[]{:S(2)}) collective-permute-start(f32[16,1024]{1,0:T(8,128)S(1)} %get-tuple-element.21), channel_id=1, source_target_pairs={{0,2},{1,3},{2,0},{3,1},{4,6},{5,7},{6,4},{7,5},{8,10},{9,11},{10,... | collective-permute-start | bytes 196616 | tf_op jit(solution)/shard_map/ppermute | solution.py:239
  18.4 0.0 copy-done.2
  18.4 0.0 copy-done.3
  18.4 0.8 %near_terms.3.refs_1_ = f32[64,8,1024]{2,1,0:T(8,128)S(1)} custom-call(f32[64,8,1024]{2,1,0:T(8,128)S(1)} %get-tuple-element.23.signal_ref, f32[16,2048]{1,0:T(8,128)S(1)} %copy-done.2, f32[16,2048]{1,0:T(8,128)S(1)} %copy-done, f32[1,2048]{1,0:T(1,128)S(1)} %bitcast.1), custom_call_target="tpu_custom_call" | custom-call | flops 4718592 | tf_op jit(solution)/shard_map/near_terms/pallas_call | solution.py:257
  19.2 0.0 copy-start.1
  19.2 0.8 %near_terms.2.near_ref = f32[64,8,1024]{2,1,0:T(8,128)S(1)} custom-call(f32[64,8,1024]{2,1,0:T(8,128)S(1)} %get-tuple-element.17.signal_ref, f32[16,2048]{1,0:T(8,128)S(1)} %copy-done.2, f32[16,2048]{1,0:T(8,128)S(1)} %copy-done, f32[1,2048]{1,0:T(1,128)S(1)} %bitcast.2), custom_call_target="tpu_custom_call" | custom-call | flops 4718592 | tf_op jit(solution)/shard_map/near_terms/pallas_call | solution.py:257
  20.0 0.0 collective-permute-done.3.come_ref
  20.0 0.8 %copy-done.1 = bf16[512,2048]{1,0:T(8,128)(2,1)S(1)} copy-done((bf16[512,2048]{1,0:T(8,128)(2,1)S(1)}, bf16[512,2048]{1,0:T(8,128)(2,1)}, u32[]{:S(2)}) %copy-start.1) | copy-done | bytes 2097176
  20.8 3.8 %spread_states.2.held_ref = bf16[512,2048]{1,0:T(8,128)(2,1)} custom-call(bf16[512,2048]{1,0:T(8,128)(2,1)S(1)} %copy-done.1, f32[64,8,1024]{2,1,0:T(8,128)S(1)} %near_terms.3.refs_1_, f32[7,16,8,1024]{3,2,1,0:T(8,128)S(1)} %get-tuple-element.24.refs_2_, f32[8,16,1024]{2,1,0:T(8,128)S(1)} %get-tuple-element.25.refs_3_, f32[16,1024]{1,0:T(8,128)S(1)} %carry.7.refs_4_, ...), custom_call_target="tpu_custom_call" | custom-call | flops 16777216 | bytes 1048576 | tf_op jit(solution)/shard_map/spread_states/pallas_call | solution.py:276
  24.6 0.0 collective-permute-done.1.come_ref
  24.6 3.8 %spread_states.3 = bf16[512,2048]{1,0:T(8,128)(2,1)} custom-call(bf16[512,2048]{1,0:T(8,128)(2,1)S(1)} %copy-done.1, f32[64,8,1024]{2,1,0:T(8,128)S(1)} %near_terms.2.near_ref, f32[7,16,8,1024]{3,2,1,0:T(8,128)S(1)} %get-tuple-element.18.sums_ref, f32[8,16,1024]{2,1,0:T(8,128)S(1)} %get-tuple-element.19.scan_ref, ...), custom_call_target="tpu_custom_call", output_to_operand_aliasing={{}: (7, {})} | custom-call | flops 16777216 | bytes 1048576 | tf_op jit(solution)/shard_map/spread_states/pallas_call | solution.py:276
  (4 shorter events, 0.1 us)
Async XLA Ops:
  4.1 7.4 %copy-start = (f32[16,2048]{1,0:T(8,128)S(1)}, f32[16,2048]{1,0:T(8,128)}, u32[]{:S(2)}) copy-start(f32[16,2048]{1,0:T(8,128)} %decays_ref.17) | copy-start | bytes 393220
  4.1 14.3 %copy-start.2 = (f32[16,2048]{1,0:T(8,128)S(1)}, f32[16,2048]{1,0:T(8,128)}, u32[]{:S(2)}) copy-start(f32[16,2048]{1,0:T(8,128)} %residues_ref.5) | copy-start | bytes 393220
  4.2 14.3 %copy-start.3 = (f32[2048]{0:T(1024)S(1)}, f32[2048]{0:T(1024)}, u32[]{:S(2)}) copy-start(f32[2048]{0:T(1024)} %param.11) | copy-start | bytes 24580
  4.2 7.3 %collective-permute-start.2 = (f32[16,1024]{1,0:T(8,128)S(1)}, f32[16,1024]{1,0:T(8,128)S(1)}, u32[]{:S(2)}, u32[]{:S(2)}) collective-permute-start(f32[16,1024]{1,0:T(8,128)S(1)} %get-tuple-element.26.refs_0_), channel_id=1, source_target_pairs={{0,1},{1,0},{2,3},{3,2},{4,5},{5,4},{6,7},{7,6},{8,9},{9,8},{10,11... | collective-permute-start | bytes 196616 | tf_op jit(solution)/shard_map/ppermute | solution.py:239
  11.4 4.7 %collective-permute-start = (f32[16,1024]{1,0:T(8,128)S(1)}, f32[16,1024]{1,0:T(8,128)S(1)}, u32[]{:S(2)}, u32[]{:S(2)}) collective-permute-start(f32[16,1024]{1,0:T(8,128)S(1)} %get-tuple-element.20.refs_0_), channel_id=1, source_target_pairs={{0,1},{1,0},{2,3},{3,2},{4,5},{5,4},{6,7},{7,6},{8,9},{9,8},{10,11... | collective-permute-start | bytes 196616 | tf_op jit(solution)/shard_map/ppermute | solution.py:239
  11.6 8.4 %collective-permute-start.3 = (f32[16,1024]{1,0:T(8,128)S(1)}, f32[16,1024]{1,0:T(8,128)S(1)}, u32[]{:S(2)}, u32[]{:S(2)}) collective-permute-start(f32[16,1024]{1,0:T(8,128)S(1)} %get-tuple-element.27), channel_id=1, source_target_pairs={{0,2},{1,3},{2,0},{3,1},{4,6},{5,7},{6,4},{7,5},{8,10},{9,11},{10,... | collective-permute-start | bytes 196616 | tf_op jit(solution)/shard_map/ppermute | solution.py:239
  16.2 8.4 %collective-permute-start.1 = (f32[16,1024]{1,0:T(8,128)S(1)}, f32[16,1024]{1,0:T(8,128)S(1)}, u32[]{:S(2)}, u32[]{:S(2)}) collective-permute-start(f32[16,1024]{1,0:T(8,128)S(1)} %get-tuple-element.21), channel_id=1, source_target_pairs={{0,2},{1,3},{2,0},{3,1},{4,6},{5,7},{6,4},{7,5},{8,10},{9,11},{10,... | collective-permute-start | bytes 196616 | tf_op jit(solution)/shard_map/ppermute | solution.py:239
  19.2 1.6 %copy-start.1 = (bf16[512,2048]{1,0:T(8,128)(2,1)S(1)}, bf16[512,2048]{1,0:T(8,128)(2,1)}, u32[]{:S(2)}) copy-start(bf16[512,2048]{1,0:T(8,128)(2,1)} %query_ref.1) | copy-start | bytes 6291460

commit v4 on v3

v4 whole, which is shorter than its diff:
```python
import functools

import jax
import jax.numpy as jnp
from jax import lax
from jax.experimental import pallas as pl
from jax.experimental.pallas import tpu as pltpu
from jax.sharding import PartitionSpec as P

SEG = 8
CHUNK = 8
LANES = 128
LEAD = 9
SLABS = (0, 1, 4)
MIB = 2**20

VMEM = pl.BlockSpec(memory_space=pltpu.VMEM)
HBM = pl.BlockSpec(memory_space=pltpu.HBM)


def row(ref, index, lanes=slice(None)):
    return jnp.broadcast_to(ref[pl.ds(index, 1), lanes], (SEG, LANES))


def lane_block(block):
    return pl.ds(pl.multiple_of(block * LANES, LANES), LANES)


def gather_states(first, key_ref, value_ref, decays_ref, signal_ref, sums_ref, scan_ref, end_ref, natural, turned, damp, damp_chunk, arrive=None):
    rows, width = key_ref.shape
    modes = decays_ref.shape[0]
    seg_len = rows // SEG
    chunks = seg_len // CHUNK
    pitch = seg_len + 1

    @pl.loop(0, width // LANES)
    def _(block):
        if arrive is not None:
            arrive(block)
        lanes = lane_block(block)
        decay = decays_ref[:, pl.ds(pl.multiple_of(first + block * LANES, LANES), LANES)]
        damp[...] = jnp.exp(-decay)
        damp_chunk[...] = jnp.exp(-CHUNK * decay)
        damp_segment = jnp.exp(-seg_len * decay)
        for start in range(0, rows, 16):
            part = pl.ds(start, 16)
            place = start // seg_len * pitch + start % seg_len
            natural[pl.ds(place, 16), :] = key_ref[part, lanes].astype(jnp.float32) * value_ref[part, lanes].astype(jnp.float32)
        states = [None] * modes
        for chunk in range(chunks):
            signal = [natural[pl.ds(chunk * CHUNK + step, SEG, stride=pitch), :] for step in range(CHUNK)]
            for step in range(CHUNK):
                signal_ref[chunk * CHUNK + step, :, lanes] = signal[step]
            for mode in range(modes):
                factor = row(damp, mode)
                total = signal[0]
                for step in range(1, CHUNK):
                    total = total * factor + signal[step]
                if chunk < chunks - 1:
                    sums_ref[chunk, mode, :, lanes] = total
                states[mode] = total if chunk == 0 else states[mode] * row(damp_chunk, mode) + total
        for mode in range(modes):
            turned[pl.ds(mode * (SEG + 1), SEG), :] = states[mode]
        state = jnp.zeros((modes, LANES), jnp.float32)
        for segment in range(SEG):
            scan_ref[segment, :, lanes] = state
            state = state * damp_segment + turned[pl.ds(segment, modes, stride=SEG + 1), :]
        end_ref[:, lanes] = state


def load_and_gather(
    key_ref, value_ref, query_ref, decays_ref, signal_ref, sums_ref, scan_ref, end_ref, later_key_ref, later_value_ref, later_query_ref, natural, turned, damp, damp_chunk, keys, values, rates, sems
):
    width = keys.shape[1]
    blocks = width // LANES
    rate_copy = pltpu.make_async_copy(decays_ref.at[:, pl.ds(0, width)], rates, sems.at[2, 0])
    starts = [start for start in SLABS if start < blocks]
    slabs = []
    for index, (start, stop) in enumerate(zip(starts, starts[1:] + [blocks])):
        lanes = pl.ds(start * LANES, (stop - start) * LANES)
        slabs.append(
            (
                pltpu.make_async_copy(key_ref.at[:, lanes], keys.at[:, lanes], sems.at[0, index]),
                pltpu.make_async_copy(value_ref.at[:, lanes], values.at[:, lanes], sems.at[1, index]),
            )
        )
        for copy in slabs[-1]:
            copy.start()
        if index == 0:
            rate_copy.start()
    later = pl.ds(width, key_ref.shape[1] - width)
    later_copies = (
        pltpu.make_async_copy(key_ref.at[:, later], later_key_ref, sems.at[2, 1]),
        pltpu.make_async_copy(value_ref.at[:, later], later_value_ref, sems.at[2, 2]),
        pltpu.make_async_copy(query_ref, later_query_ref, sems.at[2, 3]),
    )
    for copy in later_copies:
        copy.start()
    rate_copy.wait()

    def arrive(block):
        for start, copies in zip(starts, slabs):

            @pl.when(block == start)
            def _(copies=copies):
                for copy in copies:
                    copy.wait()

    gather_states(0, keys, values, rates, signal_ref, sums_ref, scan_ref, end_ref, natural, turned, damp, damp_chunk, arrive)
    for copy in later_copies:
        copy.wait()


def carry(first, positions, reach, opening, final, after, decays_ref, come_ref, *refs):
    decay = decays_ref[:, pl.ds(first, come_ref.shape[1])]
    come = come_ref[...]
    rank = lax.axis_index("ctx")
    upper = rank & reach != 0
    behind = ((rank & (reach - 1)) * (positions // reach)).astype(jnp.float32)
    refs = list(refs[after:])
    total = None if final else refs.pop(0)[...]
    enter = 0.0 if opening else refs.pop(0)[...]
    refs[0][...] = enter + jnp.where(upper, jnp.exp(-behind * decay) * come, 0.0)
    if not final:
        over = jnp.exp(-positions * decay)
        refs[1][...] = jnp.where(upper, total + over * come, come + over * total)


def near_terms(first, signal_ref, sums_ref, residues_ref, decays_ref, skip_ref, near_ref, scaled_ref):
    steps, _, width = signal_ref.shape
    modes = decays_ref.shape[0]
    chunks = steps // CHUNK

    @pl.loop(0, width // LANES)
    def _(block):
        lanes = lane_block(block)
        wide = pl.ds(pl.multiple_of(first + block * LANES, LANES), LANES)
        decay = decays_ref[:, wide]
        term = residues_ref[:, wide] * jnp.sqrt(decay)
        damp = jnp.exp(-decay)
        weight = term * damp
        taps = []
        for step in range(CHUNK):
            tap = jnp.sum(term, 0, keepdims=True)
            if step == 0:
                tap = tap + skip_ref[:, wide]
            taps.append(jnp.broadcast_to(tap, (SEG, LANES)))
            term = term * damp
        for chunk in range(chunks):
            signal = [signal_ref[chunk * CHUNK + step, :, lanes] for step in range(CHUNK)]
            for step in range(CHUNK):
                total = taps[0] * signal[step]
                for back in range(1, step + 1):
                    total = total + taps[back] * signal[step - back]
                near_ref[chunk * CHUNK + step, :, lanes] = total
        for mode in range(modes):
            factor = jnp.broadcast_to(weight[mode : mode + 1, :], (SEG, LANES))
            scaled = [factor * sums_ref[chunk, mode, :, lanes] for chunk in range(chunks - 1)]
            for chunk in range(chunks - 1):
                scaled_ref[chunk, mode, :, lanes] = scaled[chunk]


def spread_states(first, query_ref, near_ref, sums_ref, scan_ref, enter_ref, residues_ref, decays_ref, gated_ref, natural, turned, damp, leave=None):
    rows, width = gated_ref.shape
    modes = decays_ref.shape[0]
    seg_len = rows // SEG
    chunks = seg_len // CHUNK
    pitch = seg_len + 1

    @pl.loop(0, width // LANES)
    def _(block):
        lanes = lane_block(block)
        wide = pl.ds(pl.multiple_of(first + block * LANES, LANES), LANES)
        decay = decays_ref[:, wide]
        once = jnp.exp(-decay)
        damp[...] = once
        scale = residues_ref[:, wide] * jnp.sqrt(decay) * once
        damp_segment = jnp.exp(-seg_len * decay)
        enter = enter_ref[:, lanes]
        for segment in range(SEG):
            turned[pl.ds(segment * (modes + 1), modes), :] = (scan_ref[segment, :, lanes] + enter) * scale
            enter = enter * damp_segment
        states = [turned[pl.ds(mode, SEG, stride=modes + 1), :] for mode in range(modes)]
        for chunk in range(chunks):
            conv = [near_ref[chunk * CHUNK + step, :, lanes] for step in range(CHUNK)]
            for mode in range(modes):
                factor = row(damp, mode)
                state = states[mode]
                for step in range(CHUNK):
                    conv[step] = conv[step] + state
                    if step < CHUNK - 1 or chunk < chunks - 1:
                        state = state * factor
                if chunk < chunks - 1:
                    states[mode] = state + sums_ref[chunk, mode, :, lanes]
            for step in range(CHUNK):
                natural[pl.ds(chunk * CHUNK + step, SEG, stride=pitch), :] = conv[step]
        for start in range(0, rows, 16):
            part = pl.ds(start, 16)
            place = start // seg_len * pitch + start % seg_len
            gated_ref[part, lanes] = (query_ref[part, wide].astype(jnp.float32) * natural[pl.ds(place, 16), :]).astype(jnp.bfloat16)
        if leave is not None:
            leave(block)


def spread_and_store(
    first, query_ref, near_ref, sums_ref, scan_ref, enter_ref, residues_ref, decays_ref, held_ref, mixed_ref, natural, turned, damp, gated, sems
):
    blocks = gated.shape[1] // LANES
    held_copy = pltpu.make_async_copy(held_ref, mixed_ref.at[:, pl.ds(0, first)], sems.at[blocks])
    held_copy.start()

    def copy(block):
        wide = pl.ds(pl.multiple_of(first + block * LANES, LANES), LANES)
        return pltpu.make_async_copy(gated.at[:, lane_block(block)], mixed_ref.at[:, wide], sems.at[block])

    spread_states(
        first, query_ref, near_ref, sums_ref, scan_ref, enter_ref, residues_ref, decays_ref, gated, natural, turned, damp, lambda block: copy(block).start()
    )

    @pl.loop(0, blocks)
    def _(block):
        copy(block).wait()

    held_copy.wait()


def shards(query_gate, key_gate, value_input, residues, decays, skip_gain):
    rows, width = key_gate.shape
    modes = residues.shape[0]
    seg_len = rows // SEG
    chunks = seg_len // CHUNK
    ctx_size = lax.axis_size("ctx")
    skip_gain = skip_gain[None, :]
    lead = width * LEAD // 16
    groups = [(0, lead), (lead, width - lead)]
    real = functools.partial(pltpu.VMEM, dtype=jnp.float32)
    half = functools.partial(pltpu.VMEM, dtype=jnp.bfloat16)
    natural = real((SEG * (seg_len + 1), LANES))
    table = real((modes, LANES))

    def cost(ops, moved, count):
        return pl.CostEstimate(flops=ops * rows * count, bytes_accessed=moved * rows * count, transcendentals=0)

    gathered = []
    for first, count in groups:
        shapes = [
            real((seg_len, SEG, count)),
            real((chunks - 1, modes, SEG, count)),
            real((SEG, modes, count)),
            real((modes, count)),
        ]
        scratch = [natural, real((modes * (SEG + 1), LANES)), table, table]
        if first == 0:
            later = half((rows, width - count))
            *states, later_keys, later_values, queries = pl.pallas_call(
                load_and_gather,
                in_specs=[HBM] * 4,
                out_specs=[VMEM] * 7,
                out_shape=shapes + [later, later, half((rows, width))],
                scratch_shapes=scratch
                + [half((rows, count)), half((rows, count)), real((modes, count)), pltpu.SemaphoreType.DMA((3, 4))],
                compiler_params=pltpu.CompilerParams(vmem_limit_bytes=12 * MIB),
                cost_estimate=cost(2 * modes, 19, count),
                name="load_and_gather",
            )(*(pltpu.with_memory_space_constraint(array, pltpu.HBM) for array in (key_gate, value_input, query_gate, decays)))
        else:
            states = pl.pallas_call(
                functools.partial(gather_states, first),
                in_specs=[VMEM] * 3,
                out_specs=[VMEM] * 4,
                out_shape=shapes,
                scratch_shapes=scratch,
                compiler_params=pltpu.CompilerParams(vmem_limit_bytes=4 * MIB),
                cost_estimate=cost(2 * modes, 19, count),
                name="gather_states",
            )(later_keys, later_values, decays)
        gathered.append(states)

    nears = []
    for (first, count), (signal, sums, _, _) in zip(groups, gathered):
        nears.append(
            pl.pallas_call(
                functools.partial(near_terms, first),
                in_specs=[VMEM] * 5,
                out_specs=[VMEM] * 2,
                out_shape=[real(signal.shape), real(sums.shape)],
                compiler_params=pltpu.CompilerParams(vmem_limit_bytes=4 * MIB),
                cost_estimate=cost(10, 7, count),
                name="near_terms",
            )(signal, sums, residues, decays, skip_gain)
        )

    held = None
    for part, (first, count) in enumerate(groups):
        total = gathered[part][3]
        enter = None
        reach = 1
        while reach < ctx_size:
            come = lax.ppermute(total, "ctx", [(i, i ^ reach) for i in range(ctx_size)])
            final = 2 * reach == ctx_size
            after = []
            if part and reach == 1:
                after = [near for near, _ in nears]
            elif part and final:
                after = [held]
            operands = [decays, come] + after + ([] if final else [total]) + ([] if enter is None else [enter])
            result = pl.pallas_call(
                functools.partial(carry, first, reach * rows, reach, reach == 1, final, len(after)),
                in_specs=[VMEM] * len(operands),
                out_specs=[VMEM] * (1 if final else 2),
                out_shape=[real((modes, count))] * (1 if final else 2),
                compiler_params=pltpu.CompilerParams(vmem_limit_bytes=4 * MIB),
                name="carry",
            )(*operands)
            enter = result[0]
            total = result[-1]
            reach *= 2
        operands = [queries, *nears[part], gathered[part][2], enter, residues, decays]
        scratch = [natural, real((SEG * (modes + 1), LANES)), table]
        if part == 0:
            held = pl.pallas_call(
                functools.partial(spread_states, first),
                in_specs=[VMEM] * len(operands),
                out_specs=VMEM,
                out_shape=half((rows, count)),
                scratch_shapes=scratch,
                compiler_params=pltpu.CompilerParams(vmem_limit_bytes=4 * MIB),
                cost_estimate=cost(2 * modes, 21, count),
                name="spread_states",
            )(*operands)
        else:
            mixed = pl.pallas_call(
                functools.partial(spread_and_store, first),
                in_specs=[VMEM] * (len(operands) + 1),
                out_specs=HBM,
                out_shape=jax.ShapeDtypeStruct((rows, width), jnp.bfloat16),
                scratch_shapes=scratch + [half((rows, count)), pltpu.SemaphoreType.DMA((count // LANES + 1,))],
                compiler_params=pltpu.CompilerParams(vmem_limit_bytes=6 * MIB),
                cost_estimate=cost(2 * modes, 21, count),
                name="spread_and_store",
            )(*operands, held)
    return mixed


def solution(mesh):
    placed = (
        P("ctx", "chan"),
        P("ctx", "chan"),
        P("ctx", "chan"),
        P(None, "chan"),
        P(None, "chan"),
        P("chan"),
    )
    return jax.shard_map(shards, mesh=mesh, in_specs=placed, out_specs=P("ctx", "chan"), check_vma=False)
```

time: 28.6 us -> 23.4 us (0.82)
  Pallas kernels: 17.5 us -> 15 us
  waiting for transfers between devices: 1.54 us -> 0.23 us
  local copies, waits for them, and re-layouts: 0.79 us -> 0.02 us
  starting transfers between devices: 8.5 us -> 7.94 us
    pallas_call x10, Pallas kernels: 17.5 us -> 15 us  [the longest x1 4.14 us: shards(): pl.pallas_call(load_and_gather, in_specs=[HBM] * 4, out_specs=[VMEM] * 7,...]
    ppermute x4, waiting for transfers between devices: 1.54 us -> 0.23 us  [shards(): come = lax.ppermute(total, 'ctx', [(i, i ^ reach) for i in range(ctx_size)])]
    unnamed x8 -> x6, local copies, waits for them, and re-layouts: 0.79 us -> 0.02 us
    ppermute x4, starting transfers between devices: 8.5 us -> 7.94 us  [shards(): come = lax.ppermute(total, 'ctx', [(i, i ^ reach) for i in range(ctx_size)])]
  transfers between devices with their start and end apart: 4 -> 4, of which waited for: 1 -> 1; matrix products, arithmetic and copies ran while one was open for 0% -> 0% of each run, Pallas kernels for 34% -> 33%
where the time goes in v4:
time: 23.4 us; the launch traced here: 23.2 us
  Pallas kernels  15 us (64%)
  starting transfers between devices  7.94 us (34%)
    ppermute x4, starting transfers between devices, shards(): come = lax.ppermute(total, 'ctx', [(i, i ^ reach) for i in range(ctx_size)])  7.94 us
    pallas_call x1, Pallas kernels, shards(): pl.pallas_call(load_and_gather, in_specs=[HBM] * 4, out_specs=[VMEM] * 7,...  4.14 us
    pallas_call x1, Pallas kernels, shards(): pl.pallas_call(functools.partial(spread_and_store, first), in_specs=[VMEM...  3.24 us
    pallas_call x1, Pallas kernels, shards(): pl.pallas_call(functools.partial(spread_states, first), in_specs=[VMEM] *...  3.2 us
    pallas_call x1, Pallas kernels, shards(): pl.pallas_call(functools.partial(gather_states, first), in_specs=[VMEM] *...  2.31 us
    pallas_call x2, Pallas kernels, shards(): pl.pallas_call(functools.partial(near_terms, first), in_specs=[VMEM] * 5,...  1.96 us
  transfers between devices with their start and end apart: 4, of which 1 were waited for; matrix products, arithmetic and copies ran while one was open for 0% of the time, Pallas kernels for 33%

profile of v4, /device:TPU:0, one launch (start us, length us, event | category | flops | bytes accessed | tf_op | source)
XLA Modules:
  0.0 23.2 jit_solution(10357489059009751743)
XLA Ops:
  0.0 0.0 copy-start
  0.0 4.1 %load_and_gather.1 = (f32[64,8,1152]{2,1,0:T(8,128)S(1)}, f32[7,16,8,1152]{3,2,1,0:T(8,128)S(1)}, f32[8,16,1152]{2,1,0:T(8,128)S(1)}, f32[16,1152]{1,0:T(8,128)S...) custom-call(bf16[512,2048]{1,0:T(8,128)(2,1)} %key_ref.1, ...), custom_call_target="tpu_custom_call" | custom-call | flops 18874368 | bytes 11206656 | tf_op jit(solution)/shard_map/load_and_gather/pallas_call | solution.py:255
  4.1 0.0 copy-start.1
  4.2 0.0 copy-start.2
  4.2 3.1 %collective-permute-start.2 = (f32[16,1152]{1,0:T(8,128)S(1)}, f32[16,1152]{1,0:T(8,128)S(1)}, u32[]{:S(2)}, u32[]{:S(2)}) collective-permute-start(f32[16,1152]{1,0:T(8,128)S(1)} %get-tuple-element.39.refs_0_), channel_id=1, source_target_pairs={{0,1},{1,0},{2,3},{3,2},{4,5},{5,4},{6,7},{7,6},{8,9},{9,8},{10,11... | collective-permute-start | bytes 221192 | tf_op jit(solution)/shard_map/ppermute | solution.py:299
  7.3 0.0 copy-done
  7.3 2.3 %gather_states.1 = (f32[64,8,896]{2,1,0:T(8,128)S(1)}, f32[7,16,8,896]{3,2,1,0:T(8,128)S(1)}, f32[8,16,896]{2,1,0:T(8,128)S(1)}, f32[16,896]{1,0:T(8,128)S(1)}) custom-call(bf16[512,896]{1,0:T(8,128)(2,1)S(1)} %get-tuple-element.25.key_ref, bf16[512,896]{1,0:T(8,128)(2,1)S(1)} %get-tuple-element.26.value_ref, f32[16,2048]{1,0:T(8,128)S(1)} %copy-done), custom_call_target="tpu_custom_call" | custom-call | flops 14680064 | bytes 8716288 | tf_op jit(solution)/shard_map/gather_states/pallas_call | solution.py:267
  9.6 0.1 collective-permute-start
  9.7 0.0 collective-permute-done.2.come_ref
  9.7 3.1 %collective-permute-start.3 = (f32[16,1152]{1,0:T(8,128)S(1)}, f32[16,1152]{1,0:T(8,128)S(1)}, u32[]{:S(2)}, u32[]{:S(2)}) collective-permute-start(f32[16,1152]{1,0:T(8,128)S(1)} %get-tuple-element.40), channel_id=1, source_target_pairs={{0,2},{1,3},{2,0},{3,1},{4,6},{5,7},{6,4},{7,5},{8,10},{9,11},{10,... | collective-permute-start | bytes 221192 | tf_op jit(solution)/shard_map/ppermute | solution.py:299
  12.8 0.0 copy-done.1
  12.8 0.0 copy-done.2
  12.8 0.9 %near_terms.2 = (f32[64,8,896]{2,1,0:T(8,128)S(1)}, f32[7,16,8,896]{3,2,1,0:T(8,128)S(1)}) custom-call(f32[64,8,896]{2,1,0:T(8,128)S(1)} %get-tuple-element.27.signal_ref, f32[7,16,8,896]{3,2,1,0:T(8,128)S(1)} %get-tuple-element.28.sums_ref, f32[16,2048]{1,0:T(8,128)S(1)} %copy-done.1, f32[16,2048]{1,0:T(8,128)S(1)} %copy-done, f32[1,2048]{1,0:T(1,128)S(1)} %bitcast.1), custom_call_target="tpu_custom_call" | custom-call | flops 4587520 | bytes 3211264 | tf_op jit(solution)/shard_map/near_terms/pallas_call | solution.py:282
  13.7 1.1 %near_terms.3 = (f32[64,8,1152]{2,1,0:T(8,128)S(1)}, f32[7,16,8,1152]{3,2,1,0:T(8,128)S(1)}) custom-call(f32[64,8,1152]{2,1,0:T(8,128)S(1)} %get-tuple-element.33.signal_ref, f32[7,16,8,1152]{3,2,1,0:T(8,128)S(1)} %get-tuple-element.34.sums_ref, f32[16,2048]{1,0:T(8,128)S(1)} %copy-done.1, f32[16,2048]{1,0:T(8,128)S(1)} %copy-done, f32[1,2048]{1,0:T(1,128)S(1)} %bitcast.2), custom_call_target="tpu_custom_call" | custom-call | flops 5898240 | bytes 4128768 | tf_op jit(solution)/shard_map/near_terms/pallas_call | solution.py:282
  14.8 0.0 collective-permute-done.come_ref
  14.8 1.7 %collective-permute-start.1 = (f32[16,896]{1,0:T(8,128)S(1)}, f32[16,896]{1,0:T(8,128)S(1)}, u32[]{:S(2)}, u32[]{:S(2)}) collective-permute-start(f32[16,896]{1,0:T(8,128)S(1)} %get-tuple-element.36), channel_id=1, source_target_pairs={{0,2},{1,3},{2,0},{3,1},{4,6},{5,7},{6,4},{7,5},{8,10},{9,11},{10,... | collective-permute-start | bytes 172040 | tf_op jit(solution)/shard_map/ppermute | solution.py:299
  16.5 0.0 collective-permute-done.3.come_ref
  16.5 3.2 %spread_states.1.refs_0_.held_ref = bf16[512,1152]{1,0:T(8,128)(2,1)S(1)} custom-call(bf16[512,2048]{1,0:T(8,128)(2,1)S(1)} %get-tuple-element.24.query_ref, f32[64,8,1152]{2,1,0:T(8,128)S(1)} %get-tuple-element.35.refs_0_.near_ref, f32[7,16,8,1152]{3,2,1,0:T(8,128)S(1)} %get-tuple-element.37.sums_ref, f32[8,16,1152]{2,1,0:T(8,128)S(1)} %get-tuple-element.38.scan_ref, ...), custom_call_target="tpu_custom_call" | custom-call | flops 18874368 | bytes 12386304 | tf_op jit(solution)/shard_map/spread_states/pallas_call | solution.py:321
  19.7 0.2 collective-permute-done.1.come_ref
  20.0 3.2 %spread_and_store.1 = bf16[512,2048]{1,0:T(8,128)(2,1)} custom-call(bf16[512,2048]{1,0:T(8,128)(2,1)S(1)} %get-tuple-element.24.query_ref, f32[64,8,896]{2,1,0:T(8,128)S(1)} %get-tuple-element.29.refs_1_.near_ref, f32[7,16,8,896]{3,2,1,0:T(8,128)S(1)} %get-tuple-element.30.sums_ref, f32[8,16,896]{2,1,0:T(8,128)S(1)} %get-tuple-element.31.scan_ref, ...), custom_call_target="tpu_custom_call" | custom-call | flops 14680064 | bytes 9633792 | tf_op jit(solution)/shard_map/spread_and_store/pallas_call | solution.py:332
  (4 shorter events, 0.1 us)
Async XLA Ops:
  0.0 7.3 %copy-start = (f32[16,2048]{1,0:T(8,128)S(1)}, f32[16,2048]{1,0:T(8,128)}, u32[]{:S(2)}) copy-start(f32[16,2048]{1,0:T(8,128)} %decays_ref.19) | copy-start | bytes 393220
  4.1 8.6 %copy-start.1 = (f32[16,2048]{1,0:T(8,128)S(1)}, f32[16,2048]{1,0:T(8,128)}, u32[]{:S(2)}) copy-start(f32[16,2048]{1,0:T(8,128)} %residues_ref.7) | copy-start | bytes 393220
  4.2 8.6 %copy-start.2 = (f32[2048]{0:T(1024)S(1)}, f32[2048]{0:T(1024)}, u32[]{:S(2)}) copy-start(f32[2048]{0:T(1024)} %param.11) | copy-start | bytes 24580
  4.2 5.5 %collective-permute-start.2 = (f32[16,1152]{1,0:T(8,128)S(1)}, f32[16,1152]{1,0:T(8,128)S(1)}, u32[]{:S(2)}, u32[]{:S(2)}) collective-permute-start(f32[16,1152]{1,0:T(8,128)S(1)} %get-tuple-element.39.refs_0_), channel_id=1, source_target_pairs={{0,1},{1,0},{2,3},{3,2},{4,5},{5,4},{6,7},{7,6},{8,9},{9,8},{10,11... | collective-permute-start | bytes 221192 | tf_op jit(solution)/shard_map/ppermute | solution.py:299
  9.6 5.2 %collective-permute-start = (f32[16,896]{1,0:T(8,128)S(1)}, f32[16,896]{1,0:T(8,128)S(1)}, u32[]{:S(2)}, u32[]{:S(2)}) collective-permute-start(f32[16,896]{1,0:T(8,128)S(1)} %get-tuple-element.32.refs_2_), channel_id=1, source_target_pairs={{0,1},{1,0},{2,3},{3,2},{4,5},{5,4},{6,7},{7,6},{8,9},{9,8},{10,11... | collective-permute-start | bytes 172040 | tf_op jit(solution)/shard_map/ppermute | solution.py:299
  9.7 6.8 %collective-permute-start.3 = (f32[16,1152]{1,0:T(8,128)S(1)}, f32[16,1152]{1,0:T(8,128)S(1)}, u32[]{:S(2)}, u32[]{:S(2)}) collective-permute-start(f32[16,1152]{1,0:T(8,128)S(1)} %get-tuple-element.40), channel_id=1, source_target_pairs={{0,2},{1,3},{2,0},{3,1},{4,6},{5,7},{6,4},{7,5},{8,10},{9,11},{10,... | collective-permute-start | bytes 221192 | tf_op jit(solution)/shard_map/ppermute | solution.py:299
  14.8 5.1 %collective-permute-start.1 = (f32[16,896]{1,0:T(8,128)S(1)}, f32[16,896]{1,0:T(8,128)S(1)}, u32[]{:S(2)}, u32[]{:S(2)}) collective-permute-start(f32[16,896]{1,0:T(8,128)S(1)} %get-tuple-element.36), channel_id=1, source_target_pairs={{0,2},{1,3},{2,0},{3,1},{4,6},{5,7},{6,4},{7,5},{8,10},{9,11},{10,... | collective-permute-start | bytes 172040 | tf_op jit(solution)/shard_map/ppermute | solution.py:299

commit v5 on v4

v5 whole, which is shorter than its diff:
```python
import functools

import jax
import jax.numpy as jnp
from jax import lax
from jax.experimental import pallas as pl
from jax.experimental.pallas import tpu as pltpu
from jax.sharding import PartitionSpec as P

SEG = 8
CHUNK = 8
LANES = 128
SLABS = (0, 1, 4)
MIB = 2**20

VMEM = pl.BlockSpec(memory_space=pltpu.VMEM)
HBM = pl.BlockSpec(memory_space=pltpu.HBM)


def row(ref, index, lanes=slice(None)):
    return jnp.broadcast_to(ref[pl.ds(index, 1), lanes], (SEG, LANES))


def lane_block(block):
    return pl.ds(pl.multiple_of(block * LANES, LANES), LANES)


def channels_of(other, count):
    mine = lax.axis_index("half")
    return pl.multiple_of((1 - mine if other else mine) * count, LANES)


def gather_states(other, key_ref, value_ref, decays_ref, signal_ref, sums_ref, scan_ref, natural, turned, damp, damp_chunk, end_ref=None, arrive=None):
    rows = key_ref.shape[0]
    blocks, _, modes, _ = scan_ref.shape
    seg_len = rows // SEG
    chunks = seg_len // CHUNK
    pitch = seg_len + 1
    first = channels_of(other, blocks * LANES) if other else 0

    @pl.loop(0, blocks)
    def _(block):
        if arrive is not None:
            arrive(block)
        lanes = lane_block(block)
        decay = decays_ref[:, pl.ds(pl.multiple_of(first + block * LANES, LANES), LANES)]
        damp[...] = jnp.exp(-decay)
        damp_chunk[...] = jnp.exp(-CHUNK * decay)
        damp_segment = jnp.exp(-seg_len * decay)
        for start in range(0, rows, 16):
            part = pl.ds(start, 16)
            place = start // seg_len * pitch + start % seg_len
            natural[pl.ds(place, 16), :] = key_ref[part, lanes].astype(jnp.float32) * value_ref[part, lanes].astype(jnp.float32)
        states = [None] * modes
        for chunk in range(chunks):
            signal = [natural[pl.ds(chunk * CHUNK + step, SEG, stride=pitch), :] for step in range(CHUNK)]
            for step in range(CHUNK):
                signal_ref[block, chunk * CHUNK + step] = signal[step]
            for mode in range(modes):
                factor = row(damp, mode)
                total = signal[0]
                for step in range(1, CHUNK):
                    total = total * factor + signal[step]
                if chunk < chunks - 1:
                    sums_ref[block, chunk, mode] = total
                states[mode] = total if chunk == 0 else states[mode] * row(damp_chunk, mode) + total
        for mode in range(modes):
            turned[pl.ds(mode * (SEG + 1), SEG), :] = states[mode]
        state = jnp.zeros((modes, LANES), jnp.float32)
        for segment in range(SEG):
            scan_ref[block, segment] = state
            if end_ref is not None or segment < SEG - 1:
                state = state * damp_segment + turned[pl.ds(segment, modes, stride=SEG + 1), :]
        if end_ref is not None:
            end_ref[:, lanes] = state


def load_and_gather(
    key_ref, value_ref, query_ref, decays_ref, signal_ref, sums_ref, scan_ref, end_ref, later_key_ref, later_value_ref, later_query_ref, natural, turned, damp, damp_chunk, keys, values, rates, sems
):
    blocks = scan_ref.shape[0]
    width = blocks * LANES
    first = channels_of(False, width)
    rate_copy = pltpu.make_async_copy(decays_ref.at[:, pl.ds(first, width)], rates, sems.at[2, 0])
    starts = [start for start in SLABS if start < blocks]
    slabs = []
    for index, (start, stop) in enumerate(zip(starts, starts[1:] + [blocks])):
        lanes = pl.ds(start * LANES, (stop - start) * LANES)
        wide = pl.ds(pl.multiple_of(first + start * LANES, LANES), (stop - start) * LANES)
        slabs.append(
            (
                pltpu.make_async_copy(key_ref.at[:, wide], keys.at[:, lanes], sems.at[0, index]),
                pltpu.make_async_copy(value_ref.at[:, wide], values.at[:, lanes], sems.at[1, index]),
            )
        )
        for copy in slabs[-1]:
            copy.start()
        if index == 0:
            rate_copy.start()
    later = pl.ds(channels_of(True, width), width)
    later_copies = (
        pltpu.make_async_copy(key_ref.at[:, later], later_key_ref.at[:, pl.ds(0, width)], sems.at[2, 1]),
        pltpu.make_async_copy(value_ref.at[:, later], later_value_ref.at[:, pl.ds(0, width)], sems.at[2, 2]),
        pltpu.make_async_copy(query_ref, later_query_ref.at[:, pl.ds(0, query_ref.shape[1])], sems.at[2, 3]),
    )
    for copy in later_copies:
        copy.start()
    rate_copy.wait()

    def arrive(block):
        for start, copies in zip(starts, slabs):

            @pl.when(block == start)
            def _(copies=copies):
                for copy in copies:
                    copy.wait()

    gather_states(False, keys, values, rates, signal_ref, sums_ref, scan_ref, natural, turned, damp, damp_chunk, end_ref, arrive)
    for copy in later_copies:
        copy.wait()


def carry(other, reach, radix, rows, after, decays_ref, total_ref, *refs):
    refs = list(refs[after:])
    come = [total_ref[...]] + [refs.pop(0)[...] for _ in range(1, radix)][::-1]
    enter = refs.pop(0)[...] if reach > 1 else 0.0
    count = total_ref.shape[1]
    decay = decays_ref[:, pl.ds(channels_of(other, count), count)]
    rank = lax.axis_index("ctx")
    digit = rank // reach & (radix - 1)
    inside = rank & (reach - 1)
    total = 0.0
    for turn in range(radix):
        source = digit ^ turn
        if turn:
            behind = jnp.maximum(digit - 1 - source, 0) * reach + inside
            enter = enter + jnp.where(source < digit, jnp.exp(-(behind * rows).astype(jnp.float32) * decay) * come[turn], 0.0)
        if len(refs) > 1:
            total = total + jnp.exp(-((radix - 1 - source) * (reach * rows)).astype(jnp.float32) * decay) * come[turn]
    refs[0][...] = enter
    if len(refs) > 1:
        refs[1][...] = total


def near_terms(other, signal_ref, sums_ref, residues_ref, decays_ref, skip_ref, near_ref, scaled_ref):
    blocks, steps, _, _ = signal_ref.shape
    modes = decays_ref.shape[0]
    chunks = steps // CHUNK
    first = channels_of(other, blocks * LANES)

    @pl.loop(0, blocks)
    def _(block):
        wide = pl.ds(pl.multiple_of(first + block * LANES, LANES), LANES)
        decay = decays_ref[:, wide]
        term = residues_ref[:, wide] * jnp.sqrt(decay)
        damp = jnp.exp(-decay)
        weight = term * damp
        taps = []
        for step in range(CHUNK):
            tap = jnp.sum(term, 0, keepdims=True)
            if step == 0:
                tap = tap + skip_ref[:, wide]
            taps.append(jnp.broadcast_to(tap, (SEG, LANES)))
            term = term * damp
        for chunk in range(chunks):
            signal = [signal_ref[block, chunk * CHUNK + step] for step in range(CHUNK)]
            for step in range(CHUNK):
                total = taps[0] * signal[step]
                for back in range(1, step + 1):
                    total = total + taps[back] * signal[step - back]
                near_ref[block, chunk * CHUNK + step] = total
        for mode in range(modes):
            factor = jnp.broadcast_to(weight[mode : mode + 1, :], (SEG, LANES))
            scaled = [factor * sums_ref[block, chunk, mode] for chunk in range(chunks - 1)]
            for chunk in range(chunks - 1):
                scaled_ref[block, chunk, mode] = scaled[chunk]


def spread_states(other, query_ref, near_ref, sums_ref, scan_ref, enter_ref, residues_ref, decays_ref, _, gated_ref, natural, turned, damp, leave=None):
    rows = gated_ref.shape[0]
    blocks, _, modes, _ = scan_ref.shape
    first = channels_of(other, blocks * LANES)
    seg_len = rows // SEG
    chunks = seg_len // CHUNK
    pitch = seg_len + 1

    @pl.loop(0, blocks)
    def _(block):
        lanes = lane_block(block)
        wide = pl.ds(pl.multiple_of(first + block * LANES, LANES), LANES)
        decay = decays_ref[:, wide]
        once = jnp.exp(-decay)
        damp[...] = once
        scale = residues_ref[:, wide] * jnp.sqrt(decay) * once
        damp_segment = jnp.exp(-seg_len * decay)
        enter = enter_ref[:, lanes]
        for segment in range(SEG):
            turned[pl.ds(segment * (modes + 1), modes), :] = (scan_ref[block, segment] + enter) * scale
            enter = enter * damp_segment
        states = [turned[pl.ds(mode, SEG, stride=modes + 1), :] for mode in range(modes)]
        for chunk in range(chunks):
            conv = [near_ref[block, chunk * CHUNK + step] for step in range(CHUNK)]
            for mode in range(modes):
                factor = row(damp, mode)
                state = states[mode]
                for step in range(CHUNK):
                    conv[step] = conv[step] + state
                    if step < CHUNK - 1 or chunk < chunks - 1:
                        state = state * factor
                if chunk < chunks - 1:
                    states[mode] = state + sums_ref[block, chunk, mode]
            for step in range(CHUNK):
                natural[pl.ds(chunk * CHUNK + step, SEG, stride=pitch), :] = conv[step]
        for start in range(0, rows, 16):
            part = pl.ds(start, 16)
            place = start // seg_len * pitch + start % seg_len
            gated_ref[part, lanes] = (query_ref[part, wide].astype(jnp.float32) * natural[pl.ds(place, 16), :]).astype(jnp.bfloat16)
        if leave is not None:
            leave(block)


def spread_and_store(
    other, query_ref, near_ref, sums_ref, scan_ref, enter_ref, residues_ref, decays_ref, held_ref, mixed_ref, natural, turned, damp, gated, sems
):
    blocks = scan_ref.shape[0]
    width = blocks * LANES
    first = channels_of(other, width)
    held_copy = pltpu.make_async_copy(held_ref.at[:, pl.ds(0, width)], mixed_ref.at[:, pl.ds(channels_of(not other, width), width)], sems.at[blocks])
    held_copy.start()

    def copy(block):
        wide = pl.ds(pl.multiple_of(first + block * LANES, LANES), LANES)
        return pltpu.make_async_copy(gated.at[:, lane_block(block)], mixed_ref.at[:, wide], sems.at[block])

    spread_states(
        other, query_ref, near_ref, sums_ref, scan_ref, enter_ref, residues_ref, decays_ref, None, gated, natural, turned, damp, lambda block: copy(block).start()
    )

    @pl.loop(0, blocks)
    def _(block):
        copy(block).wait()

    held_copy.wait()


def shards(query_gate, key_gate, value_input, residues, decays, skip_gain):
    rows, width = key_gate.shape
    modes = residues.shape[0]
    seg_len = rows // SEG
    chunks = seg_len // CHUNK
    ctx_size = lax.axis_size("ctx")
    count = width // lax.axis_size("half")
    blocks = count // LANES
    padded = count + LANES * (1 - blocks % 2)
    skip_gain = skip_gain[None, :]
    real = functools.partial(pltpu.VMEM, dtype=jnp.float32)
    half = functools.partial(pltpu.VMEM, dtype=jnp.bfloat16)
    natural = real((SEG * (seg_len + 1), LANES))
    table = real((modes, LANES))

    def call(body, operands, out_shape, scratch, ops, moved, in_specs=None, out_specs=None, limit=4):
        return pl.pallas_call(
            body,
            in_specs=in_specs or [VMEM] * len(operands),
            out_specs=out_specs or jax.tree.map(lambda _: VMEM, out_shape),
            out_shape=out_shape,
            scratch_shapes=scratch,
            compiler_params=pltpu.CompilerParams(vmem_limit_bytes=limit * MIB),
            cost_estimate=pl.CostEstimate(flops=ops * rows * count, bytes_accessed=moved * rows * count, transcendentals=0),
            name=getattr(body, "func", body).__name__,
        )(*operands)

    state_shapes = [
        real((blocks, seg_len, SEG, LANES)),
        real((blocks, chunks - 1, modes, SEG, LANES)),
        real((blocks, SEG, modes, LANES)),
    ]
    scratch = [natural, real((modes * (SEG + 1), LANES)), table, table]
    *mine, later_keys, later_values, queries = call(
        load_and_gather,
        [pltpu.with_memory_space_constraint(array, pltpu.HBM) for array in (key_gate, value_input, query_gate, decays)],
        state_shapes + [real((modes, count)), half((rows, padded)), half((rows, padded)), half((rows, width + LANES))],
        scratch + [half((rows, padded)), half((rows, padded)), real((modes, count)), pltpu.SemaphoreType.DMA((3, 4))],
        2 * modes,
        19,
        in_specs=[HBM] * 4,
        limit=8,
    )
    theirs = call(functools.partial(gather_states, True), [later_keys, later_values, decays], state_shapes, scratch, 2 * modes, 19)
    nears = [
        call(
            functools.partial(near_terms, other),
            [signal, sums, residues, decays, skip_gain],
            [real(signal.shape), real(sums.shape)],
            [],
            10,
            7,
        )
        for other, (signal, sums, *_) in ((False, mine), (True, theirs))
    ]

    total, enter, reach = mine[3], None, 1
    while reach < ctx_size:
        radix = min(4, ctx_size // reach)
        come = [lax.ppermute(total, "ctx", [(i, i ^ (turn * reach)) for i in range(ctx_size)]) for turn in reversed(range(1, radix))]
        after = [near for near, _ in nears] if reach == 1 else []
        last = radix * reach == ctx_size
        result = call(
            functools.partial(carry, False, reach, radix, rows, len(after)),
            [decays, total, *after, *come] + ([] if enter is None else [enter]),
            [real((modes, count))] * (1 if last else 2),
            [],
            0,
            0,
        )
        enter, total = result[0], result[-1]
        reach *= radix
    enter_theirs = lax.ppermute(enter, "half", [(0, 1), (1, 0)])

    scratch = [natural, real((SEG * (modes + 1), LANES)), table]
    held = call(
        functools.partial(spread_states, False),
        [queries, *nears[0], mine[2], enter, residues, decays, nears[1][0]],
        half((rows, padded)),
        scratch,
        2 * modes,
        21,
    )
    return call(
        functools.partial(spread_and_store, True),
        [queries, *nears[1], theirs[2], enter_theirs, residues, decays, held],
        jax.ShapeDtypeStruct((rows, width), jnp.bfloat16),
        scratch + [half((rows, padded)), pltpu.SemaphoreType.DMA((blocks + 1,))],
        2 * modes,
        21,
        out_specs=HBM,
        limit=6,
    )


def solution(mesh):
    placed = (
        P("ctx", "chan"),
        P("ctx", "chan"),
        P("ctx", "chan"),
        P(None, "chan"),
        P(None, "chan"),
        P("chan"),
    )
    return jax.shard_map(shards, mesh=mesh, in_specs=placed, out_specs=P("ctx", "chan"), check_vma=False)
```

time: 23.4 us -> 22.5 us (0.962)
  starting transfers between devices: 7.94 us -> 7.34 us
  Pallas kernels: 15 us -> 14.6 us
    ppermute x4, starting transfers between devices: 7.94 us -> 7.34 us  [the longest x3 5.76 us: shards(): lax.ppermute(total, 'ctx', [(i, i ^ turn * reach) for i in range(ctx_size)])]
    pallas_call x10 -> x7, Pallas kernels: 15 us -> 14.6 us  [call(): pl.pallas_call(body, in_specs=in_specs or [VMEM] * len(operands), out_spe...]
where the time goes in v5:
time: 22.5 us; the launch traced here: 22.4 us
  Pallas kernels  14.6 us (65%)
  starting transfers between devices  7.34 us (33%)
  waiting for transfers between devices  0.34 us (2%)
    pallas_call x7, Pallas kernels, call(): pl.pallas_call(body, in_specs=in_specs or [VMEM] * len(operands), out_spe...  14.6 us
    ppermute x3, starting transfers between devices, shards(): lax.ppermute(total, 'ctx', [(i, i ^ turn * reach) for i in range(ctx_size)])  5.76 us
    ppermute x1, starting transfers between devices, shards(): enter_theirs = lax.ppermute(enter, 'half', [(0, 1), (1, 0)])  1.58 us
  transfers between devices with their start and end apart: 4, of which 1 were waited for; matrix products, arithmetic and copies ran while one was open for 0% of the time, Pallas kernels for 33%

profile of v5, /device:TPU:0, one launch (start us, length us, event | category | flops | bytes accessed | tf_op | source)
XLA Modules:
  0.0 22.4 jit_solution(6915593461436112468)
XLA Ops:
  0.0 0.0 copy-start
  0.0 3.8 %load_and_gather.1 = (f32[8,64,8,128]{3,2,1,0:T(8,128)S(1)}, f32[8,7,16,8,128]{4,3,2,1,0:T(8,128)S(1)}, f32[8,8,16,128]{3,2,1,0:T(8,128)S(1)}, f32[16,1024]{1,0:...) custom-call(bf16[512,2048]{1,0:T(8,128)(2,1)} %key_ref.1, ...), custom_call_target="tpu_custom_call" | custom-call | flops 16777216 | bytes 9961472 | tf_op jit(solution)/shard_map/load_and_gather/pallas_call | solution.py:262
  3.8 0.0 copy-start.1
  3.8 0.0 copy-start.2
  3.8 5.1 %collective-permute-start = (f32[16,1024]{1,0:T(8,128)S(1)}, f32[16,1024]{1,0:T(8,128)S(1)}, u32[]{:S(2)}, u32[]{:S(2)}) collective-permute-start(f32[16,1024]{1,0:T(8,128)S(1)} %get-tuple-element.27.total_ref), channel_id=1, source_target_pairs={{0,3},{1,2},{2,1},{3,0},{4,7},{5,6},{6,5},{7,4},{8,11},{9,10},{10,... | collective-permute-start | bytes 196616 | tf_op jit(solution)/shard_map/ppermute | solution.py:305
  8.9 0.0 collective-permute-start.1
  8.9 0.6 %collective-permute-start.2 = (f32[16,1024]{1,0:T(8,128)S(1)}, f32[16,1024]{1,0:T(8,128)S(1)}, u32[]{:S(2)}, u32[]{:S(2)}) collective-permute-start(f32[16,1024]{1,0:T(8,128)S(1)} %get-tuple-element.27.total_ref), channel_id=1, source_target_pairs={{0,1},{1,0},{2,3},{3,2},{4,5},{5,4},{6,7},{7,6},{8,9},{9,8},{10,11... | collective-permute-start | bytes 196616 | tf_op jit(solution)/shard_map/ppermute | solution.py:305
  9.5 0.0 copy-done
  9.6 2.6 %gather_states.1 = (f32[8,64,8,128]{3,2,1,0:T(8,128)S(1)}, f32[8,7,16,8,128]{4,3,2,1,0:T(8,128)S(1)}, f32[8,8,16,128]{3,2,1,0:T(8,128)S(1)}) custom-call(bf16[512,1152]{1,0:T(8,128)(2,1)S(1)} %get-tuple-element.20.key_ref, bf16[512,1152]{1,0:T(8,128)(2,1)S(1)} %get-tuple-element.21.value_ref, f32[16,2048]{1,0:T(8,128)S(1)} %copy-done), custom_call_target="tpu_custom_call" | custom-call | flops 16777216 | bytes 9961472 | tf_op jit(solution)/shard_map/gather_states/pallas_call | solution.py:262
  12.2 0.0 copy-done.1
  12.2 0.0 copy-done.2
  12.2 1.0 %near_terms.2 = (f32[8,64,8,128]{3,2,1,0:T(8,128)S(1)}, f32[8,7,16,8,128]{4,3,2,1,0:T(8,128)S(1)}) custom-call(f32[8,64,8,128]{3,2,1,0:T(8,128)S(1)} %get-tuple-element.22.signal_ref, f32[8,7,16,8,128]{4,3,2,1,0:T(8,128)S(1)} %get-tuple-element.23.sums_ref, f32[16,2048]{1,0:T(8,128)S(1)} %copy-done.1, f32[16,2048]{1,0:T(8,128)S(1)} %copy-done, ...), custom_call_target="tpu_custom_call" | custom-call | flops 5242880 | bytes 3670016 | tf_op jit(solution)/shard_map/near_terms/pallas_call | solution.py:262
  13.2 1.0 %near_terms.3 = (f32[8,64,8,128]{3,2,1,0:T(8,128)S(1)}, f32[8,7,16,8,128]{4,3,2,1,0:T(8,128)S(1)}) custom-call(f32[8,64,8,128]{3,2,1,0:T(8,128)S(1)} %get-tuple-element.28.signal_ref, f32[8,7,16,8,128]{4,3,2,1,0:T(8,128)S(1)} %get-tuple-element.29.sums_ref, f32[16,2048]{1,0:T(8,128)S(1)} %copy-done.1, f32[16,2048]{1,0:T(8,128)S(1)} %copy-done, ...), custom_call_target="tpu_custom_call" | custom-call | flops 5242880 | bytes 3670016 | tf_op jit(solution)/shard_map/near_terms/pallas_call | solution.py:262
  14.2 0.0 collective-permute-done.refs_2_
  14.2 0.3 %collective-permute-done.1.refs_3_ = f32[16,1024]{1,0:T(8,128)S(1)} collective-permute-done((f32[16,1024]{1,0:T(8,128)S(1)}, f32[16,1024]{1,0:T(8,128)S(1)}, u32[]{:S(2)}, u32[]{:S(2)}) %collective-permute-start.1) | collective-permute-done | bytes 65568 | tf_op jit(solution)/shard_map/ppermute | solution.py:305
  14.5 0.0 collective-permute-done.2.refs_4_
  14.6 1.6 %collective-permute-start.3 = (f32[16,1024]{1,0:T(8,128)S(1)}, f32[16,1024]{1,0:T(8,128)S(1)}, u32[]{:S(2)}, u32[]{:S(2)}) collective-permute-start(f32[16,1024]{1,0:T(8,128)S(1)} %carry.1.enter_ref), channel_id=1, source_target_pairs={{0,4},{4,0},{1,5},{5,1},{2,6},{6,2},{3,7},{7,3},{8,12},{12,8},{9,1... | collective-permute-start | bytes 196616 | tf_op jit(solution)/shard_map/ppermute | solution.py:318
  16.1 2.8 %spread_states.1.held_ref = bf16[512,1152]{1,0:T(8,128)(2,1)S(1)} custom-call(bf16[512,2176]{1,0:T(8,128)(2,1)S(1)} %get-tuple-element.19.query_ref, f32[8,64,8,128]{3,2,1,0:T(8,128)S(1)} %get-tuple-element.30.refs_0_.near_ref, f32[8,7,16,8,128]{4,3,2,1,0:T(8,128)S(1)} %get-tuple-element.31.sums_ref, f32[8,8,16,128]{3,2,1,0:T(8,128)S(1)} %get-tuple-element.32.scan_ref, ...), custom_call_target="tpu_custom_call" | custom-call | flops 16777216 | bytes 11010048 | tf_op jit(solution)/shard_map/spread_states/pallas_call | solution.py:262
  18.9 0.0 collective-permute-done.3.enter_ref
  18.9 3.5 %spread_and_store.1 = bf16[512,2048]{1,0:T(8,128)(2,1)} custom-call(bf16[512,2176]{1,0:T(8,128)(2,1)S(1)} %get-tuple-element.19.query_ref, f32[8,64,8,128]{3,2,1,0:T(8,128)S(1)} %get-tuple-element.24.refs_1_._.near_ref, f32[8,7,16,8,128]{4,3,2,1,0:T(8,128)S(1)} %get-tuple-element.25.sums_ref, f32[8,8,16,128]{3,2,1,0:T(8,128)S(1)} %get-tuple-element.26.scan_ref, ...), custom_call_target="tpu_custom_call" | custom-call | flops 16777216 | bytes 11010048 | tf_op jit(solution)/shard_map/spread_and_store/pallas_call | solution.py:262
  (1 shorter events, 0.0 us)
Async XLA Ops:
  0.0 9.6 %copy-start = (f32[16,2048]{1,0:T(8,128)S(1)}, f32[16,2048]{1,0:T(8,128)}, u32[]{:S(2)}) copy-start(f32[16,2048]{1,0:T(8,128)} %decays_ref.13) | copy-start | bytes 393220
  3.8 8.4 %copy-start.1 = (f32[16,2048]{1,0:T(8,128)S(1)}, f32[16,2048]{1,0:T(8,128)}, u32[]{:S(2)}) copy-start(f32[16,2048]{1,0:T(8,128)} %residues_ref.7) | copy-start | bytes 393220
  3.8 8.4 %copy-start.2 = (f32[2048]{0:T(1024)S(1)}, f32[2048]{0:T(1024)}, u32[]{:S(2)}) copy-start(f32[2048]{0:T(1024)} %param.11) | copy-start | bytes 24580
  3.8 10.4 %collective-permute-start = (f32[16,1024]{1,0:T(8,128)S(1)}, f32[16,1024]{1,0:T(8,128)S(1)}, u32[]{:S(2)}, u32[]{:S(2)}) collective-permute-start(f32[16,1024]{1,0:T(8,128)S(1)} %get-tuple-element.27.total_ref), channel_id=1, source_target_pairs={{0,3},{1,2},{2,1},{3,0},{4,7},{5,6},{6,5},{7,4},{8,11},{9,10},{10,... | collective-permute-start | bytes 196616 | tf_op jit(solution)/shard_map/ppermute | solution.py:305
  8.9 5.6 %collective-permute-start.1 = (f32[16,1024]{1,0:T(8,128)S(1)}, f32[16,1024]{1,0:T(8,128)S(1)}, u32[]{:S(2)}, u32[]{:S(2)}) collective-permute-start(f32[16,1024]{1,0:T(8,128)S(1)} %get-tuple-element.27.total_ref), channel_id=1, source_target_pairs={{0,2},{1,3},{2,0},{3,1},{4,6},{5,7},{6,4},{7,5},{8,10},{9,11},{10,... | collective-permute-start | bytes 196616 | tf_op jit(solution)/shard_map/ppermute | solution.py:305
  8.9 5.6 %collective-permute-start.2 = (f32[16,1024]{1,0:T(8,128)S(1)}, f32[16,1024]{1,0:T(8,128)S(1)}, u32[]{:S(2)}, u32[]{:S(2)}) collective-permute-start(f32[16,1024]{1,0:T(8,128)S(1)} %get-tuple-element.27.total_ref), channel_id=1, source_target_pairs={{0,1},{1,0},{2,3},{3,2},{4,5},{5,4},{6,7},{7,6},{8,9},{9,8},{10,11... | collective-permute-start | bytes 196616 | tf_op jit(solution)/shard_map/ppermute | solution.py:305
  14.6 4.3 %collective-permute-start.3 = (f32[16,1024]{1,0:T(8,128)S(1)}, f32[16,1024]{1,0:T(8,128)S(1)}, u32[]{:S(2)}, u32[]{:S(2)}) collective-permute-start(f32[16,1024]{1,0:T(8,128)S(1)} %carry.1.enter_ref), channel_id=1, source_target_pairs={{0,4},{4,0},{1,5},{5,1},{2,6},{6,2},{3,7},{7,3},{8,12},{12,8},{9,1... | collective-permute-start | bytes 196616 | tf_op jit(solution)/shard_map/ppermute | solution.py:318

commit v6 on v5

--- a/solution.py
+++ b/solution.py
@@ -10,8 +10,10 @@
 SEG = 8
 CHUNK = 8
 LANES = 128
-SLABS = (0, 1, 4)
+SLABS = (0, 2, 4)
+PAIR = 2
 MIB = 2**20
+TURNS = {2: (1,), 4: (2, 3, 1)}
 
 VMEM = pl.BlockSpec(memory_space=pltpu.VMEM)
 HBM = pl.BlockSpec(memory_space=pltpu.HBM)
@@ -30,7 +32,7 @@
     return pl.multiple_of((1 - mine if other else mine) * count, LANES)
 
 
-def gather_states(other, key_ref, value_ref, decays_ref, signal_ref, sums_ref, scan_ref, natural, turned, damp, damp_chunk, end_ref=None, arrive=None):
+def gather_states(other, key_ref, value_ref, decays_ref, signal_ref, sums_ref, scan_ref, *scratch, end_ref=None, arrive=None):
     rows = key_ref.shape[0]
     blocks, _, modes, _ = scan_ref.shape
     seg_len = rows // SEG
@@ -38,10 +40,7 @@
     pitch = seg_len + 1
     first = channels_of(other, blocks * LANES) if other else 0
 
-    @pl.loop(0, blocks)
-    def _(block):
-        if arrive is not None:
-            arrive(block)
+    def one(block, natural, turned, damp, damp_chunk):
         lanes = lane_block(block)
         decay = decays_ref[:, pl.ds(pl.multiple_of(first + block * LANES, LANES), LANES)]
         damp[...] = jnp.exp(-decay)
@@ -74,10 +73,18 @@
         if end_ref is not None:
             end_ref[:, lanes] = state
 
+    @pl.loop(0, blocks // PAIR)
+    def _(pair):
+        if arrive is not None:
+            arrive(pair)
+        for turn in range(PAIR):
+            one(pair * PAIR + turn, *scratch[turn::PAIR])
+
 
 def load_and_gather(
-    key_ref, value_ref, query_ref, decays_ref, signal_ref, sums_ref, scan_ref, end_ref, later_key_ref, later_value_ref, later_query_ref, natural, turned, damp, damp_chunk, keys, values, rates, sems
+    key_ref, value_ref, query_ref, decays_ref, signal_ref, sums_ref, scan_ref, end_ref, later_key_ref, later_value_ref, later_query_ref, *scratch
 ):
+    *scratch, keys, values, rates, sems = scratch
     blocks = scan_ref.shape[0]
     width = blocks * LANES
     first = channels_of(False, width)
@@ -107,22 +114,23 @@
         copy.start()
     rate_copy.wait()
 
-    def arrive(block):
+    def arrive(pair):
         for start, copies in zip(starts, slabs):
 
-            @pl.when(block == start)
+            @pl.when(pair * PAIR == start)
             def _(copies=copies):
                 for copy in copies:
                     copy.wait()
 
-    gather_states(False, keys, values, rates, signal_ref, sums_ref, scan_ref, natural, turned, damp, damp_chunk, end_ref, arrive)
+    gather_states(False, keys, values, rates, signal_ref, sums_ref, scan_ref, *scratch, end_ref=end_ref, arrive=arrive)
     for copy in later_copies:
         copy.wait()
 
 
 def carry(other, reach, radix, rows, after, decays_ref, total_ref, *refs):
     refs = list(refs[after:])
-    come = [total_ref[...]] + [refs.pop(0)[...] for _ in range(1, radix)][::-1]
+    come = {turn: refs.pop(0)[...] for turn in TURNS[radix]}
+    come[0] = total_ref[...]
     enter = refs.pop(0)[...] if reach > 1 else 0.0
     count = total_ref.shape[1]
     decay = decays_ref[:, pl.ds(channels_of(other, count), count)]
@@ -176,7 +184,7 @@
                 scaled_ref[block, chunk, mode] = scaled[chunk]
 
 
-def spread_states(other, query_ref, near_ref, sums_ref, scan_ref, enter_ref, residues_ref, decays_ref, _, gated_ref, natural, turned, damp, leave=None):
+def spread_states(other, query_ref, near_ref, sums_ref, scan_ref, enter_ref, residues_ref, decays_ref, _, gated_ref, *scratch, leave=None):
     rows = gated_ref.shape[0]
     blocks, _, modes, _ = scan_ref.shape
     first = channels_of(other, blocks * LANES)
@@ -184,8 +192,7 @@
     chunks = seg_len // CHUNK
     pitch = seg_len + 1
 
-    @pl.loop(0, blocks)
-    def _(block):
+    def one(block, natural, turned, damp):
         lanes = lane_block(block)
         wide = pl.ds(pl.multiple_of(first + block * LANES, LANES), LANES)
         decay = decays_ref[:, wide]
@@ -215,13 +222,20 @@
             part = pl.ds(start, 16)
             place = start // seg_len * pitch + start % seg_len
             gated_ref[part, lanes] = (query_ref[part, wide].astype(jnp.float32) * natural[pl.ds(place, 16), :]).astype(jnp.bfloat16)
+
+    @pl.loop(0, blocks // PAIR)
+    def _(pair):
+        for turn in range(PAIR):
+            one(pair * PAIR + turn, *scratch[turn::PAIR])
         if leave is not None:
-            leave(block)
+            for turn in range(PAIR):
+                leave(pair * PAIR + turn)
 
 
 def spread_and_store(
-    other, query_ref, near_ref, sums_ref, scan_ref, enter_ref, residues_ref, decays_ref, held_ref, mixed_ref, natural, turned, damp, gated, sems
+    other, query_ref, near_ref, sums_ref, scan_ref, enter_ref, residues_ref, decays_ref, held_ref, mixed_ref, *scratch
 ):
+    *scratch, gated, sems = scratch
     blocks = scan_ref.shape[0]
     width = blocks * LANES
     first = channels_of(other, width)
@@ -233,7 +247,7 @@
         return pltpu.make_async_copy(gated.at[:, lane_block(block)], mixed_ref.at[:, wide], sems.at[block])
 
     spread_states(
-        other, query_ref, near_ref, sums_ref, scan_ref, enter_ref, residues_ref, decays_ref, None, gated, natural, turned, damp, lambda block: copy(block).start()
+        other, query_ref, near_ref, sums_ref, scan_ref, enter_ref, residues_ref, decays_ref, None, gated, *scratch, leave=lambda block: copy(block).start()
     )
 
     @pl.loop(0, blocks)
@@ -275,7 +289,7 @@
         real((blocks, chunks - 1, modes, SEG, LANES)),
         real((blocks, SEG, modes, LANES)),
     ]
-    scratch = [natural, real((modes * (SEG + 1), LANES)), table, table]
+    scratch = [shape for shape in (natural, real((modes * (SEG + 1), LANES)), table, table) for _ in range(PAIR)]
     *mine, later_keys, later_values, queries = call(
         load_and_gather,
         [pltpu.with_memory_space_constraint(array, pltpu.HBM) for array in (key_gate, value_input, query_gate, decays)],
@@ -286,9 +300,9 @@
         in_specs=[HBM] * 4,
         limit=8,
     )
-    theirs = call(functools.partial(gather_states, True), [later_keys, later_values, decays], state_shapes, scratch, 2 * modes, 19)
-    nears = [
-        call(
+    def near(other, states):
+        signal, sums = states[:2]
+        return call(
             functools.partial(near_terms, other),
             [signal, sums, residues, decays, skip_gain],
             [real(signal.shape), real(sums.shape)],
@@ -296,14 +310,16 @@
             10,
             7,
         )
-        for other, (signal, sums, *_) in ((False, mine), (True, theirs))
-    ]
+
+    theirs = call(functools.partial(gather_states, True), [later_keys, later_values, decays], state_shapes, scratch, 2 * modes, 19)
+    near_mine = near(False, mine)
+    near_theirs = near(True, theirs)
 
     total, enter, reach = mine[3], None, 1
     while reach < ctx_size:
         radix = min(4, ctx_size // reach)
-        come = [lax.ppermute(total, "ctx", [(i, i ^ (turn * reach)) for i in range(ctx_size)]) for turn in reversed(range(1, radix))]
-        after = [near for near, _ in nears] if reach == 1 else []
+        come = [lax.ppermute(total, "ctx", [(i, i ^ (turn * reach)) for i in range(ctx_size)]) for turn in TURNS[radix]]
+        after = [near_mine[0], near_theirs[0]] if reach == 1 else []
         last = radix * reach == ctx_size
         result = call(
             functools.partial(carry, False, reach, radix, rows, len(after)),
@@ -317,10 +333,10 @@
         reach *= radix
     enter_theirs = lax.ppermute(enter, "half", [(0, 1), (1, 0)])
 
-    scratch = [natural, real((SEG * (modes + 1), LANES)), table]
+    scratch = [shape for shape in (natural, real((SEG * (modes + 1), LANES)), table) for _ in range(PAIR)]
     held = call(
         functools.partial(spread_states, False),
-        [queries, *nears[0], mine[2], enter, residues, decays, nears[1][0]],
+        [queries, *near_mine, mine[2], enter, residues, decays, near_theirs[0]],
         half((rows, padded)),
         scratch,
         2 * modes,
@@ -328,7 +344,7 @@
     )
     return call(
         functools.partial(spread_and_store, True),
-        [queries, *nears[1], theirs[2], enter_theirs, residues, decays, held],
+        [queries, *near_theirs, theirs[2], enter_theirs, residues, decays, held],
         jax.ShapeDtypeStruct((rows, width), jnp.bfloat16),
         scratch + [half((rows, padded)), pltpu.SemaphoreType.DMA((blocks + 1,))],
         2 * modes,

time: 22.5 us -> 22.2 us (0.987)
  transfers between devices with their start and end apart: 4 -> 4, of which waited for: 1 -> 2; matrix products, arithmetic and copies ran while one was open for 0% -> 0% of each run, Pallas kernels for 33% -> 33%
where the time goes in v6:
time: 22.2 us; the launch traced here: 22.1 us
  Pallas kernels  14.5 us (65%)
  starting transfers between devices  7.27 us (33%)
    pallas_call x7, Pallas kernels, call(): pl.pallas_call(body, in_specs=in_specs or [VMEM] * len(operands), out_spe...  14.5 us
    ppermute x3, starting transfers between devices, shards(): lax.ppermute(total, 'ctx', [(i, i ^ turn * reach) for i in range(ctx_size)])  5.68 us
    ppermute x1, starting transfers between devices, shards(): enter_theirs = lax.ppermute(enter, 'half', [(0, 1), (1, 0)])  1.59 us
  transfers between devices with their start and end apart: 4, of which 2 were waited for; matrix products, arithmetic and copies ran while one was open for 0% of the time, Pallas kernels for 33%

profile of v6, /device:TPU:0, one launch (start us, length us, event | category | flops | bytes accessed | tf_op | source)
XLA Modules:
  0.0 22.1 jit_solution(12993384667866366104)
XLA Ops:
  0.0 0.0 copy-start
  0.0 3.7 %load_and_gather.1 = (f32[8,64,8,128]{3,2,1,0:T(8,128)S(1)}, f32[8,7,16,8,128]{4,3,2,1,0:T(8,128)S(1)}, f32[8,8,16,128]{3,2,1,0:T(8,128)S(1)}, f32[16,1024]{1,0:...) custom-call(bf16[512,2048]{1,0:T(8,128)(2,1)} %key_ref.1, ...), custom_call_target="tpu_custom_call" | custom-call | flops 16777216 | bytes 9961472 | tf_op jit(solution)/shard_map/load_and_gather/pallas_call | solution.py:276
  3.7 0.0 copy-start.1
  3.7 0.0 copy-start.2
  3.8 4.1 %collective-permute-start = (f32[16,1024]{1,0:T(8,128)S(1)}, f32[16,1024]{1,0:T(8,128)S(1)}, u32[]{:S(2)}, u32[]{:S(2)}) collective-permute-start(f32[16,1024]{1,0:T(8,128)S(1)} %get-tuple-element.27.total_ref), channel_id=1, source_target_pairs={{0,2},{1,3},{2,0},{3,1},{4,6},{5,7},{6,4},{7,5},{8,10},{9,11},{10,... | collective-permute-start | bytes 196616 | tf_op jit(solution)/shard_map/ppermute | solution.py:321
  7.9 1.3 %collective-permute-start.1 = (f32[16,1024]{1,0:T(8,128)S(1)}, f32[16,1024]{1,0:T(8,128)S(1)}, u32[]{:S(2)}, u32[]{:S(2)}) collective-permute-start(f32[16,1024]{1,0:T(8,128)S(1)} %get-tuple-element.27.total_ref), channel_id=1, source_target_pairs={{0,3},{1,2},{2,1},{3,0},{4,7},{5,6},{6,5},{7,4},{8,11},{9,10},{10,... | collective-permute-start | bytes 196616 | tf_op jit(solution)/shard_map/ppermute | solution.py:321
  9.2 0.2 %collective-permute-start.2 = (f32[16,1024]{1,0:T(8,128)S(1)}, f32[16,1024]{1,0:T(8,128)S(1)}, u32[]{:S(2)}, u32[]{:S(2)}) collective-permute-start(f32[16,1024]{1,0:T(8,128)S(1)} %get-tuple-element.27.total_ref), channel_id=1, source_target_pairs={{0,1},{1,0},{2,3},{3,2},{4,5},{5,4},{6,7},{7,6},{8,9},{9,8},{10,11... | collective-permute-start | bytes 196616 | tf_op jit(solution)/shard_map/ppermute | solution.py:321
  9.4 0.0 copy-done
  9.4 2.5 %gather_states.1 = (f32[8,64,8,128]{3,2,1,0:T(8,128)S(1)}, f32[8,7,16,8,128]{4,3,2,1,0:T(8,128)S(1)}, f32[8,8,16,128]{3,2,1,0:T(8,128)S(1)}) custom-call(bf16[512,1152]{1,0:T(8,128)(2,1)S(1)} %get-tuple-element.20.key_ref, bf16[512,1152]{1,0:T(8,128)(2,1)S(1)} %get-tuple-element.21.value_ref, f32[16,2048]{1,0:T(8,128)S(1)} %copy-done), custom_call_target="tpu_custom_call" | custom-call | flops 16777216 | bytes 9961472 | tf_op jit(solution)/shard_map/gather_states/pallas_call | solution.py:276
  12.0 0.0 copy-done.1
  12.0 0.0 copy-done.2
  12.0 1.0 %near_terms.2 = (f32[8,64,8,128]{3,2,1,0:T(8,128)S(1)}, f32[8,7,16,8,128]{4,3,2,1,0:T(8,128)S(1)}) custom-call(f32[8,64,8,128]{3,2,1,0:T(8,128)S(1)} %get-tuple-element.22.signal_ref, f32[8,7,16,8,128]{4,3,2,1,0:T(8,128)S(1)} %get-tuple-element.23.sums_ref, f32[16,2048]{1,0:T(8,128)S(1)} %copy-done.1, f32[16,2048]{1,0:T(8,128)S(1)} %copy-done, ...), custom_call_target="tpu_custom_call" | custom-call | flops 5242880 | bytes 3670016 | tf_op jit(solution)/shard_map/near_terms/pallas_call | solution.py:276
  13.0 1.0 %near_terms.3 = (f32[8,64,8,128]{3,2,1,0:T(8,128)S(1)}, f32[8,7,16,8,128]{4,3,2,1,0:T(8,128)S(1)}) custom-call(f32[8,64,8,128]{3,2,1,0:T(8,128)S(1)} %get-tuple-element.28.signal_ref, f32[8,7,16,8,128]{4,3,2,1,0:T(8,128)S(1)} %get-tuple-element.29.sums_ref, f32[16,2048]{1,0:T(8,128)S(1)} %copy-done.1, f32[16,2048]{1,0:T(8,128)S(1)} %copy-done, ...), custom_call_target="tpu_custom_call" | custom-call | flops 5242880 | bytes 3670016 | tf_op jit(solution)/shard_map/near_terms/pallas_call | solution.py:276
  14.0 0.0 collective-permute-done.refs_2_
  14.0 0.1 collective-permute-done.1.refs_3_
  14.1 0.1 collective-permute-done.2.refs_4_
  14.2 1.6 %collective-permute-start.3 = (f32[16,1024]{1,0:T(8,128)S(1)}, f32[16,1024]{1,0:T(8,128)S(1)}, u32[]{:S(2)}, u32[]{:S(2)}) collective-permute-start(f32[16,1024]{1,0:T(8,128)S(1)} %carry.1.enter_ref), channel_id=1, source_target_pairs={{0,4},{4,0},{1,5},{5,1},{2,6},{6,2},{3,7},{7,3},{8,12},{12,8},{9,1... | collective-permute-start | bytes 196616 | tf_op jit(solution)/shard_map/ppermute | solution.py:334
  15.8 2.7 %spread_states.1.held_ref = bf16[512,1152]{1,0:T(8,128)(2,1)S(1)} custom-call(bf16[512,2176]{1,0:T(8,128)(2,1)S(1)} %get-tuple-element.19.query_ref, f32[8,64,8,128]{3,2,1,0:T(8,128)S(1)} %get-tuple-element.30.refs_0_.near_ref, f32[8,7,16,8,128]{4,3,2,1,0:T(8,128)S(1)} %get-tuple-element.31.sums_ref, f32[8,8,16,128]{3,2,1,0:T(8,128)S(1)} %get-tuple-element.32.scan_ref, ...), custom_call_target="tpu_custom_call" | custom-call | flops 16777216 | bytes 11010048 | tf_op jit(solution)/shard_map/spread_states/pallas_call | solution.py:276
  18.5 0.0 collective-permute-done.3.enter_ref
  18.6 3.5 %spread_and_store.1 = bf16[512,2048]{1,0:T(8,128)(2,1)} custom-call(bf16[512,2176]{1,0:T(8,128)(2,1)S(1)} %get-tuple-element.19.query_ref, f32[8,64,8,128]{3,2,1,0:T(8,128)S(1)} %get-tuple-element.24.refs_1_._.near_ref, f32[8,7,16,8,128]{4,3,2,1,0:T(8,128)S(1)} %get-tuple-element.25.sums_ref, f32[8,8,16,128]{3,2,1,0:T(8,128)S(1)} %get-tuple-element.26.scan_ref, ...), custom_call_target="tpu_custom_call" | custom-call | flops 16777216 | bytes 11010048 | tf_op jit(solution)/shard_map/spread_and_store/pallas_call | solution.py:276
  (1 shorter events, 0.0 us)
Async XLA Ops:
  0.0 9.4 %copy-start = (f32[16,2048]{1,0:T(8,128)S(1)}, f32[16,2048]{1,0:T(8,128)}, u32[]{:S(2)}) copy-start(f32[16,2048]{1,0:T(8,128)} %decays_ref.13) | copy-start | bytes 393220
  3.7 8.2 %copy-start.1 = (f32[16,2048]{1,0:T(8,128)S(1)}, f32[16,2048]{1,0:T(8,128)}, u32[]{:S(2)}) copy-start(f32[16,2048]{1,0:T(8,128)} %residues_ref.7) | copy-start | bytes 393220
  3.7 8.2 %copy-start.2 = (f32[2048]{0:T(1024)S(1)}, f32[2048]{0:T(1024)}, u32[]{:S(2)}) copy-start(f32[2048]{0:T(1024)} %param.11) | copy-start | bytes 24580
  3.8 10.2 %collective-permute-start = (f32[16,1024]{1,0:T(8,128)S(1)}, f32[16,1024]{1,0:T(8,128)S(1)}, u32[]{:S(2)}, u32[]{:S(2)}) collective-permute-start(f32[16,1024]{1,0:T(8,128)S(1)} %get-tuple-element.27.total_ref), channel_id=1, source_target_pairs={{0,2},{1,3},{2,0},{3,1},{4,6},{5,7},{6,4},{7,5},{8,10},{9,11},{10,... | collective-permute-start | bytes 196616 | tf_op jit(solution)/shard_map/ppermute | solution.py:321
  7.9 6.2 %collective-permute-start.1 = (f32[16,1024]{1,0:T(8,128)S(1)}, f32[16,1024]{1,0:T(8,128)S(1)}, u32[]{:S(2)}, u32[]{:S(2)}) collective-permute-start(f32[16,1024]{1,0:T(8,128)S(1)} %get-tuple-element.27.total_ref), channel_id=1, source_target_pairs={{0,3},{1,2},{2,1},{3,0},{4,7},{5,6},{6,5},{7,4},{8,11},{9,10},{10,... | collective-permute-start | bytes 196616 | tf_op jit(solution)/shard_map/ppermute | solution.py:321
  9.2 5.0 %collective-permute-start.2 = (f32[16,1024]{1,0:T(8,128)S(1)}, f32[16,1024]{1,0:T(8,128)S(1)}, u32[]{:S(2)}, u32[]{:S(2)}) collective-permute-start(f32[16,1024]{1,0:T(8,128)S(1)} %get-tuple-element.27.total_ref), channel_id=1, source_target_pairs={{0,1},{1,0},{2,3},{3,2},{4,5},{5,4},{6,7},{7,6},{8,9},{9,8},{10,11... | collective-permute-start | bytes 196616 | tf_op jit(solution)/shard_map/ppermute | solution.py:321
  14.2 4.3 %collective-permute-start.3 = (f32[16,1024]{1,0:T(8,128)S(1)}, f32[16,1024]{1,0:T(8,128)S(1)}, u32[]{:S(2)}, u32[]{:S(2)}) collective-permute-start(f32[16,1024]{1,0:T(8,128)S(1)} %carry.1.enter_ref), channel_id=1, source_target_pairs={{0,4},{4,0},{1,5},{5,1},{2,6},{6,2},{3,7},{7,3},{8,12},{12,8},{9,1... | collective-permute-start | bytes 196616 | tf_op jit(solution)/shard_map/ppermute | solution.py:334

commit v7 on v6

--- a/solution.py
+++ b/solution.py
@@ -12,11 +12,19 @@
 LANES = 128
 SLABS = (0, 2, 4)
 PAIR = 2
+AHEAD = 2
 MIB = 2**20
 TURNS = {2: (1,), 4: (2, 3, 1)}
 
 VMEM = pl.BlockSpec(memory_space=pltpu.VMEM)
 HBM = pl.BlockSpec(memory_space=pltpu.HBM)
+
+
+def leads():
+    origin = True
+    for axis in ("chan", "half", "ctx"):
+        origin = (lax.axis_index(axis) == 0) & origin
+    return origin
 
 
 def row(ref, index, lanes=slice(None)):
@@ -150,13 +158,14 @@
         refs[1][...] = total
 
 
-def near_terms(other, signal_ref, sums_ref, residues_ref, decays_ref, skip_ref, near_ref, scaled_ref):
+def near_terms(other, share, signal_ref, sums_ref, residues_ref, decays_ref, skip_ref, *refs):
+    near_ref, scaled_ref = refs[1:3] if share == "lead" else refs[-2:]
     blocks, steps, _, _ = signal_ref.shape
     modes = decays_ref.shape[0]
     chunks = steps // CHUNK
     first = channels_of(other, blocks * LANES)
 
-    @pl.loop(0, blocks)
+    @pl.loop(0, blocks if share is None else jnp.where(leads() == (share == "lead"), blocks, 0))
     def _(block):
         wide = pl.ds(pl.multiple_of(first + block * LANES, LANES), LANES)
         decay = decays_ref[:, wide]
@@ -184,7 +193,7 @@
                 scaled_ref[block, chunk, mode] = scaled[chunk]
 
 
-def spread_states(other, query_ref, near_ref, sums_ref, scan_ref, enter_ref, residues_ref, decays_ref, _, gated_ref, *scratch, leave=None):
+def spread_states(other, span, enter_ref, query_ref, near_ref, sums_ref, scan_ref, residues_ref, decays_ref, gated_ref, *scratch, leave=None):
     rows = gated_ref.shape[0]
     blocks, _, modes, _ = scan_ref.shape
     first = channels_of(other, blocks * LANES)
@@ -200,7 +209,7 @@
         damp[...] = once
         scale = residues_ref[:, wide] * jnp.sqrt(decay) * once
         damp_segment = jnp.exp(-seg_len * decay)
-        enter = enter_ref[:, lanes]
+        enter = jnp.zeros((modes, LANES), jnp.float32) if enter_ref is None else enter_ref[:, lanes]
         for segment in range(SEG):
             turned[pl.ds(segment * (modes + 1), modes), :] = (scan_ref[block, segment] + enter) * scale
             enter = enter * damp_segment
@@ -223,7 +232,7 @@
             place = start // seg_len * pitch + start % seg_len
             gated_ref[part, lanes] = (query_ref[part, wide].astype(jnp.float32) * natural[pl.ds(place, 16), :]).astype(jnp.bfloat16)
 
-    @pl.loop(0, blocks // PAIR)
+    @pl.loop(*span)
     def _(pair):
         for turn in range(PAIR):
             one(pair * PAIR + turn, *scratch[turn::PAIR])
@@ -232,22 +241,51 @@
                 leave(pair * PAIR + turn)
 
 
+def spread_ahead(other, query_ref, near_ref, sums_ref, scan_ref, residues_ref, decays_ref, *refs):
+    gated_ref, *scratch = refs[1:] if other else refs
+    span = 0, jnp.where(leads(), AHEAD, 0)
+    spread_states(other, span, None, query_ref, near_ref, sums_ref, scan_ref, residues_ref, decays_ref, gated_ref, *scratch)
+
+
+def spread_mine(query_ref, near_ref, sums_ref, scan_ref, residues_ref, decays_ref, enter_ref, *refs):
+    gated_ref, *scratch = refs[2:]
+    span = jnp.where(leads(), AHEAD, 0), scan_ref.shape[0] // PAIR
+    spread_states(False, span, enter_ref, query_ref, near_ref, sums_ref, scan_ref, residues_ref, decays_ref, gated_ref, *scratch)
+
+
 def spread_and_store(
-    other, query_ref, near_ref, sums_ref, scan_ref, enter_ref, residues_ref, decays_ref, held_ref, mixed_ref, *scratch
+    query_ref, near_ref, sums_ref, scan_ref, residues_ref, decays_ref, enter_ref, held_ref, _, mixed_ref, gated, *scratch
 ):
-    *scratch, gated, sems = scratch
+    *scratch, sems = scratch
     blocks = scan_ref.shape[0]
     width = blocks * LANES
-    first = channels_of(other, width)
-    held_copy = pltpu.make_async_copy(held_ref.at[:, pl.ds(0, width)], mixed_ref.at[:, pl.ds(channels_of(not other, width), width)], sems.at[blocks])
+    first = channels_of(True, width)
+    held_copy = pltpu.make_async_copy(held_ref.at[:, pl.ds(0, width)], mixed_ref.at[:, pl.ds(channels_of(False, width), width)], sems.at[blocks])
     held_copy.start()
 
     def copy(block):
         wide = pl.ds(pl.multiple_of(first + block * LANES, LANES), LANES)
         return pltpu.make_async_copy(gated.at[:, lane_block(block)], mixed_ref.at[:, wide], sems.at[block])
 
+    ahead = jnp.where(leads(), AHEAD, 0)
+
+    @pl.loop(0, ahead * PAIR)
+    def _(block):
+        copy(block).start()
+
     spread_states(
-        other, query_ref, near_ref, sums_ref, scan_ref, enter_ref, residues_ref, decays_ref, None, gated, *scratch, leave=lambda block: copy(block).start()
+        True,
+        (ahead, blocks // PAIR),
+        enter_ref,
+        query_ref,
+        near_ref,
+        sums_ref,
+        scan_ref,
+        residues_ref,
+        decays_ref,
+        gated,
+        *scratch,
+        leave=lambda block: copy(block).start(),
     )
 
     @pl.loop(0, blocks)
@@ -272,13 +310,14 @@
     natural = real((SEG * (seg_len + 1), LANES))
     table = real((modes, LANES))
 
-    def call(body, operands, out_shape, scratch, ops, moved, in_specs=None, out_specs=None, limit=4):
+    def call(body, operands, out_shape, scratch, ops, moved, in_specs=None, out_specs=None, limit=4, aliases=None):
         return pl.pallas_call(
             body,
             in_specs=in_specs or [VMEM] * len(operands),
             out_specs=out_specs or jax.tree.map(lambda _: VMEM, out_shape),
             out_shape=out_shape,
             scratch_shapes=scratch,
+            input_output_aliases=aliases or {},
             compiler_params=pltpu.CompilerParams(vmem_limit_bytes=limit * MIB),
             cost_estimate=pl.CostEstimate(flops=ops * rows * count, bytes_accessed=moved * rows * count, transcendentals=0),
             name=getattr(body, "func", body).__name__,
@@ -300,26 +339,32 @@
         in_specs=[HBM] * 4,
         limit=8,
     )
-    def near(other, states):
+    def near(other, share, states, handed=()):
         signal, sums = states[:2]
+        shapes = [real(signal.shape), real(sums.shape)]
         return call(
-            functools.partial(near_terms, other),
-            [signal, sums, residues, decays, skip_gain],
-            [real(signal.shape), real(sums.shape)],
+            functools.partial(near_terms, other, share),
+            [signal, sums, residues, decays, skip_gain, *handed],
+            shapes + [real(handed[0].shape)] if share == "lead" else shapes,
             [],
             10,
             7,
+            aliases={5: 2} if share == "lead" else {5 + index: index for index in range(len(handed))},
         )
 
+    *near_mine, total = near(False, "lead", mine, [mine[3]])
+    near_mine = near(False, "rest", mine, near_mine)
     theirs = call(functools.partial(gather_states, True), [later_keys, later_values, decays], state_shapes, scratch, 2 * modes, 19)
-    near_mine = near(False, mine)
-    near_theirs = near(True, theirs)
-
-    total, enter, reach = mine[3], None, 1
+    near_theirs = near(True, None, theirs)
+    scratch = [shape for shape in (natural, real((SEG * (modes + 1), LANES)), table) for _ in range(PAIR)]
+    operands_mine = [queries, *near_mine, mine[2], residues, decays]
+    ahead = call(functools.partial(spread_ahead, False), operands_mine, half((rows, padded)), scratch, 2 * modes, 5)
+
+    enter, reach = None, 1
     while reach < ctx_size:
         radix = min(4, ctx_size // reach)
         come = [lax.ppermute(total, "ctx", [(i, i ^ (turn * reach)) for i in range(ctx_size)]) for turn in TURNS[radix]]
-        after = [near_mine[0], near_theirs[0]] if reach == 1 else []
+        after = [near_theirs[0], ahead] if reach == 1 else []
         last = radix * reach == ctx_size
         result = call(
             functools.partial(carry, False, reach, radix, rows, len(after)),
@@ -333,25 +378,20 @@
         reach *= radix
     enter_theirs = lax.ppermute(enter, "half", [(0, 1), (1, 0)])
 
-    scratch = [shape for shape in (natural, real((SEG * (modes + 1), LANES)), table) for _ in range(PAIR)]
-    held = call(
-        functools.partial(spread_states, False),
-        [queries, *near_mine, mine[2], enter, residues, decays, near_theirs[0]],
-        half((rows, padded)),
-        scratch,
+    operands_theirs = [queries, *near_theirs, theirs[2], residues, decays]
+    ahead_theirs = call(functools.partial(spread_ahead, True), [*operands_theirs, enter], half((rows, padded)), scratch, 2 * modes, 5)
+    held = call(spread_mine, [*operands_mine, enter, ahead, ahead_theirs], half((rows, padded)), scratch, 2 * modes, 21, aliases={7: 0})
+    mixed, _ = call(
+        spread_and_store,
+        [*operands_theirs, enter_theirs, held, ahead_theirs],
+        [jax.ShapeDtypeStruct((rows, width), jnp.bfloat16), half((rows, padded))],
+        scratch + [pltpu.SemaphoreType.DMA((blocks + 1,))],
         2 * modes,
         21,
+        out_specs=[HBM, VMEM],
+        aliases={8: 1},
     )
-    return call(
-        functools.partial(spread_and_store, True),
-        [queries, *near_theirs, theirs[2], enter_theirs, residues, decays, held],
-        jax.ShapeDtypeStruct((rows, width), jnp.bfloat16),
-        scratch + [half((rows, padded)), pltpu.SemaphoreType.DMA((blocks + 1,))],
-        2 * modes,
-        21,
-        out_specs=HBM,
-        limit=6,
-    )
+    return mixed
 
 
 def solution(mesh):

time: 22.2 us -> 21.1 us (0.950)
  starting transfers between devices: 7.27 us -> 6.08 us
    ppermute x3, starting transfers between devices: 5.68 us -> 4.72 us  [shards(): lax.ppermute(total, 'ctx', [(i, i ^ turn * reach) for i in range(ctx_size)])]
    ppermute x1, starting transfers between devices: 1.59 us -> 1.36 us  [shards(): enter_theirs = lax.ppermute(enter, 'half', [(0, 1), (1, 0)])]
    pallas_call x7 -> x10, Pallas kernels: 14.5 us -> 14.6 us  [call(): pl.pallas_call(body, in_specs=in_specs or [VMEM] * len(operands), out_spe...]
  transfers between devices with their start and end apart: 4 -> 4, of which waited for: 2 -> 1; matrix products, arithmetic and copies ran while one was open for 0% -> 0% of each run, Pallas kernels for 33% -> 36%
where the time goes in v7:
time: 21.1 us; the launch traced here: 21 us
  Pallas kernels  14.6 us (69%)
  starting transfers between devices  6.08 us (29%)
  waiting for transfers between devices  0.23 us (1%)
    pallas_call x10, Pallas kernels, call(): pl.pallas_call(body, in_specs=in_specs or [VMEM] * len(operands), out_spe...  14.6 us
    ppermute x3, starting transfers between devices, shards(): lax.ppermute(total, 'ctx', [(i, i ^ turn * reach) for i in range(ctx_size)])  4.72 us
    ppermute x1, starting transfers between devices, shards(): enter_theirs = lax.ppermute(enter, 'half', [(0, 1), (1, 0)])  1.36 us
  transfers between devices with their start and end apart: 4, of which 1 were waited for; matrix products, arithmetic and copies ran while one was open for 0% of the time, Pallas kernels for 36%

profile of v7, /device:TPU:0, one launch (start us, length us, event | category | flops | bytes accessed | tf_op | source)
XLA Modules:
  0.0 21.0 jit_solution(15124248630709162288)
XLA Ops:
  0.0 0.0 copy-start
  0.0 0.0 copy-start.2
  0.0 0.0 copy-start.1
  0.0 3.7 %load_and_gather.1 = (f32[8,64,8,128]{3,2,1,0:T(8,128)S(1)}, f32[8,7,16,8,128]{4,3,2,1,0:T(8,128)S(1)}, f32[8,8,16,128]{3,2,1,0:T(8,128)S(1)}, f32[16,1024]{1,0:...) custom-call(bf16[512,2048]{1,0:T(8,128)(2,1)} %key_ref.1, ...), custom_call_target="tpu_custom_call" | custom-call | flops 16777216 | bytes 9961472 | tf_op jit(solution)/shard_map/load_and_gather/pallas_call | solution.py:314
  3.7 0.0 copy-done
  3.8 0.0 copy-done.2
  3.8 0.0 copy-done.1
  3.8 1.0 %near_terms.4 = (f32[8,64,8,128]{3,2,1,0:T(8,128)S(1)}, f32[8,7,16,8,128]{4,3,2,1,0:T(8,128)S(1)}, f32[16,1024]{1,0:T(8,128)S(1)}) custom-call(f32[8,64,8,128]{3,2,1,0:T(8,128)S(1)} %get-tuple-element.31.signal_ref, f32[8,7,16,8,128]{4,3,2,1,0:T(8,128)S(1)} %get-tuple-element.32.sums_ref, f32[16,2048]{1,0:T(8,128)S(1)} %copy-done.1, ...), custom_call_target="tpu_custom_call", output_to_operand_aliasing={{2}: (5, {})} | custom-call | flops 5242880 | bytes 3670016 | tf_op jit(solution)/shard_map/near_terms/pallas_call | solution.py:314
  4.8 3.1 %collective-permute-start = (f32[16,1024]{1,0:T(8,128)S(1)}, f32[16,1024]{1,0:T(8,128)S(1)}, u32[]{:S(2)}, u32[]{:S(2)}) collective-permute-start(f32[16,1024]{1,0:T(8,128)S(1)} %get-tuple-element.34.total_ref), channel_id=1, source_target_pairs={{0,2},{1,3},{2,0},{3,1},{4,6},{5,7},{6,4},{7,5},{8,10},{9,11},{10,... | collective-permute-start | bytes 196616 | tf_op jit(solution)/shard_map/ppermute | solution.py:366
  7.9 1.3 %collective-permute-start.1 = (f32[16,1024]{1,0:T(8,128)S(1)}, f32[16,1024]{1,0:T(8,128)S(1)}, u32[]{:S(2)}, u32[]{:S(2)}) collective-permute-start(f32[16,1024]{1,0:T(8,128)S(1)} %get-tuple-element.34.total_ref), channel_id=1, source_target_pairs={{0,3},{1,2},{2,1},{3,0},{4,7},{5,6},{6,5},{7,4},{8,11},{9,10},{10,... | collective-permute-start | bytes 196616 | tf_op jit(solution)/shard_map/ppermute | solution.py:366
  9.3 0.2 %collective-permute-start.2 = (f32[16,1024]{1,0:T(8,128)S(1)}, f32[16,1024]{1,0:T(8,128)S(1)}, u32[]{:S(2)}, u32[]{:S(2)}) collective-permute-start(f32[16,1024]{1,0:T(8,128)S(1)} %get-tuple-element.34.total_ref), channel_id=1, source_target_pairs={{0,1},{1,0},{2,3},{3,2},{4,5},{5,4},{6,7},{7,6},{8,9},{9,8},{10,11... | collective-permute-start | bytes 196616 | tf_op jit(solution)/shard_map/ppermute | solution.py:366
  9.5 2.5 %gather_states.1 = (f32[8,64,8,128]{3,2,1,0:T(8,128)S(1)}, f32[8,7,16,8,128]{4,3,2,1,0:T(8,128)S(1)}, f32[8,8,16,128]{3,2,1,0:T(8,128)S(1)}) custom-call(bf16[512,1152]{1,0:T(8,128)(2,1)S(1)} %get-tuple-element.24.key_ref, bf16[512,1152]{1,0:T(8,128)(2,1)S(1)} %get-tuple-element.25.value_ref, f32[16,2048]{1,0:T(8,128)S(1)} %copy-done), custom_call_target="tpu_custom_call" | custom-call | flops 16777216 | bytes 9961472 | tf_op jit(solution)/shard_map/gather_states/pallas_call | solution.py:314
  12.0 1.0 %near_terms.3 = (f32[8,64,8,128]{3,2,1,0:T(8,128)S(1)}, f32[8,7,16,8,128]{4,3,2,1,0:T(8,128)S(1)}) custom-call(f32[8,64,8,128]{3,2,1,0:T(8,128)S(1)} %get-tuple-element.26.signal_ref, f32[8,7,16,8,128]{4,3,2,1,0:T(8,128)S(1)} %get-tuple-element.27.sums_ref, f32[16,2048]{1,0:T(8,128)S(1)} %copy-done.1, f32[16,2048]{1,0:T(8,128)S(1)} %copy-done, ...), custom_call_target="tpu_custom_call" | custom-call | flops 5242880 | bytes 3670016 | tf_op jit(solution)/shard_map/near_terms/pallas_call | solution.py:314
  13.0 1.4 %spread_ahead.2.refs_1_.refs_0_ = bf16[512,1152]{1,0:T(8,128)(2,1)S(1)} custom-call(bf16[512,2176]{1,0:T(8,128)(2,1)S(1)} %get-tuple-element.23.query_ref, f32[8,64,8,128]{3,2,1,0:T(8,128)S(1)} %get-tuple-element.37.near_ref, f32[8,7,16,8,128]{4,3,2,1,0:T(8,128)S(1)} %get-tuple-element.38.sums_ref, f32[8,8,16,128]{3,2,1,0:T(8,128)S(1)} %get-tuple-element.39.scan_ref, ...), custom_call_target="tpu_custom_call" | custom-call | flops 16777216 | bytes 2621440 | tf_op jit(solution)/shard_map/spread_ahead/pallas_call | solution.py:314
  14.4 0.0 collective-permute-done.refs_2_
  14.4 0.0 collective-permute-done.1.refs_3_
  14.4 0.0 collective-permute-done.2.refs_4_
  14.4 0.1 carry.1.refs_0_.enter_ref
  14.5 1.4 %collective-permute-start.3 = (f32[16,1024]{1,0:T(8,128)S(1)}, f32[16,1024]{1,0:T(8,128)S(1)}, u32[]{:S(2)}, u32[]{:S(2)}) collective-permute-start(f32[16,1024]{1,0:T(8,128)S(1)} %carry.1.refs_0_.enter_ref), channel_id=1, source_target_pairs={{0,4},{4,0},{1,5},{5,1},{2,6},{6,2},{3,7},{7,3},{8,12},{12,8},{9,1... | collective-permute-start | bytes 196616 | tf_op jit(solution)/shard_map/ppermute | solution.py:379
  15.9 1.4 %spread_ahead.3.refs_1_._ = bf16[512,1152]{1,0:T(8,128)(2,1)S(1)} custom-call(bf16[512,2176]{1,0:T(8,128)(2,1)S(1)} %get-tuple-element.23.query_ref, f32[8,64,8,128]{3,2,1,0:T(8,128)S(1)} %get-tuple-element.28.refs_0_.near_ref, f32[8,7,16,8,128]{4,3,2,1,0:T(8,128)S(1)} %get-tuple-element.29.sums_ref, f32[8,8,16,128]{3,2,1,0:T(8,128)S(1)} %get-tuple-element.30.scan_ref, ...), custom_call_target="tpu_custom_call" | custom-call | flops 16777216 | bytes 2621440 | tf_op jit(solution)/shard_map/spread_ahead/pallas_call | solution.py:314
  17.2 1.4 %spread_mine.1.held_ref = bf16[512,1152]{1,0:T(8,128)(2,1)S(1)} custom-call(bf16[512,2176]{1,0:T(8,128)(2,1)S(1)} %get-tuple-element.23.query_ref, f32[8,64,8,128]{3,2,1,0:T(8,128)S(1)} %get-tuple-element.37.near_ref, f32[8,7,16,8,128]{4,3,2,1,0:T(8,128)S(1)} %get-tuple-element.38.sums_ref, ...), custom_call_target="tpu_custom_call", output_to_operand_aliasing={{}: (7, {})} | custom-call | flops 16777216 | bytes 11010048 | tf_op jit(solution)/shard_map/spread_mine/pallas_call | solution.py:314
  18.6 0.2 %collective-permute-done.3.enter_ref = f32[16,1024]{1,0:T(8,128)S(1)} collective-permute-done((f32[16,1024]{1,0:T(8,128)S(1)}, f32[16,1024]{1,0:T(8,128)S(1)}, u32[]{:S(2)}, u32[]{:S(2)}) %collective-permute-start.3) | collective-permute-done | bytes 65568 | tf_op jit(solution)/shard_map/ppermute | solution.py:379
  18.8 2.1 %spread_and_store.1 = (bf16[512,2048]{1,0:T(8,128)(2,1)}, bf16[512,1152]{1,0:T(8,128)(2,1)S(1)}) custom-call(bf16[512,2176]{1,0:T(8,128)(2,1)S(1)} %get-tuple-element.23.query_ref, f32[8,64,8,128]{3,2,1,0:T(8,128)S(1)} %get-tuple-element.28.refs_0_.near_ref, f32[8,7,16,8,128]{4,3,2,1,0:T(8,128)S(1)} %get-tuple-element.29.sums_ref, ...), custom_call_target="tpu_custom_call", output_to_operand_aliasing={{1}: (8, {})} | custom-call | flops 16777216 | bytes 11010048 | tf_op jit(solution)/shard_map/spread_and_store/pallas_call | solution.py:314
  (1 shorter events, 0.0 us)
Async XLA Ops:
  0.0 3.7 %copy-start = (f32[16,2048]{1,0:T(8,128)S(1)}, f32[16,2048]{1,0:T(8,128)}, u32[]{:S(2)}) copy-start(f32[16,2048]{1,0:T(8,128)} %decays_ref.19) | copy-start | bytes 393220
  0.0 3.8 %copy-start.2 = (f32[2048]{0:T(1024)S(1)}, f32[2048]{0:T(1024)}, u32[]{:S(2)}) copy-start(f32[2048]{0:T(1024)} %param.11) | copy-start | bytes 24580
  0.0 3.8 %copy-start.1 = (f32[16,2048]{1,0:T(8,128)S(1)}, f32[16,2048]{1,0:T(8,128)}, u32[]{:S(2)}) copy-start(f32[16,2048]{1,0:T(8,128)} %residues_ref.13) | copy-start | bytes 393220
  4.8 9.6 %collective-permute-start = (f32[16,1024]{1,0:T(8,128)S(1)}, f32[16,1024]{1,0:T(8,128)S(1)}, u32[]{:S(2)}, u32[]{:S(2)}) collective-permute-start(f32[16,1024]{1,0:T(8,128)S(1)} %get-tuple-element.34.total_ref), channel_id=1, source_target_pairs={{0,2},{1,3},{2,0},{3,1},{4,6},{5,7},{6,4},{7,5},{8,10},{9,11},{10,... | collective-permute-start | bytes 196616 | tf_op jit(solution)/shard_map/ppermute | solution.py:366
  7.9 6.5 %collective-permute-start.1 = (f32[16,1024]{1,0:T(8,128)S(1)}, f32[16,1024]{1,0:T(8,128)S(1)}, u32[]{:S(2)}, u32[]{:S(2)}) collective-permute-start(f32[16,1024]{1,0:T(8,128)S(1)} %get-tuple-element.34.total_ref), channel_id=1, source_target_pairs={{0,3},{1,2},{2,1},{3,0},{4,7},{5,6},{6,5},{7,4},{8,11},{9,10},{10,... | collective-permute-start | bytes 196616 | tf_op jit(solution)/shard_map/ppermute | solution.py:366
  9.3 5.2 %collective-permute-start.2 = (f32[16,1024]{1,0:T(8,128)S(1)}, f32[16,1024]{1,0:T(8,128)S(1)}, u32[]{:S(2)}, u32[]{:S(2)}) collective-permute-start(f32[16,1024]{1,0:T(8,128)S(1)} %get-tuple-element.34.total_ref), channel_id=1, source_target_pairs={{0,1},{1,0},{2,3},{3,2},{4,5},{5,4},{6,7},{7,6},{8,9},{9,8},{10,11... | collective-permute-start | bytes 196616 | tf_op jit(solution)/shard_map/ppermute | solution.py:366
  14.5 4.3 %collective-permute-start.3 = (f32[16,1024]{1,0:T(8,128)S(1)}, f32[16,1024]{1,0:T(8,128)S(1)}, u32[]{:S(2)}, u32[]{:S(2)}) collective-permute-start(f32[16,1024]{1,0:T(8,128)S(1)} %carry.1.refs_0_.enter_ref), channel_id=1, source_target_pairs={{0,4},{4,0},{1,5},{5,1},{2,6},{6,2},{3,7},{7,3},{8,12},{12,8},{9,1... | collective-permute-start | bytes 196616 | tf_op jit(solution)/shard_map/ppermute | solution.py:379

commit v8 on v7

--- a/solution.py
+++ b/solution.py
@@ -10,7 +10,7 @@
 SEG = 8
 CHUNK = 8
 LANES = 128
-SLABS = (0, 2, 4)
+SLABS = (0, 1, 2, 4)
 PAIR = 2
 AHEAD = 2
 MIB = 2**20
@@ -40,7 +40,28 @@
     return pl.multiple_of((1 - mine if other else mine) * count, LANES)
 
 
-def gather_states(other, key_ref, value_ref, decays_ref, signal_ref, sums_ref, scan_ref, *scratch, end_ref=None, arrive=None):
+def near_tables(residue, decay, skip):
+    term = residue * jnp.sqrt(decay)
+    damp = jnp.exp(-decay)
+    weight = term * damp
+    taps = []
+    for step in range(CHUNK):
+        tap = jnp.sum(term, 0, keepdims=True)
+        if step == 0:
+            tap = tap + skip
+        taps.append(jnp.broadcast_to(tap, (SEG, LANES)))
+        term = term * damp
+    return taps, weight
+
+
+def near_sum(taps, signal, step):
+    total = taps[0] * signal[step]
+    for back in range(1, step + 1):
+        total = total + taps[back] * signal[step - back]
+    return total
+
+
+def gather_states(other, key_ref, value_ref, decays_ref, signal_ref, sums_ref, scan_ref, *scratch, end_ref=None, arrive=None, near=None):
     rows = key_ref.shape[0]
     blocks, _, modes, _ = scan_ref.shape
     seg_len = rows // SEG
@@ -48,9 +69,12 @@
     pitch = seg_len + 1
     first = channels_of(other, blocks * LANES) if other else 0
 
-    def one(block, natural, turned, damp, damp_chunk):
+    def one(block, natural, turned, damp, damp_chunk, *weights):
         lanes = lane_block(block)
-        decay = decays_ref[:, pl.ds(pl.multiple_of(first + block * LANES, LANES), LANES)]
+        wide = pl.ds(pl.multiple_of(first + block * LANES, LANES), LANES)
+        decay = decays_ref[:, wide]
+        if near is not None:
+            taps, weights[0][...] = near_tables(near[0][:, wide], decay, near[1][:, wide])
         damp[...] = jnp.exp(-decay)
         damp_chunk[...] = jnp.exp(-CHUNK * decay)
         damp_segment = jnp.exp(-seg_len * decay)
@@ -62,14 +86,14 @@
         for chunk in range(chunks):
             signal = [natural[pl.ds(chunk * CHUNK + step, SEG, stride=pitch), :] for step in range(CHUNK)]
             for step in range(CHUNK):
-                signal_ref[block, chunk * CHUNK + step] = signal[step]
+                signal_ref[block, chunk * CHUNK + step] = signal[step] if near is None else near_sum(taps, signal, step)
             for mode in range(modes):
                 factor = row(damp, mode)
                 total = signal[0]
                 for step in range(1, CHUNK):
                     total = total * factor + signal[step]
                 if chunk < chunks - 1:
-                    sums_ref[block, chunk, mode] = total
+                    sums_ref[block, chunk, mode] = total if near is None else total * row(weights[0], mode)
                 states[mode] = total if chunk == 0 else states[mode] * row(damp_chunk, mode) + total
         for mode in range(modes):
             turned[pl.ds(mode * (SEG + 1), SEG), :] = states[mode]
@@ -81,12 +105,21 @@
         if end_ref is not None:
             end_ref[:, lanes] = state
 
-    @pl.loop(0, blocks // PAIR)
+    if arrive is not None:
+        for turn in range(PAIR):
+            arrive(turn)
+            one(turn, *scratch[turn::PAIR])
+
+    @pl.loop(0 if arrive is None else 1, blocks // PAIR)
     def _(pair):
         if arrive is not None:
-            arrive(pair)
+            arrive(pair * PAIR)
         for turn in range(PAIR):
             one(pair * PAIR + turn, *scratch[turn::PAIR])
+
+
+def gather_with_near(key_ref, value_ref, decays_ref, residues_ref, skip_ref, near_ref, scaled_ref, scan_ref, *scratch):
+    gather_states(True, key_ref, value_ref, decays_ref, near_ref, scaled_ref, scan_ref, *scratch, near=(residues_ref, skip_ref))
 
 
 def load_and_gather(
@@ -122,10 +155,10 @@
         copy.start()
     rate_copy.wait()
 
-    def arrive(pair):
+    def arrive(block):
         for start, copies in zip(starts, slabs):
 
-            @pl.when(pair * PAIR == start)
+            @pl.when(block == start)
             def _(copies=copies):
                 for copy in copies:
                     copy.wait()
@@ -158,34 +191,21 @@
         refs[1][...] = total
 
 
-def near_terms(other, share, signal_ref, sums_ref, residues_ref, decays_ref, skip_ref, *refs):
+def near_terms(share, signal_ref, sums_ref, residues_ref, decays_ref, skip_ref, *refs):
     near_ref, scaled_ref = refs[1:3] if share == "lead" else refs[-2:]
     blocks, steps, _, _ = signal_ref.shape
     modes = decays_ref.shape[0]
     chunks = steps // CHUNK
-    first = channels_of(other, blocks * LANES)
-
-    @pl.loop(0, blocks if share is None else jnp.where(leads() == (share == "lead"), blocks, 0))
+    first = channels_of(False, blocks * LANES)
+
+    @pl.loop(0, jnp.where(leads() == (share == "lead"), blocks, 0))
     def _(block):
         wide = pl.ds(pl.multiple_of(first + block * LANES, LANES), LANES)
-        decay = decays_ref[:, wide]
-        term = residues_ref[:, wide] * jnp.sqrt(decay)
-        damp = jnp.exp(-decay)
-        weight = term * damp
-        taps = []
-        for step in range(CHUNK):
-            tap = jnp.sum(term, 0, keepdims=True)
-            if step == 0:
-                tap = tap + skip_ref[:, wide]
-            taps.append(jnp.broadcast_to(tap, (SEG, LANES)))
-            term = term * damp
+        taps, weight = near_tables(residues_ref[:, wide], decays_ref[:, wide], skip_ref[:, wide])
         for chunk in range(chunks):
             signal = [signal_ref[block, chunk * CHUNK + step] for step in range(CHUNK)]
             for step in range(CHUNK):
-                total = taps[0] * signal[step]
-                for back in range(1, step + 1):
-                    total = total + taps[back] * signal[step - back]
-                near_ref[block, chunk * CHUNK + step] = total
+                near_ref[block, chunk * CHUNK + step] = near_sum(taps, signal, step)
         for mode in range(modes):
             factor = jnp.broadcast_to(weight[mode : mode + 1, :], (SEG, LANES))
             scaled = [factor * sums_ref[block, chunk, mode] for chunk in range(chunks - 1)]
@@ -333,17 +353,17 @@
         load_and_gather,
         [pltpu.with_memory_space_constraint(array, pltpu.HBM) for array in (key_gate, value_input, query_gate, decays)],
         state_shapes + [real((modes, count)), half((rows, padded)), half((rows, padded)), half((rows, width + LANES))],
-        scratch + [half((rows, padded)), half((rows, padded)), real((modes, count)), pltpu.SemaphoreType.DMA((3, 4))],
+        scratch + [half((rows, padded)), half((rows, padded)), real((modes, count)), pltpu.SemaphoreType.DMA((3, max(4, len(SLABS))))],
         2 * modes,
         19,
         in_specs=[HBM] * 4,
         limit=8,
     )
-    def near(other, share, states, handed=()):
+    def near(share, states, handed):
         signal, sums = states[:2]
         shapes = [real(signal.shape), real(sums.shape)]
         return call(
-            functools.partial(near_terms, other, share),
+            functools.partial(near_terms, share),
             [signal, sums, residues, decays, skip_gain, *handed],
             shapes + [real(handed[0].shape)] if share == "lead" else shapes,
             [],
@@ -352,10 +372,16 @@
             aliases={5: 2} if share == "lead" else {5 + index: index for index in range(len(handed))},
         )
 
-    *near_mine, total = near(False, "lead", mine, [mine[3]])
-    near_mine = near(False, "rest", mine, near_mine)
-    theirs = call(functools.partial(gather_states, True), [later_keys, later_values, decays], state_shapes, scratch, 2 * modes, 19)
-    near_theirs = near(True, None, theirs)
+    *near_mine, total = near("lead", mine, [mine[3]])
+    near_mine = near("rest", mine, near_mine)
+    *near_theirs, scan_theirs = call(
+        gather_with_near,
+        [later_keys, later_values, decays, residues, skip_gain],
+        state_shapes,
+        scratch + [table] * PAIR,
+        2 * modes,
+        24,
+    )
     scratch = [shape for shape in (natural, real((SEG * (modes + 1), LANES)), table) for _ in range(PAIR)]
     operands_mine = [queries, *near_mine, mine[2], residues, decays]
     ahead = call(functools.partial(spread_ahead, False), operands_mine, half((rows, padded)), scratch, 2 * modes, 5)
@@ -378,7 +404,7 @@
         reach *= radix
     enter_theirs = lax.ppermute(enter, "half", [(0, 1), (1, 0)])
 
-    operands_theirs = [queries, *near_theirs, theirs[2], residues, decays]
+    operands_theirs = [queries, *near_theirs, scan_theirs, residues, decays]
     ahead_theirs = call(functools.partial(spread_ahead, True), [*operands_theirs, enter], half((rows, padded)), scratch, 2 * modes, 5)
     held = call(spread_mine, [*operands_mine, enter, ahead, ahead_theirs], half((rows, padded)), scratch, 2 * modes, 21, aliases={7: 0})
     mixed, _ = call(

time: 21.1 us -> 20.9 us (level)
  starting transfers between devices: 6.08 us -> 6.3 us
    ppermute x1, starting transfers between devices: 1.36 us -> 1.58 us  [shards(): enter_theirs = lax.ppermute(enter, 'half', [(0, 1), (1, 0)])]
    ppermute x1, waiting for transfers between devices: 0.23 us -> 0.01 us  [shards(): enter_theirs = lax.ppermute(enter, 'half', [(0, 1), (1, 0)])]
    pallas_call x10 -> x9, Pallas kernels: 14.6 us -> 14.4 us  [call(): pl.pallas_call(body, in_specs=in_specs or [VMEM] * len(operands), out_spe...]
  transfers between devices with their start and end apart: 4 -> 4, of which waited for: 1 -> 0; matrix products, arithmetic and copies ran while one was open for 0% -> 0% of each run, Pallas kernels for 36% -> 36%
where the time goes in v8:
time: 20.9 us; the launch traced here: 20.8 us
  Pallas kernels  14.4 us (69%)
  starting transfers between devices  6.3 us (30%)
    pallas_call x9, Pallas kernels, call(): pl.pallas_call(body, in_specs=in_specs or [VMEM] * len(operands), out_spe...  14.4 us
    ppermute x3, starting transfers between devices, shards(): lax.ppermute(total, 'ctx', [(i, i ^ turn * reach) for i in range(ctx_size)])  4.72 us
    ppermute x1, starting transfers between devices, shards(): enter_theirs = lax.ppermute(enter, 'half', [(0, 1), (1, 0)])  1.58 us
  transfers between devices with their start and end apart: 4, of which 0 were waited for; matrix products, arithmetic and copies ran while one was open for 0% of the time, Pallas kernels for 36%

profile of v8, /device:TPU:0, one launch (start us, length us, event | category | flops | bytes accessed | tf_op | source)
XLA Modules:
  0.0 20.8 jit_solution(7606779028442916064)
XLA Ops:
  0.0 0.0 copy-start
  0.0 0.0 copy-start.2
  0.0 0.0 copy-start.1
  0.0 3.7 %load_and_gather.1 = (f32[8,64,8,128]{3,2,1,0:T(8,128)S(1)}, f32[8,7,16,8,128]{4,3,2,1,0:T(8,128)S(1)}, f32[8,8,16,128]{3,2,1,0:T(8,128)S(1)}, f32[16,1024]{1,0:...) custom-call(bf16[512,2048]{1,0:T(8,128)(2,1)} %key_ref.1, ...), custom_call_target="tpu_custom_call" | custom-call | flops 16777216 | bytes 9961472 | tf_op jit(solution)/shard_map/load_and_gather/pallas_call | solution.py:334
  3.7 0.0 copy-done
  3.7 0.0 copy-done.2
  3.7 0.0 copy-done.1
  3.7 1.0 %near_terms.2 = (f32[8,64,8,128]{3,2,1,0:T(8,128)S(1)}, f32[8,7,16,8,128]{4,3,2,1,0:T(8,128)S(1)}, f32[16,1024]{1,0:T(8,128)S(1)}) custom-call(f32[8,64,8,128]{3,2,1,0:T(8,128)S(1)} %get-tuple-element.27.signal_ref, f32[8,7,16,8,128]{4,3,2,1,0:T(8,128)S(1)} %get-tuple-element.28.sums_ref, f32[16,2048]{1,0:T(8,128)S(1)} %copy-done.1, ...), custom_call_target="tpu_custom_call", output_to_operand_aliasing={{2}: (5, {})} | custom-call | flops 5242880 | bytes 3670016 | tf_op jit(solution)/shard_map/near_terms/pallas_call | solution.py:334
  4.8 3.1 %collective-permute-start = (f32[16,1024]{1,0:T(8,128)S(1)}, f32[16,1024]{1,0:T(8,128)S(1)}, u32[]{:S(2)}, u32[]{:S(2)}) collective-permute-start(f32[16,1024]{1,0:T(8,128)S(1)} %get-tuple-element.30.total_ref), channel_id=1, source_target_pairs={{0,2},{1,3},{2,0},{3,1},{4,6},{5,7},{6,4},{7,5},{8,10},{9,11},{10,... | collective-permute-start | bytes 196616 | tf_op jit(solution)/shard_map/ppermute | solution.py:392
  7.9 1.3 %collective-permute-start.1 = (f32[16,1024]{1,0:T(8,128)S(1)}, f32[16,1024]{1,0:T(8,128)S(1)}, u32[]{:S(2)}, u32[]{:S(2)}) collective-permute-start(f32[16,1024]{1,0:T(8,128)S(1)} %get-tuple-element.30.total_ref), channel_id=1, source_target_pairs={{0,3},{1,2},{2,1},{3,0},{4,7},{5,6},{6,5},{7,4},{8,11},{9,10},{10,... | collective-permute-start | bytes 196616 | tf_op jit(solution)/shard_map/ppermute | solution.py:392
  9.2 0.2 %collective-permute-start.2 = (f32[16,1024]{1,0:T(8,128)S(1)}, f32[16,1024]{1,0:T(8,128)S(1)}, u32[]{:S(2)}, u32[]{:S(2)}) collective-permute-start(f32[16,1024]{1,0:T(8,128)S(1)} %get-tuple-element.30.total_ref), channel_id=1, source_target_pairs={{0,1},{1,0},{2,3},{3,2},{4,5},{5,4},{6,7},{7,6},{8,9},{9,8},{10,11... | collective-permute-start | bytes 196616 | tf_op jit(solution)/shard_map/ppermute | solution.py:392
  9.5 3.3 %gather_with_near.1 = (f32[8,64,8,128]{3,2,1,0:T(8,128)S(1)}, f32[8,7,16,8,128]{4,3,2,1,0:T(8,128)S(1)}, f32[8,8,16,128]{3,2,1,0:T(8,128)S(1)}) custom-call(bf16[512,1152]{1,0:T(8,128)(2,1)S(1)} %get-tuple-element.22.key_ref, bf16[512,1152]{1,0:T(8,128)(2,1)S(1)} %get-tuple-element.23.value_ref, f32[16,2048]{1,0:T(8,128)S(1)} %copy-done, ...), custom_call_target="tpu_custom_call" | custom-call | flops 16777216 | bytes 12582912 | tf_op jit(solution)/shard_map/gather_with_near/pallas_call | solution.py:334
  12.8 1.4 %spread_ahead.2.refs_1_.refs_0_ = bf16[512,1152]{1,0:T(8,128)(2,1)S(1)} custom-call(bf16[512,2176]{1,0:T(8,128)(2,1)S(1)} %get-tuple-element.21.query_ref, f32[8,64,8,128]{3,2,1,0:T(8,128)S(1)} %get-tuple-element.33.near_ref, f32[8,7,16,8,128]{4,3,2,1,0:T(8,128)S(1)} %get-tuple-element.34.sums_ref, f32[8,8,16,128]{3,2,1,0:T(8,128)S(1)} %get-tuple-element.35.scan_ref, ...), custom_call_target="tpu_custom_call" | custom-call | flops 16777216 | bytes 2621440 | tf_op jit(solution)/shard_map/spread_ahead/pallas_call | solution.py:334
  14.2 0.0 collective-permute-done.refs_2_
  14.2 0.0 collective-permute-done.1.refs_3_
  14.2 0.0 collective-permute-done.2.refs_4_
  14.3 1.6 %collective-permute-start.3 = (f32[16,1024]{1,0:T(8,128)S(1)}, f32[16,1024]{1,0:T(8,128)S(1)}, u32[]{:S(2)}, u32[]{:S(2)}) collective-permute-start(f32[16,1024]{1,0:T(8,128)S(1)} %carry.1.refs_0_.enter_ref), channel_id=1, source_target_pairs={{0,4},{4,0},{1,5},{5,1},{2,6},{6,2},{3,7},{7,3},{8,12},{12,8},{9,1... | collective-permute-start | bytes 196616 | tf_op jit(solution)/shard_map/ppermute | solution.py:405
  15.8 1.4 %spread_ahead.3.refs_1_._ = bf16[512,1152]{1,0:T(8,128)(2,1)S(1)} custom-call(bf16[512,2176]{1,0:T(8,128)(2,1)S(1)} %get-tuple-element.21.query_ref, f32[8,64,8,128]{3,2,1,0:T(8,128)S(1)} %get-tuple-element.24.refs_0_.near_ref, f32[8,7,16,8,128]{4,3,2,1,0:T(8,128)S(1)} %get-tuple-element.25.sums_ref, f32[8,8,16,128]{3,2,1,0:T(8,128)S(1)} %get-tuple-element.26.scan_ref, ...), custom_call_target="tpu_custom_call" | custom-call | flops 16777216 | bytes 2621440 | tf_op jit(solution)/shard_map/spread_ahead/pallas_call | solution.py:334
  17.2 1.4 %spread_mine.1.held_ref = bf16[512,1152]{1,0:T(8,128)(2,1)S(1)} custom-call(bf16[512,2176]{1,0:T(8,128)(2,1)S(1)} %get-tuple-element.21.query_ref, f32[8,64,8,128]{3,2,1,0:T(8,128)S(1)} %get-tuple-element.33.near_ref, f32[8,7,16,8,128]{4,3,2,1,0:T(8,128)S(1)} %get-tuple-element.34.sums_ref, ...), custom_call_target="tpu_custom_call", output_to_operand_aliasing={{}: (7, {})} | custom-call | flops 16777216 | bytes 11010048 | tf_op jit(solution)/shard_map/spread_mine/pallas_call | solution.py:334
  18.6 0.0 collective-permute-done.3.enter_ref
  18.6 2.2 %spread_and_store.1 = (bf16[512,2048]{1,0:T(8,128)(2,1)}, bf16[512,1152]{1,0:T(8,128)(2,1)S(1)}) custom-call(bf16[512,2176]{1,0:T(8,128)(2,1)S(1)} %get-tuple-element.21.query_ref, f32[8,64,8,128]{3,2,1,0:T(8,128)S(1)} %get-tuple-element.24.refs_0_.near_ref, f32[8,7,16,8,128]{4,3,2,1,0:T(8,128)S(1)} %get-tuple-element.25.sums_ref, ...), custom_call_target="tpu_custom_call", output_to_operand_aliasing={{1}: (8, {})} | custom-call | flops 16777216 | bytes 11010048 | tf_op jit(solution)/shard_map/spread_and_store/pallas_call | solution.py:334
  (2 shorter events, 0.0 us)
Async XLA Ops:
  0.0 3.7 %copy-start = (f32[16,2048]{1,0:T(8,128)S(1)}, f32[16,2048]{1,0:T(8,128)}, u32[]{:S(2)}) copy-start(f32[16,2048]{1,0:T(8,128)} %decays_ref.17) | copy-start | bytes 393220
  0.0 3.7 %copy-start.2 = (f32[2048]{0:T(1024)S(1)}, f32[2048]{0:T(1024)}, u32[]{:S(2)}) copy-start(f32[2048]{0:T(1024)} %param.11) | copy-start | bytes 24580
  0.0 3.7 %copy-start.1 = (f32[16,2048]{1,0:T(8,128)S(1)}, f32[16,2048]{1,0:T(8,128)}, u32[]{:S(2)}) copy-start(f32[16,2048]{1,0:T(8,128)} %residues_ref.13) | copy-start | bytes 393220
  4.8 9.4 %collective-permute-start = (f32[16,1024]{1,0:T(8,128)S(1)}, f32[16,1024]{1,0:T(8,128)S(1)}, u32[]{:S(2)}, u32[]{:S(2)}) collective-permute-start(f32[16,1024]{1,0:T(8,128)S(1)} %get-tuple-element.30.total_ref), channel_id=1, source_target_pairs={{0,2},{1,3},{2,0},{3,1},{4,6},{5,7},{6,4},{7,5},{8,10},{9,11},{10,... | collective-permute-start | bytes 196616 | tf_op jit(solution)/shard_map/ppermute | solution.py:392
  7.9 6.3 %collective-permute-start.1 = (f32[16,1024]{1,0:T(8,128)S(1)}, f32[16,1024]{1,0:T(8,128)S(1)}, u32[]{:S(2)}, u32[]{:S(2)}) collective-permute-start(f32[16,1024]{1,0:T(8,128)S(1)} %get-tuple-element.30.total_ref), channel_id=1, source_target_pairs={{0,3},{1,2},{2,1},{3,0},{4,7},{5,6},{6,5},{7,4},{8,11},{9,10},{10,... | collective-permute-start | bytes 196616 | tf_op jit(solution)/shard_map/ppermute | solution.py:392
  9.2 5.0 %collective-permute-start.2 = (f32[16,1024]{1,0:T(8,128)S(1)}, f32[16,1024]{1,0:T(8,128)S(1)}, u32[]{:S(2)}, u32[]{:S(2)}) collective-permute-start(f32[16,1024]{1,0:T(8,128)S(1)} %get-tuple-element.30.total_ref), channel_id=1, source_target_pairs={{0,1},{1,0},{2,3},{3,2},{4,5},{5,4},{6,7},{7,6},{8,9},{9,8},{10,11... | collective-permute-start | bytes 196616 | tf_op jit(solution)/shard_map/ppermute | solution.py:392
  14.3 4.3 %collective-permute-start.3 = (f32[16,1024]{1,0:T(8,128)S(1)}, f32[16,1024]{1,0:T(8,128)S(1)}, u32[]{:S(2)}, u32[]{:S(2)}) collective-permute-start(f32[16,1024]{1,0:T(8,128)S(1)} %carry.1.refs_0_.enter_ref), channel_id=1, source_target_pairs={{0,4},{4,0},{1,5},{5,1},{2,6},{6,2},{3,7},{7,3},{8,12},{12,8},{9,1... | collective-permute-start | bytes 196616 | tf_op jit(solution)/shard_map/ppermute | solution.py:405

commit v9 on v8

--- a/solution.py
+++ b/solution.py
@@ -256,8 +256,7 @@
     def _(pair):
         for turn in range(PAIR):
             one(pair * PAIR + turn, *scratch[turn::PAIR])
-        if leave is not None:
-            for turn in range(PAIR):
+            if leave is not None:
                 leave(pair * PAIR + turn)
 
 

time: 20.9 us -> 20.9 us (level)
  no operation moved by 1% of the time
where the time goes in v9:
time: 20.9 us; the launch traced here: 20.8 us
  Pallas kernels  14.3 us (68%)
  starting transfers between devices  6.3 us (30%)
    pallas_call x9, Pallas kernels, call(): pl.pallas_call(body, in_specs=in_specs or [VMEM] * len(operands), out_spe...  14.3 us
    ppermute x3, starting transfers between devices, shards(): lax.ppermute(total, 'ctx', [(i, i ^ turn * reach) for i in range(ctx_size)])  4.72 us
    ppermute x1, starting transfers between devices, shards(): enter_theirs = lax.ppermute(enter, 'half', [(0, 1), (1, 0)])  1.58 us
  transfers between devices with their start and end apart: 4, of which 0 were waited for; matrix products, arithmetic and copies ran while one was open for 0% of the time, Pallas kernels for 36%

profile of v9, /device:TPU:0, one launch (start us, length us, event | category | flops | bytes accessed | tf_op | source)
XLA Modules:
  0.0 20.8 jit_solution(17026382640114238570)
XLA Ops:
  0.0 0.0 copy-start
  0.0 0.0 copy-start.2
  0.0 0.0 copy-start.1
  0.0 3.7 %load_and_gather.1 = (f32[8,64,8,128]{3,2,1,0:T(8,128)S(1)}, f32[8,7,16,8,128]{4,3,2,1,0:T(8,128)S(1)}, f32[8,8,16,128]{3,2,1,0:T(8,128)S(1)}, f32[16,1024]{1,0:...) custom-call(bf16[512,2048]{1,0:T(8,128)(2,1)} %key_ref.1, ...), custom_call_target="tpu_custom_call" | custom-call | flops 16777216 | bytes 9961472 | tf_op jit(solution)/shard_map/load_and_gather/pallas_call | solution.py:333
  3.7 0.0 copy-done
  3.7 0.0 copy-done.2
  3.7 0.0 copy-done.1
  3.7 1.0 %near_terms.2 = (f32[8,64,8,128]{3,2,1,0:T(8,128)S(1)}, f32[8,7,16,8,128]{4,3,2,1,0:T(8,128)S(1)}, f32[16,1024]{1,0:T(8,128)S(1)}) custom-call(f32[8,64,8,128]{3,2,1,0:T(8,128)S(1)} %get-tuple-element.27.signal_ref, f32[8,7,16,8,128]{4,3,2,1,0:T(8,128)S(1)} %get-tuple-element.28.sums_ref, f32[16,2048]{1,0:T(8,128)S(1)} %copy-done.1, ...), custom_call_target="tpu_custom_call", output_to_operand_aliasing={{2}: (5, {})} | custom-call | flops 5242880 | bytes 3670016 | tf_op jit(solution)/shard_map/near_terms/pallas_call | solution.py:333
  4.8 3.1 %collective-permute-start = (f32[16,1024]{1,0:T(8,128)S(1)}, f32[16,1024]{1,0:T(8,128)S(1)}, u32[]{:S(2)}, u32[]{:S(2)}) collective-permute-start(f32[16,1024]{1,0:T(8,128)S(1)} %get-tuple-element.30.total_ref), channel_id=1, source_target_pairs={{0,2},{1,3},{2,0},{3,1},{4,6},{5,7},{6,4},{7,5},{8,10},{9,11},{10,... | collective-permute-start | bytes 196616 | tf_op jit(solution)/shard_map/ppermute | solution.py:391
  7.9 1.3 %collective-permute-start.1 = (f32[16,1024]{1,0:T(8,128)S(1)}, f32[16,1024]{1,0:T(8,128)S(1)}, u32[]{:S(2)}, u32[]{:S(2)}) collective-permute-start(f32[16,1024]{1,0:T(8,128)S(1)} %get-tuple-element.30.total_ref), channel_id=1, source_target_pairs={{0,3},{1,2},{2,1},{3,0},{4,7},{5,6},{6,5},{7,4},{8,11},{9,10},{10,... | collective-permute-start | bytes 196616 | tf_op jit(solution)/shard_map/ppermute | solution.py:391
  9.2 0.2 %collective-permute-start.2 = (f32[16,1024]{1,0:T(8,128)S(1)}, f32[16,1024]{1,0:T(8,128)S(1)}, u32[]{:S(2)}, u32[]{:S(2)}) collective-permute-start(f32[16,1024]{1,0:T(8,128)S(1)} %get-tuple-element.30.total_ref), channel_id=1, source_target_pairs={{0,1},{1,0},{2,3},{3,2},{4,5},{5,4},{6,7},{7,6},{8,9},{9,8},{10,11... | collective-permute-start | bytes 196616 | tf_op jit(solution)/shard_map/ppermute | solution.py:391
  9.5 3.3 %gather_with_near.1 = (f32[8,64,8,128]{3,2,1,0:T(8,128)S(1)}, f32[8,7,16,8,128]{4,3,2,1,0:T(8,128)S(1)}, f32[8,8,16,128]{3,2,1,0:T(8,128)S(1)}) custom-call(bf16[512,1152]{1,0:T(8,128)(2,1)S(1)} %get-tuple-element.22.key_ref, bf16[512,1152]{1,0:T(8,128)(2,1)S(1)} %get-tuple-element.23.value_ref, f32[16,2048]{1,0:T(8,128)S(1)} %copy-done, ...), custom_call_target="tpu_custom_call" | custom-call | flops 16777216 | bytes 12582912 | tf_op jit(solution)/shard_map/gather_with_near/pallas_call | solution.py:333
  12.8 1.4 %spread_ahead.2.refs_1_.refs_0_ = bf16[512,1152]{1,0:T(8,128)(2,1)S(1)} custom-call(bf16[512,2176]{1,0:T(8,128)(2,1)S(1)} %get-tuple-element.21.query_ref, f32[8,64,8,128]{3,2,1,0:T(8,128)S(1)} %get-tuple-element.33.near_ref, f32[8,7,16,8,128]{4,3,2,1,0:T(8,128)S(1)} %get-tuple-element.34.sums_ref, f32[8,8,16,128]{3,2,1,0:T(8,128)S(1)} %get-tuple-element.35.scan_ref, ...), custom_call_target="tpu_custom_call" | custom-call | flops 16777216 | bytes 2621440 | tf_op jit(solution)/shard_map/spread_ahead/pallas_call | solution.py:333
  14.2 0.0 collective-permute-done.refs_2_
  14.2 0.0 collective-permute-done.1.refs_3_
  14.2 0.0 collective-permute-done.2.refs_4_
  14.3 1.6 %collective-permute-start.3 = (f32[16,1024]{1,0:T(8,128)S(1)}, f32[16,1024]{1,0:T(8,128)S(1)}, u32[]{:S(2)}, u32[]{:S(2)}) collective-permute-start(f32[16,1024]{1,0:T(8,128)S(1)} %carry.1.refs_0_.enter_ref), channel_id=1, source_target_pairs={{0,4},{4,0},{1,5},{5,1},{2,6},{6,2},{3,7},{7,3},{8,12},{12,8},{9,1... | collective-permute-start | bytes 196616 | tf_op jit(solution)/shard_map/ppermute | solution.py:404
  15.8 1.4 %spread_ahead.3.refs_1_._ = bf16[512,1152]{1,0:T(8,128)(2,1)S(1)} custom-call(bf16[512,2176]{1,0:T(8,128)(2,1)S(1)} %get-tuple-element.21.query_ref, f32[8,64,8,128]{3,2,1,0:T(8,128)S(1)} %get-tuple-element.24.refs_0_.near_ref, f32[8,7,16,8,128]{4,3,2,1,0:T(8,128)S(1)} %get-tuple-element.25.sums_ref, f32[8,8,16,128]{3,2,1,0:T(8,128)S(1)} %get-tuple-element.26.scan_ref, ...), custom_call_target="tpu_custom_call" | custom-call | flops 16777216 | bytes 2621440 | tf_op jit(solution)/shard_map/spread_ahead/pallas_call | solution.py:333
  17.2 1.4 %spread_mine.1.held_ref = bf16[512,1152]{1,0:T(8,128)(2,1)S(1)} custom-call(bf16[512,2176]{1,0:T(8,128)(2,1)S(1)} %get-tuple-element.21.query_ref, f32[8,64,8,128]{3,2,1,0:T(8,128)S(1)} %get-tuple-element.33.near_ref, f32[8,7,16,8,128]{4,3,2,1,0:T(8,128)S(1)} %get-tuple-element.34.sums_ref, ...), custom_call_target="tpu_custom_call", output_to_operand_aliasing={{}: (7, {})} | custom-call | flops 16777216 | bytes 11010048 | tf_op jit(solution)/shard_map/spread_mine/pallas_call | solution.py:333
  18.6 0.0 collective-permute-done.3.enter_ref
  18.6 2.2 %spread_and_store.1 = (bf16[512,2048]{1,0:T(8,128)(2,1)}, bf16[512,1152]{1,0:T(8,128)(2,1)S(1)}) custom-call(bf16[512,2176]{1,0:T(8,128)(2,1)S(1)} %get-tuple-element.21.query_ref, f32[8,64,8,128]{3,2,1,0:T(8,128)S(1)} %get-tuple-element.24.refs_0_.near_ref, f32[8,7,16,8,128]{4,3,2,1,0:T(8,128)S(1)} %get-tuple-element.25.sums_ref, ...), custom_call_target="tpu_custom_call", output_to_operand_aliasing={{1}: (8, {})} | custom-call | flops 16777216 | bytes 11010048 | tf_op jit(solution)/shard_map/spread_and_store/pallas_call | solution.py:333
  (2 shorter events, 0.0 us)
Async XLA Ops:
  0.0 3.7 %copy-start = (f32[16,2048]{1,0:T(8,128)S(1)}, f32[16,2048]{1,0:T(8,128)}, u32[]{:S(2)}) copy-start(f32[16,2048]{1,0:T(8,128)} %decays_ref.17) | copy-start | bytes 393220
  0.0 3.7 %copy-start.2 = (f32[2048]{0:T(1024)S(1)}, f32[2048]{0:T(1024)}, u32[]{:S(2)}) copy-start(f32[2048]{0:T(1024)} %param.11) | copy-start | bytes 24580
  0.0 3.7 %copy-start.1 = (f32[16,2048]{1,0:T(8,128)S(1)}, f32[16,2048]{1,0:T(8,128)}, u32[]{:S(2)}) copy-start(f32[16,2048]{1,0:T(8,128)} %residues_ref.13) | copy-start | bytes 393220
  4.8 9.4 %collective-permute-start = (f32[16,1024]{1,0:T(8,128)S(1)}, f32[16,1024]{1,0:T(8,128)S(1)}, u32[]{:S(2)}, u32[]{:S(2)}) collective-permute-start(f32[16,1024]{1,0:T(8,128)S(1)} %get-tuple-element.30.total_ref), channel_id=1, source_target_pairs={{0,2},{1,3},{2,0},{3,1},{4,6},{5,7},{6,4},{7,5},{8,10},{9,11},{10,... | collective-permute-start | bytes 196616 | tf_op jit(solution)/shard_map/ppermute | solution.py:391
  7.9 6.3 %collective-permute-start.1 = (f32[16,1024]{1,0:T(8,128)S(1)}, f32[16,1024]{1,0:T(8,128)S(1)}, u32[]{:S(2)}, u32[]{:S(2)}) collective-permute-start(f32[16,1024]{1,0:T(8,128)S(1)} %get-tuple-element.30.total_ref), channel_id=1, source_target_pairs={{0,3},{1,2},{2,1},{3,0},{4,7},{5,6},{6,5},{7,4},{8,11},{9,10},{10,... | collective-permute-start | bytes 196616 | tf_op jit(solution)/shard_map/ppermute | solution.py:391
  9.2 5.0 %collective-permute-start.2 = (f32[16,1024]{1,0:T(8,128)S(1)}, f32[16,1024]{1,0:T(8,128)S(1)}, u32[]{:S(2)}, u32[]{:S(2)}) collective-permute-start(f32[16,1024]{1,0:T(8,128)S(1)} %get-tuple-element.30.total_ref), channel_id=1, source_target_pairs={{0,1},{1,0},{2,3},{3,2},{4,5},{5,4},{6,7},{7,6},{8,9},{9,8},{10,11... | collective-permute-start | bytes 196616 | tf_op jit(solution)/shard_map/ppermute | solution.py:391
  14.3 4.3 %collective-permute-start.3 = (f32[16,1024]{1,0:T(8,128)S(1)}, f32[16,1024]{1,0:T(8,128)S(1)}, u32[]{:S(2)}, u32[]{:S(2)}) collective-permute-start(f32[16,1024]{1,0:T(8,128)S(1)} %carry.1.refs_0_.enter_ref), channel_id=1, source_target_pairs={{0,4},{4,0},{1,5},{5,1},{2,6},{6,2},{3,7},{7,3},{8,12},{12,8},{9,1... | collective-permute-start | bytes 196616 | tf_op jit(solution)/shard_map/ppermute | solution.py:404

commit v10 on v9

--- a/solution.py
+++ b/solution.py
@@ -11,8 +11,8 @@
 CHUNK = 8
 LANES = 128
 SLABS = (0, 1, 2, 4)
-PAIR = 2
-AHEAD = 2
+PAIR = 4
+AHEAD = 1
 MIB = 2**20
 TURNS = {2: (1,), 4: (2, 3, 1)}
 

time: 20.9 us -> 20.9 us (level)
  transfers between devices with their start and end apart: 4 -> 4, of which waited for: 0 -> 1; matrix products, arithmetic and copies ran while one was open for 0% -> 0% of each run, Pallas kernels for 36% -> 36%
where the time goes in v10:
time: 20.9 us; the launch traced here: 20.7 us
  Pallas kernels  14.2 us (68%)
  starting transfers between devices  6.3 us (30%)
    pallas_call x9, Pallas kernels, call(): pl.pallas_call(body, in_specs=in_specs or [VMEM] * len(operands), out_spe...  14.2 us
    ppermute x3, starting transfers between devices, shards(): lax.ppermute(total, 'ctx', [(i, i ^ turn * reach) for i in range(ctx_size)])  4.72 us
    ppermute x1, starting transfers between devices, shards(): enter_theirs = lax.ppermute(enter, 'half', [(0, 1), (1, 0)])  1.59 us
  transfers between devices with their start and end apart: 4, of which 1 were waited for; matrix products, arithmetic and copies ran while one was open for 0% of the time, Pallas kernels for 36%

profile of v10, /device:TPU:0, one launch (start us, length us, event | category | flops | bytes accessed | tf_op | source)
XLA Modules:
  0.0 20.7 jit_solution(12805216528341329109)
XLA Ops:
  0.0 0.0 copy-start
  0.0 0.0 copy-start.2
  0.0 0.0 copy-start.1
  0.0 3.7 %load_and_gather.1 = (f32[8,64,8,128]{3,2,1,0:T(8,128)S(1)}, f32[8,7,16,8,128]{4,3,2,1,0:T(8,128)S(1)}, f32[8,8,16,128]{3,2,1,0:T(8,128)S(1)}, f32[16,1024]{1,0:...) custom-call(bf16[512,2048]{1,0:T(8,128)(2,1)} %key_ref.1, ...), custom_call_target="tpu_custom_call" | custom-call | flops 16777216 | bytes 9961472 | tf_op jit(solution)/shard_map/load_and_gather/pallas_call | solution.py:333
  3.7 0.0 copy-done
  3.7 0.0 copy-done.2
  3.7 0.0 copy-done.1
  3.7 1.0 %near_terms.2 = (f32[8,64,8,128]{3,2,1,0:T(8,128)S(1)}, f32[8,7,16,8,128]{4,3,2,1,0:T(8,128)S(1)}, f32[16,1024]{1,0:T(8,128)S(1)}) custom-call(f32[8,64,8,128]{3,2,1,0:T(8,128)S(1)} %get-tuple-element.27.signal_ref, f32[8,7,16,8,128]{4,3,2,1,0:T(8,128)S(1)} %get-tuple-element.28.sums_ref, f32[16,2048]{1,0:T(8,128)S(1)} %copy-done.1, ...), custom_call_target="tpu_custom_call", output_to_operand_aliasing={{2}: (5, {})} | custom-call | flops 5242880 | bytes 3670016 | tf_op jit(solution)/shard_map/near_terms/pallas_call | solution.py:333
  4.7 3.1 %collective-permute-start = (f32[16,1024]{1,0:T(8,128)S(1)}, f32[16,1024]{1,0:T(8,128)S(1)}, u32[]{:S(2)}, u32[]{:S(2)}) collective-permute-start(f32[16,1024]{1,0:T(8,128)S(1)} %get-tuple-element.30.total_ref), channel_id=1, source_target_pairs={{0,2},{1,3},{2,0},{3,1},{4,6},{5,7},{6,4},{7,5},{8,10},{9,11},{10,... | collective-permute-start | bytes 196616 | tf_op jit(solution)/shard_map/ppermute | solution.py:391
  7.9 1.3 %collective-permute-start.1 = (f32[16,1024]{1,0:T(8,128)S(1)}, f32[16,1024]{1,0:T(8,128)S(1)}, u32[]{:S(2)}, u32[]{:S(2)}) collective-permute-start(f32[16,1024]{1,0:T(8,128)S(1)} %get-tuple-element.30.total_ref), channel_id=1, source_target_pairs={{0,3},{1,2},{2,1},{3,0},{4,7},{5,6},{6,5},{7,4},{8,11},{9,10},{10,... | collective-permute-start | bytes 196616 | tf_op jit(solution)/shard_map/ppermute | solution.py:391
  9.2 0.2 %collective-permute-start.2 = (f32[16,1024]{1,0:T(8,128)S(1)}, f32[16,1024]{1,0:T(8,128)S(1)}, u32[]{:S(2)}, u32[]{:S(2)}) collective-permute-start(f32[16,1024]{1,0:T(8,128)S(1)} %get-tuple-element.30.total_ref), channel_id=1, source_target_pairs={{0,1},{1,0},{2,3},{3,2},{4,5},{5,4},{6,7},{7,6},{8,9},{9,8},{10,11... | collective-permute-start | bytes 196616 | tf_op jit(solution)/shard_map/ppermute | solution.py:391
  9.4 3.3 %gather_with_near.1 = (f32[8,64,8,128]{3,2,1,0:T(8,128)S(1)}, f32[8,7,16,8,128]{4,3,2,1,0:T(8,128)S(1)}, f32[8,8,16,128]{3,2,1,0:T(8,128)S(1)}) custom-call(bf16[512,1152]{1,0:T(8,128)(2,1)S(1)} %get-tuple-element.22.key_ref, bf16[512,1152]{1,0:T(8,128)(2,1)S(1)} %get-tuple-element.23.value_ref, f32[16,2048]{1,0:T(8,128)S(1)} %copy-done, ...), custom_call_target="tpu_custom_call" | custom-call | flops 16777216 | bytes 12582912 | tf_op jit(solution)/shard_map/gather_with_near/pallas_call | solution.py:333
  12.7 1.4 %spread_ahead.2.refs_1_.refs_0_ = bf16[512,1152]{1,0:T(8,128)(2,1)S(1)} custom-call(bf16[512,2176]{1,0:T(8,128)(2,1)S(1)} %get-tuple-element.21.query_ref, f32[8,64,8,128]{3,2,1,0:T(8,128)S(1)} %get-tuple-element.33.near_ref, f32[8,7,16,8,128]{4,3,2,1,0:T(8,128)S(1)} %get-tuple-element.34.sums_ref, f32[8,8,16,128]{3,2,1,0:T(8,128)S(1)} %get-tuple-element.35.scan_ref, ...), custom_call_target="tpu_custom_call" | custom-call | flops 16777216 | bytes 2621440 | tf_op jit(solution)/shard_map/spread_ahead/pallas_call | solution.py:333
  14.1 0.0 collective-permute-done.refs_2_
  14.1 0.0 collective-permute-done.1.refs_3_
  14.1 0.1 collective-permute-done.2.refs_4_
  14.2 1.6 %collective-permute-start.3 = (f32[16,1024]{1,0:T(8,128)S(1)}, f32[16,1024]{1,0:T(8,128)S(1)}, u32[]{:S(2)}, u32[]{:S(2)}) collective-permute-start(f32[16,1024]{1,0:T(8,128)S(1)} %carry.1.refs_0_.enter_ref), channel_id=1, source_target_pairs={{0,4},{4,0},{1,5},{5,1},{2,6},{6,2},{3,7},{7,3},{8,12},{12,8},{9,1... | collective-permute-start | bytes 196616 | tf_op jit(solution)/shard_map/ppermute | solution.py:404
  15.8 1.3 %spread_ahead.3.refs_1_._ = bf16[512,1152]{1,0:T(8,128)(2,1)S(1)} custom-call(bf16[512,2176]{1,0:T(8,128)(2,1)S(1)} %get-tuple-element.21.query_ref, f32[8,64,8,128]{3,2,1,0:T(8,128)S(1)} %get-tuple-element.24.refs_0_.near_ref, f32[8,7,16,8,128]{4,3,2,1,0:T(8,128)S(1)} %get-tuple-element.25.sums_ref, f32[8,8,16,128]{3,2,1,0:T(8,128)S(1)} %get-tuple-element.26.scan_ref, ...), custom_call_target="tpu_custom_call" | custom-call | flops 16777216 | bytes 2621440 | tf_op jit(solution)/shard_map/spread_ahead/pallas_call | solution.py:333
  17.2 1.4 %spread_mine.1.held_ref = bf16[512,1152]{1,0:T(8,128)(2,1)S(1)} custom-call(bf16[512,2176]{1,0:T(8,128)(2,1)S(1)} %get-tuple-element.21.query_ref, f32[8,64,8,128]{3,2,1,0:T(8,128)S(1)} %get-tuple-element.33.near_ref, f32[8,7,16,8,128]{4,3,2,1,0:T(8,128)S(1)} %get-tuple-element.34.sums_ref, ...), custom_call_target="tpu_custom_call", output_to_operand_aliasing={{}: (7, {})} | custom-call | flops 16777216 | bytes 11010048 | tf_op jit(solution)/shard_map/spread_mine/pallas_call | solution.py:333
  18.6 0.0 collective-permute-done.3.enter_ref
  18.6 2.2 %spread_and_store.1 = (bf16[512,2048]{1,0:T(8,128)(2,1)}, bf16[512,1152]{1,0:T(8,128)(2,1)S(1)}) custom-call(bf16[512,2176]{1,0:T(8,128)(2,1)S(1)} %get-tuple-element.21.query_ref, f32[8,64,8,128]{3,2,1,0:T(8,128)S(1)} %get-tuple-element.24.refs_0_.near_ref, f32[8,7,16,8,128]{4,3,2,1,0:T(8,128)S(1)} %get-tuple-element.25.sums_ref, ...), custom_call_target="tpu_custom_call", output_to_operand_aliasing={{1}: (8, {})} | custom-call | flops 16777216 | bytes 11010048 | tf_op jit(solution)/shard_map/spread_and_store/pallas_call | solution.py:333
  (2 shorter events, 0.0 us)
Async XLA Ops:
  0.0 3.7 %copy-start = (f32[16,2048]{1,0:T(8,128)S(1)}, f32[16,2048]{1,0:T(8,128)}, u32[]{:S(2)}) copy-start(f32[16,2048]{1,0:T(8,128)} %decays_ref.17) | copy-start | bytes 393220
  0.0 3.7 %copy-start.2 = (f32[2048]{0:T(1024)S(1)}, f32[2048]{0:T(1024)}, u32[]{:S(2)}) copy-start(f32[2048]{0:T(1024)} %param.11) | copy-start | bytes 24580
  0.0 3.7 %copy-start.1 = (f32[16,2048]{1,0:T(8,128)S(1)}, f32[16,2048]{1,0:T(8,128)}, u32[]{:S(2)}) copy-start(f32[16,2048]{1,0:T(8,128)} %residues_ref.13) | copy-start | bytes 393220
  4.7 9.4 %collective-permute-start = (f32[16,1024]{1,0:T(8,128)S(1)}, f32[16,1024]{1,0:T(8,128)S(1)}, u32[]{:S(2)}, u32[]{:S(2)}) collective-permute-start(f32[16,1024]{1,0:T(8,128)S(1)} %get-tuple-element.30.total_ref), channel_id=1, source_target_pairs={{0,2},{1,3},{2,0},{3,1},{4,6},{5,7},{6,4},{7,5},{8,10},{9,11},{10,... | collective-permute-start | bytes 196616 | tf_op jit(solution)/shard_map/ppermute | solution.py:391
  7.9 6.2 %collective-permute-start.1 = (f32[16,1024]{1,0:T(8,128)S(1)}, f32[16,1024]{1,0:T(8,128)S(1)}, u32[]{:S(2)}, u32[]{:S(2)}) collective-permute-start(f32[16,1024]{1,0:T(8,128)S(1)} %get-tuple-element.30.total_ref), channel_id=1, source_target_pairs={{0,3},{1,2},{2,1},{3,0},{4,7},{5,6},{6,5},{7,4},{8,11},{9,10},{10,... | collective-permute-start | bytes 196616 | tf_op jit(solution)/shard_map/ppermute | solution.py:391
  9.2 5.0 %collective-permute-start.2 = (f32[16,1024]{1,0:T(8,128)S(1)}, f32[16,1024]{1,0:T(8,128)S(1)}, u32[]{:S(2)}, u32[]{:S(2)}) collective-permute-start(f32[16,1024]{1,0:T(8,128)S(1)} %get-tuple-element.30.total_ref), channel_id=1, source_target_pairs={{0,1},{1,0},{2,3},{3,2},{4,5},{5,4},{6,7},{7,6},{8,9},{9,8},{10,11... | collective-permute-start | bytes 196616 | tf_op jit(solution)/shard_map/ppermute | solution.py:391
  14.2 4.3 %collective-permute-start.3 = (f32[16,1024]{1,0:T(8,128)S(1)}, f32[16,1024]{1,0:T(8,128)S(1)}, u32[]{:S(2)}, u32[]{:S(2)}) collective-permute-start(f32[16,1024]{1,0:T(8,128)S(1)} %carry.1.refs_0_.enter_ref), channel_id=1, source_target_pairs={{0,4},{4,0},{1,5},{5,1},{2,6},{6,2},{3,7},{7,3},{8,12},{12,8},{9,1... | collective-permute-start | bytes 196616 | tf_op jit(solution)/shard_map/ppermute | solution.py:404
